TPU v7x, 32 devices: a whole 2x2x4 slice. The times are simulated.
32 devices in a mesh: seq: 8 (over y, x, core), wt: 4 (over z).
Axes of the slice: x: 2, y: 2, z: 4, core: 2. Of those that a mesh axis runs over, the one named last changes fastest.
Arguments:
- tokens: bfloat16 [2048, 2048], P('seq'), may hold values from -6 to 6
- cotangent: bfloat16 [2048, 2048], P('seq'), may hold values from -6 to 6
- doc_start: int32 [2048], P('seq'), may hold values from 0 to 1, as said below
- premix_gain: float32 [2048], replicated, may hold values from 0.5 to 1.5
- inner_proj: bfloat16 [2048, 4096], P('seq', 'wt'), may hold values from -0.125 to 0.125
- switch_proj: bfloat16 [2048, 4096], P('seq', 'wt'), may hold values from -0.125 to 0.125
- conv_taps: float32 [4, 4096], P(None, 'wt'), may hold values from -3 to 3
- conv_bias: float32 [4096], P('wt'), may hold values from -3 to 3
- select_proj: bfloat16 [160, 4096], P('seq', 'wt'), may hold values from -0.09375 to 0.09375
- step_proj: bfloat16 [128, 4096], P('seq', 'wt'), may hold values from -0.5 to 0.5
- step_bias: float32 [4096], P('wt'), may hold values from -6 to -2
- decay_log: float32 [16, 4096], P(None, 'wt'), may hold values from -8 to 1
- skip_gain: float32 [4096], P('wt'), may hold values from 0.5 to 1.5
- mixer_out: bfloat16 [2048, 4096], P('seq', 'wt'), may hold values from -0.09375 to 0.09375
- preffn_gain: float32 [2048], replicated, may hold values from 0.5 to 1.5
- ffn_gate: bfloat16 [2048, 8192], P('seq', 'wt'), may hold values from -0.125 to 0.125
- ffn_up: bfloat16 [2048, 8192], P('seq', 'wt'), may hold values from -0.125 to 0.125
- ffn_down: bfloat16 [2048, 8192], P('seq', 'wt'), may hold values from -0.0625 to 0.0625
Outputs:
- block_out: bfloat16 [2048, 2048], P('seq')
- tokens_grad: bfloat16 [2048, 2048], P('seq')
- premix_gain_grad: float32 [2048], replicated
- inner_proj_grad: float32 [2048, 4096], P('seq', 'wt')
- switch_proj_grad: float32 [2048, 4096], P('seq', 'wt')
- conv_taps_grad: float32 [4, 4096], P(None, 'wt')
- conv_bias_grad: float32 [4096], P('wt')
- select_proj_grad: float32 [160, 4096], P('seq', 'wt')
- step_proj_grad: float32 [128, 4096], P('seq', 'wt')
- step_bias_grad: float32 [4096], P('wt')
- decay_log_grad: float32 [16, 4096], P(None, 'wt')
- skip_gain_grad: float32 [4096], P('wt')
- mixer_out_grad: float32 [2048, 4096], P('seq', 'wt')
- preffn_gain_grad: float32 [2048], replicated
- ffn_gate_grad: float32 [2048, 8192], P('seq', 'wt')
- ffn_up_grad: float32 [2048, 8192], P('seq', 'wt')
- ffn_down_grad: float32 [2048, 8192], P('seq', 'wt')
Inputs may be any that keep to these rules, and one draw needn't show every extreme that they name: `doc_start`: 1 marks the first token of a document; token 0 holds 0 and opens the first document. One document begins among the first 256/2 tokens and ends among the last 256/2, and no other begins in between.
All inputs are finite; a program needn't handle non-finite values.
Results may differ from a plain program's by a relative error of at most 0.012.
The roundings to bfloat16 on the way count: a program that leaves them out, or rounds other values in their place, can miss the bound.
Values may be sent and summed in bfloat16 or wider, within the bound.
A program may use at most 256 MiB of HBM per device.

v0:
```python
import jax
import jax.numpy as jnp
from jax import lax
from jax.sharding import PartitionSpec as P

NS = 16
R = 128
KC = 4


EPS = 1e-05


def from_behind(block, axis, distance):
    devices = range(lax.axis_size(axis))
    route = [(i - distance, i) for i in devices if i - distance in devices]
    return lax.ppermute(block, axis, route)


def prefix(value, axis, join, neutral, backward):
    count, mine = (lax.axis_size(axis), lax.axis_index(axis))
    pieces = jax.tree.map(lambda part: lax.all_gather(part, axis), value)
    if backward:
        pieces = jax.tree.map(lambda part: part[::-1], pieces)
        mine = count - 1 - mine
    subtotal = jax.tree.map(
        lambda part, zero: jnp.full_like(part, 0) + jnp.asarray(zero, part.dtype), value, neutral
    )

    def hop(position, subtotal):
        longer = join(subtotal, jax.tree.map(lambda part: part[position], pieces))
        return jax.tree.map(lambda new, old: jnp.where(position < mine, new, old), longer, subtotal)

    return lax.fori_loop(0, count - 1, hop, subtotal)


def contract(left_op, right_op, pattern):
    return jnp.einsum(pattern, left_op, right_op, preferred_element_type=jnp.float32)


def rms_parts(values, gain_vec):
    mean_sq = jnp.mean(values * values, axis=-1, keepdims=True)
    inverse = lax.rsqrt(mean_sq + EPS)
    normed = values * inverse
    return (normed * gain_vec, normed, inverse)


def rms_back(grad_out, normed, inverse, gain_vec):
    scaled = grad_out * gain_vec
    inner_mean = jnp.mean(scaled * normed, axis=-1, keepdims=True)
    return (inverse * (scaled - normed * inner_mean), jnp.sum(grad_out * normed, axis=0))


def silu_slope(values):
    sigma = jax.nn.sigmoid(values)
    return sigma * (1.0 + values * (1.0 - sigma))


def chain_maps(earlier, later):
    return (earlier[0] * later[0], later[0] * earlier[1] + later[1])


def local(
    tokens,
    cotangent,
    doc_start,
    premix_gain,
    inner_proj,
    switch_proj,
    conv_taps,
    conv_bias,
    select_proj,
    step_proj,
    step_bias,
    decay_log,
    skip_gain,
    mixer_out,
    preffn_gain,
    ffn_gate,
    ffn_up,
    ffn_down,
):
    tok_count = tokens.shape[0]
    edge = KC - 1
    weights_local = (
        inner_proj,
        switch_proj,
        select_proj,
        step_proj,
        mixer_out,
        ffn_gate,
        ffn_up,
        ffn_down,
    )
    gathered = (
        lax.all_gather(weights_local[0], "seq", axis=0, tiled=True),
        lax.all_gather(weights_local[1], "seq", axis=0, tiled=True),
        lax.all_gather(weights_local[2], "seq", axis=0, tiled=True),
        lax.all_gather(weights_local[3], "seq", axis=0, tiled=True),
        lax.all_gather(weights_local[4], "seq", axis=0, tiled=True),
        lax.all_gather(weights_local[5], "seq", axis=0, tiled=True),
        lax.all_gather(weights_local[6], "seq", axis=0, tiled=True),
        lax.all_gather(weights_local[7], "seq", axis=0, tiled=True),
    )
    w_inner, w_switch, w_select, w_step, w_mix, w_gate, w_up, w_down = gathered
    token_vals = tokens.astype(jnp.float32)
    first_out, first_normed, first_inv = rms_parts(token_vals, premix_gain)
    first_in = first_out.astype(jnp.bfloat16)
    inner_act = contract(first_in, w_inner, "td,dc->tc").astype(jnp.bfloat16)
    switch = contract(first_in, w_switch, "td,dc->tc")
    counts = jnp.cumsum(doc_start)
    last_count = counts[-1]
    head_keep = (counts == 0).astype(jnp.float32)
    tail_keep = (counts == last_count).astype(jnp.float32)
    tail_rows = jnp.where(
        tail_keep[-edge:, None] > 0, inner_act[-edge:], jnp.zeros_like(inner_act[-edge:])
    )
    prev_rows = from_behind(tail_rows, "seq", 1)
    extended = jnp.concatenate([prev_rows, inner_act], axis=0).astype(jnp.float32)
    ext_counts = jnp.concatenate([jnp.zeros((edge,), jnp.int32), counts])
    conv_out = jnp.zeros((tok_count, inner_act.shape[1]), jnp.float32) + conv_bias[None, :]
    for offset in range(KC):
        same_doc = (counts == ext_counts[edge - offset : edge - offset + tok_count]).astype(
            jnp.float32
        )
        conv_out = (
            conv_out
            + conv_taps[offset][None, :]
            * extended[edge - offset : edge - offset + tok_count]
            * same_doc[:, None]
        )
    mixed_in = jax.nn.silu(conv_out).astype(jnp.bfloat16)
    mixed_f = mixed_in.astype(jnp.float32)
    select = lax.psum(contract(mixed_in, w_select, "tc,jc->tj"), "wt")
    low_rank = select[:, :R].astype(jnp.bfloat16)
    write_vec = select[:, R : R + NS]
    read_vec = select[:, R + NS :]
    step_pre = contract(low_rank, w_step, "tr,rc->tc") + step_bias[None, :]
    step_size = jax.nn.softplus(step_pre)
    decay = -jnp.exp(decay_log)
    flag_vals = doc_start.astype(jnp.float32)
    summed_steps = jnp.cumsum(step_size, axis=0)
    total_steps = summed_steps[-1]
    block_keep = (last_count == 0).astype(jnp.float32)
    through = jnp.exp(decay * total_steps[None, :]) * block_keep
    drive = step_size * mixed_f * tail_keep[:, None]
    end_state = jnp.sum(
        jnp.exp(decay[None] * (total_steps[None, :] - summed_steps)[:, None, :])
        * drive[:, None, :]
        * write_vec[:, :, None],
        axis=0,
    )
    identity = (jnp.ones_like(through), jnp.zeros_like(through))
    carried_in = prefix((through, end_state), "seq", chain_maps, identity, False)[1]

    def forward_step(running, per_token):
        step_t, input_t, write_t, read_t, flag_t = per_token
        factor = jnp.exp(step_t[None, :] * decay) * (1.0 - flag_t)
        updated = factor * running + write_t[:, None] * (step_t * input_t)[None, :]
        return (updated, (jnp.sum(read_t[:, None] * updated, axis=0), running))

    final_state, (scan_out, prior_states) = lax.scan(
        forward_step, carried_in, (step_size, mixed_f, write_vec, read_vec, flag_vals), unroll=16
    )
    scanned = scan_out + skip_gain[None, :] * mixed_f
    switch_act = jax.nn.silu(switch)
    gated = (scanned * switch_act).astype(jnp.bfloat16)
    residual = token_vals + lax.psum(contract(gated, w_mix, "tc,dc->td"), "wt")
    second_out, second_normed, second_inv = rms_parts(residual, preffn_gain)
    second_in = second_out.astype(jnp.bfloat16)
    gate_pre = contract(second_in, w_gate, "td,df->tf")
    up_pre = contract(second_in, w_up, "td,df->tf")
    gate_act = jax.nn.silu(gate_pre)
    hidden = (gate_act * up_pre).astype(jnp.bfloat16)
    block_out = (
        residual
        + lax.psum(contract(hidden, w_down, "tf,df->td").astype(jnp.bfloat16), "wt").astype(
            jnp.float32
        )
    ).astype(jnp.bfloat16)
    back_inner, back_switch, back_select, back_step, back_mix, back_gate, back_up, back_down = (
        lax.all_gather(weights_local[0], "seq", axis=0, tiled=True),
        lax.all_gather(weights_local[1], "seq", axis=0, tiled=True),
        lax.all_gather(weights_local[2], "seq", axis=0, tiled=True),
        lax.all_gather(weights_local[3], "seq", axis=0, tiled=True),
        lax.all_gather(weights_local[4], "seq", axis=0, tiled=True),
        lax.all_gather(weights_local[5], "seq", axis=0, tiled=True),
        lax.all_gather(weights_local[6], "seq", axis=0, tiled=True),
        lax.all_gather(weights_local[7], "seq", axis=0, tiled=True),
    )
    d_hidden = contract(cotangent, back_down, "td,df->tf")
    grad_down = contract(cotangent, hidden, "td,tf->df")
    d_gate = (d_hidden * up_pre * silu_slope(gate_pre)).astype(jnp.bfloat16)
    d_up = (d_hidden * gate_act).astype(jnp.bfloat16)
    grad_gate = contract(second_in, d_gate, "td,tf->df")
    grad_up = contract(second_in, d_up, "td,tf->df")
    summed_ffn = (grad_gate, grad_up, grad_down)
    d_second = lax.psum(
        contract(d_gate, back_gate, "tf,df->td") + contract(d_up, back_up, "tf,df->td"), "wt"
    )
    d_from_norm, grad_preffn = rms_back(d_second, second_normed, second_inv, preffn_gain)
    d_residual = cotangent.astype(jnp.float32) + d_from_norm
    d_branch = d_residual.astype(jnp.bfloat16)
    d_gated = contract(d_branch, back_mix, "td,dc->tc")
    grad_mix = contract(d_branch, gated, "td,tc->dc")
    d_scanned = d_gated * switch_act
    d_switch = (d_gated * scanned * silu_slope(switch)).astype(jnp.bfloat16)
    grad_skip = jnp.sum(d_scanned * mixed_f, axis=0)
    head_weight = jnp.sum(
        jnp.exp(decay[None] * summed_steps[:, None, :])
        * (head_keep[:, None] * d_scanned)[:, None, :]
        * read_vec[:, :, None],
        axis=0,
    )
    carried_back = prefix((through, head_weight), "seq", chain_maps, identity, True)[1]

    def backward_step(running, per_token):
        adjoint, grad_decay = running
        step_t, input_t, write_t, read_t, flag_t, prior_t, dout_t = per_token
        factor = jnp.exp(step_t[None, :] * decay) * (1.0 - flag_t)
        updated = factor * prior_t + write_t[:, None] * (step_t * input_t)[None, :]
        total_adj = read_t[:, None] * dout_t[None, :] + adjoint
        through_decay = total_adj * prior_t * factor
        along = jnp.sum(total_adj * write_t[:, None], axis=0)
        d_step_t = along * input_t + jnp.sum(through_decay * decay, axis=0)
        d_input_t = along * step_t
        d_write_t = jnp.sum(total_adj * (step_t * input_t)[None, :], axis=1)
        d_read_t = jnp.sum(dout_t[None, :] * updated, axis=1)
        return (
            (factor * total_adj, grad_decay + through_decay * step_t[None, :]),
            (d_step_t, d_input_t, d_write_t, d_read_t),
        )

    (left_adjoint, grad_decay), (d_step, d_mixed_scan, d_write, d_read) = lax.scan(
        backward_step,
        (carried_back, jnp.zeros_like(decay)),
        (step_size, mixed_f, write_vec, read_vec, flag_vals, prior_states, d_scanned),
        reverse=True,
        unroll=16,
    )
    grad_decay_log = grad_decay * decay
    d_pre = d_step * jax.nn.sigmoid(step_pre)
    grad_step_bias = jnp.sum(d_pre, axis=0)
    d_pre_low = d_pre.astype(jnp.bfloat16)
    grad_step = contract(low_rank, d_pre_low, "tr,tc->rc")
    d_select = lax.psum(
        jnp.concatenate([contract(d_pre_low, back_step, "tc,rc->tr"), d_write, d_read], axis=1),
        "wt",
    ).astype(jnp.bfloat16)
    grad_select = contract(d_select, mixed_in, "tj,tc->jc")
    d_mixed = (
        d_mixed_scan + skip_gain[None, :] * d_scanned + contract(d_select, back_select, "tj,jc->tc")
    )
    d_conv = (d_mixed * silu_slope(conv_out)).astype(jnp.bfloat16)
    d_conv_f = d_conv.astype(jnp.float32)
    grad_conv_bias = jnp.sum(d_conv_f, axis=0)
    head_rows = jnp.where(head_keep[:edge, None] > 0, d_conv[:edge], jnp.zeros_like(d_conv[:edge]))
    next_rows = from_behind(head_rows, "seq", -1)
    ext_grad = jnp.concatenate([d_conv, next_rows], axis=0).astype(jnp.float32)
    ext_after = jnp.concatenate([counts, jnp.zeros((edge,), jnp.int32) + last_count])
    d_inner = jnp.zeros_like(d_conv_f)
    taps_rows = []
    for offset in range(KC):
        same_doc = (counts == ext_counts[edge - offset : edge - offset + tok_count]).astype(
            jnp.float32
        )
        taps_rows.append(
            jnp.sum(
                d_conv_f * extended[edge - offset : edge - offset + tok_count] * same_doc[:, None],
                axis=0,
            )
        )
        later_same = (ext_after[offset : offset + tok_count] == counts).astype(jnp.float32)
        d_inner = (
            d_inner
            + conv_taps[offset][None, :]
            * ext_grad[offset : offset + tok_count]
            * later_same[:, None]
        )
    grad_taps = jnp.stack(taps_rows, axis=0)
    d_inner_low = d_inner.astype(jnp.bfloat16)
    grad_inner = contract(first_in, d_inner_low, "td,tc->dc")
    grad_switch = contract(first_in, d_switch, "td,tc->dc")
    d_first = lax.psum(
        contract(d_inner_low, back_inner, "tc,dc->td")
        + contract(d_switch, back_switch, "tc,dc->td"),
        "wt",
    )
    d_tokens_norm, grad_premix = rms_back(d_first, first_normed, first_inv, premix_gain)
    tokens_grad = (d_residual + d_tokens_norm).astype(jnp.bfloat16)
    summed_big = (
        lax.psum_scatter(grad_inner, "seq", scatter_dimension=0, tiled=True),
        lax.psum_scatter(grad_switch, "seq", scatter_dimension=0, tiled=True),
        lax.psum_scatter(grad_select, "seq", scatter_dimension=0, tiled=True),
        lax.psum_scatter(grad_step, "seq", scatter_dimension=0, tiled=True),
        lax.psum_scatter(grad_mix, "seq", scatter_dimension=0, tiled=True),
        lax.psum_scatter(summed_ffn[0], "seq", scatter_dimension=0, tiled=True),
        lax.psum_scatter(summed_ffn[1], "seq", scatter_dimension=0, tiled=True),
        lax.psum_scatter(summed_ffn[2], "seq", scatter_dimension=0, tiled=True),
    )
    summed_small = lax.psum(
        (
            grad_premix,
            grad_taps,
            grad_conv_bias,
            grad_step_bias,
            grad_decay_log,
            grad_skip,
            grad_preffn,
        ),
        "seq",
    )
    return (
        block_out,
        tokens_grad,
        summed_small[0],
        summed_big[0],
        summed_big[1],
        summed_small[1],
        summed_small[2],
        summed_big[2],
        summed_big[3],
        summed_small[3],
        summed_small[4],
        summed_small[5],
        summed_big[4],
        summed_small[6],
        summed_big[5],
        summed_big[6],
        summed_big[7],
    )


def solution(mesh):
    placed = (
        P("seq", None),
        P("seq", None),
        P("seq"),
        P(),
        P("seq", "wt"),
        P("seq", "wt"),
        P(None, "wt"),
        P("wt"),
        P("seq", "wt"),
        P("seq", "wt"),
        P("wt"),
        P(None, "wt"),
        P("wt"),
        P("seq", "wt"),
        P(),
        P("seq", "wt"),
        P("seq", "wt"),
        P("seq", "wt"),
    )
    return jax.shard_map(
        local,
        mesh=mesh,
        in_specs=placed,
        out_specs=(
            P("seq", None),
            P("seq", None),
            P(),
            P("seq", "wt"),
            P("seq", "wt"),
            P(None, "wt"),
            P("wt"),
            P("seq", "wt"),
            P("seq", "wt"),
            P("wt"),
            P(None, "wt"),
            P("wt"),
            P("seq", "wt"),
            P(),
            P("seq", "wt"),
            P("seq", "wt"),
            P("seq", "wt"),
        ),
        check_vma=False,
    )
```

profile of v0, /device:TPU:0, one launch (start us, length us, event | category | flops | bytes accessed | tf_op | source)
XLA Modules:
  0.0 2301.1 jit_solution(11940299952191105884)
XLA Ops:
  13.7 35.7 %all-gather.11.cloned.1.call-done = bf16[2048,1024]{1,0:T(8,128)(2,1)} async-done(((bf16[256,1024]{1,0:T(8,128)(2,1)}), bf16[2048,1024]{1,0:T(8,128)(2,1)}) %all-gather.11.cloned.1.call-update) | async-done | bytes 4194320 | tf_op jit(solution)/shard_map/all_gather | solution.py:96
  49.4 3.8 convolution_convert_fusion.1
  53.3 2.2 collective-permute-start
  55.5 9.6 all-gather.3
  65.4 1.8 multiply_convert_fusion.6
  70.3 8.9 all_gather.54
  81.0 22.1 all-reduce.13.cloned.1.call-done
  108.3 11.1 all-gather
  121.8 4.5 multiply_reduce_fusion.81
  126.3 12.7 all-gather.1
  141.3 304.8 %while.67 = (s32[]{:T(128)}, f32[16,1024]{1,0:T(8,128)S(1)}, f32[16,16,1024]{2,1,0:T(8,128)}, f32[16,16,16,1024]{3,2,1,0:T(8,128)}, f32[16,16,1024]{2,1,0:T(8,12...) while((s32[]{:T(128)}, f32[16,1024]{1,0:T(8,128)S(1)}, ...), condition=%wide.region_26.27_spmd, body=%wide.region_9.26_spmd.sunk | while | flops 3145761 | bytes 7686521 | solution.py:162
  446.1 4.9 multiply_convert_fusion.5
  451.0 5.0 fusion.162
  458.1 83.3 %all-reduce.15.cloned.1.call-done = f32[256,2048]{1,0:T(8,128)} async-done(((f32[256,2048]{1,0:T(8,128)}), f32[256,2048]{1,0:T(8,128)}) %all-reduce.15.cloned.1.call-update) | async-done | bytes 2097168 | tf_op jit(solution)/shard_map/psum | solution.py:168
  541.5 1.9 multiply_reduce_fusion.84
  544.7 51.8 %all-gather.17.cloned.1.call-done = bf16[2048,2048]{1,0:T(8,128)(2,1)} async-done(((bf16[256,2048]{1,0:T(8,128)(2,1)}), bf16[2048,2048]{1,0:T(8,128)(2,1)}) %all-gather.17.cloned.1.call-update) | async-done | bytes 8388624 | tf_op jit(solution)/shard_map/all_gather | solution.py:101
  596.6 7.4 fusion.163
  604.0 48.9 %all-gather.19.cloned.1.call-done = bf16[2048,2048]{1,0:T(8,128)(2,1)} async-done(((bf16[256,2048]{1,0:T(8,128)(2,1)}), bf16[2048,2048]{1,0:T(8,128)(2,1)}) %all-gather.19.cloned.1.call-update) | async-done | bytes 8388624 | tf_op jit(solution)/shard_map/all_gather | solution.py:102
  652.9 7.4 fusion.164
  660.3 48.9 %all-gather.21.cloned.1.call-done = bf16[2048,2048]{1,0:T(8,128)(2,1)} async-done(((bf16[256,2048]{1,0:T(8,128)(2,1)}), bf16[2048,2048]{1,0:T(8,128)(2,1)}) %all-gather.21.cloned.1.call-update) | async-done | bytes 8388624 | tf_op jit(solution)/shard_map/all_gather | solution.py:103
  709.2 8.8 multiply_convert_fusion
  718.0 6.5 fusion.165
  724.6 3.7 convolution_add_fusion.1
  728.3 12.0 all-reduce.17.cloned.1.call-start
  740.2 7.1 convolution_convert_fusion
  747.9 1.9 rev.6
  749.8 65.1 %all-reduce.19.cloned.1.call-done = f32[256,2048]{1,0:T(8,128)} async-done(((f32[256,2048]{1,0:T(8,128)}), f32[256,2048]{1,0:T(8,128)}) %all-reduce.19.cloned.1.call-update) | async-done | bytes 2097168 | tf_op jit(solution)/shard_map/psum | solution.py:198
  814.9 2.7 multiply_reduce_fusion.82
  817.7 51.0 %all-reduce.17.cloned.1.call-done = bf16[256,2048]{1,0:T(8,128)(2,1)} async-done(((bf16[256,2048]{1,0:T(8,128)(2,1)}), bf16[256,2048]{1,0:T(8,128)(2,1)}) %all-reduce.17.cloned.1.call-update) | async-done | bytes 1048592 | tf_op jit(solution)/shard_map/psum | solution.py:177
  868.6 4.0 multiply_add_fusion.32
  873.2 3.1 multiply_reduce_fusion.85
  877.5 4.2 multiply_reduce_fusion.80
  881.8 9.8 all-gather.2
  891.7 6.3 while.69
  900.5 587.8 %while.70 = (s32[]{:T(128)}, f32[16,1024]{1,0:T(8,128)S(1)}, f32[16,1024]{1,0:T(8,128)S(1)}, f32[16,16,1024]{2,1,0:T(8,128)S(1)}, f32[16,16,1024]{2,1,0:T(8,128)...) while((s32[]{:T(128)}, f32[16,1024]{1,0:T(8,128)S(1)}, ...), condition=%wide.region_100.101_spmd.clone, body=%wide.region_35.100_spmd.clone.sunk | while | flops 7618083 | bytes 6783583 | solution.py:234
  953.4 1.8 multiply_reduce_fusion.104
  1026.8 1.8 multiply_reduce_fusion.104
  1488.3 2.8 bitcast_add_fusion.2
  1491.3 1.9 fusion.156
  1494.5 20.4 all-reduce.24
  1515.0 2.7 fusion.114
  1525.8 2.6 convolution_add_fusion
  1529.6 9.3 convolution_bitcast_fusion
  1541.6 4.6 fusion.148
  1547.8 5.5 fusion.135
  1553.4 5.6 fusion.150
  1559.1 9.6 fusion.167
  1568.8 10.0 fusion.168
  1580.8 2.1 fusion.169
  1582.9 20.6 fusion
  1603.6 1.9 collective-permute-start.2
  1610.1 3.8 all-reduce.21.cloned.1.call-done
  1613.9 2.2 fusion.109
  1616.2 25.0 %all-reduce.4 = (f32[2048]{0:T(1024)}, f32[4,1024]{1,0:T(4,128)}, f32[1024]{0:T(1024)}, f32[1024]{0:T(1024)}, f32[1024]{0:T(1024)}, /*index=5*/f32[2048]{0:T(1024)}) all-reduce(f32[2048]{0:T(1024)S(1)} %get-tuple-element.897, f32[4,1024]{1,0:T(4,128)S(1)} %pad_maximum_fusion.1, ...), channel_id=1, replica_groups=mesh['seq'=8,'wt'=4] {'seq'}, use_global_device_ids=true, to_apply=%region_105.106 | all-reduce | flops 11264 | bytes 90112 | tf_op jit(solution)/shard_map/psum | solution.py:301
  1641.2 3.5 fusion.108
  1644.7 88.0 %reduce-scatter.22.cloned.1.call-done = f32[256,2048]{0,1:T(8,128)} async-done(((f32[2048,2048]{0,1:T(8,128)}), f32[256,2048]{0,1:T(8,128)}) %reduce-scatter.22.cloned.1.call-update) | async-done | bytes 2097168 | tf_op jit(solution)/shard_map/reduce_scatter | solution.py:299
  1732.7 2.9 copy.79
  1735.6 53.5 %all-reduce.23.cloned.1.call-done = f32[16,1024]{1,0:T(8,128)} async-done(((f32[16,1024]{1,0:T(8,128)}), f32[16,1024]{1,0:T(8,128)}) %all-reduce.23.cloned.1.call-update) | async-done | bytes 65552 | tf_op jit(solution)/shard_map/psum | solution.py:301
  1789.2 37.1 %reduce-scatter.14.cloned.1.call-done = f32[16,1024]{1,0:T(8,128)} async-done(((f32[128,1024]{1,0:T(8,128)}), f32[16,1024]{1,0:T(8,128)}) %reduce-scatter.14.cloned.1.call-update) | async-done | bytes 65552 | tf_op jit(solution)/shard_map/reduce_scatter | solution.py:295
  1826.2 75.6 %reduce-scatter.12.cloned.1.call-done = f32[256,1024]{1,0:T(8,128)} async-done(((f32[2048,1024]{1,0:T(8,128)}), f32[256,1024]{1,0:T(8,128)}) %reduce-scatter.12.cloned.1.call-update) | async-done | bytes 1048592 | tf_op jit(solution)/shard_map/reduce_scatter | solution.py:293
  1901.8 75.2 %reduce-scatter.16.cloned.1.call-done = f32[256,1024]{1,0:T(8,128)} async-done(((f32[2048,1024]{1,0:T(8,128)}), f32[256,1024]{1,0:T(8,128)}) %reduce-scatter.16.cloned.1.call-update) | async-done | bytes 1048592 | tf_op jit(solution)/shard_map/reduce_scatter | solution.py:296
  1977.0 75.6 %reduce-scatter.10.cloned.1.call-done = f32[256,1024]{1,0:T(8,128)} async-done(((f32[2048,1024]{1,0:T(8,128)}), f32[256,1024]{1,0:T(8,128)}) %reduce-scatter.10.cloned.1.call-update) | async-done | bytes 1048592 | tf_op jit(solution)/shard_map/reduce_scatter | solution.py:292
  2052.5 120.0 %reduce-scatter.18.cloned.1.call-done = f32[256,2048]{1,0:T(8,128)} async-done(((f32[2048,2048]{1,0:T(8,128)}), f32[256,2048]{1,0:T(8,128)}) %reduce-scatter.18.cloned.1.call-update) | async-done | bytes 2097168 | tf_op jit(solution)/shard_map/reduce_scatter | solution.py:297
  2172.5 120.1 %reduce-scatter.20.cloned.1.call-done = f32[256,2048]{1,0:T(8,128)} async-done(((f32[2048,2048]{1,0:T(8,128)}), f32[256,2048]{1,0:T(8,128)}) %reduce-scatter.20.cloned.1.call-update) | async-done | bytes 2097168 | tf_op jit(solution)/shard_map/reduce_scatter | solution.py:298
  (1851 shorter events, 624.4 us)
Async XLA Ops:
  7.2 42.2 %all-gather.11.cloned.1.call-start = ((), (), s32[]{:S(2)}) async-start(), calls=%async_computation.7 | async-start | bytes 4718592 | tf_op jit(solution)/shard_map/all_gather | solution.py:96
  7.9 95.2 %all-reduce.13.cloned.1.call-start = ((), (), s32[]{:S(2)}) async-start(), calls=%async_computation.8 | async-start | bytes 327680 | tf_op jit(solution)/shard_map/psum | solution.py:134
  12.7 52.7 %copy-start.49 = (f32[256]{0:T(256)}, f32[256]{0:T(256)S(1)}, u32[]{:S(2)}) copy-start(f32[256]{0:T(256)S(1)} %get-tuple-element.1249) | copy-start | bytes 3076
  12.7 52.7 %copy-start.51 = (f32[256]{0:T(256)}, f32[256]{0:T(256)S(1)}, u32[]{:S(2)}) copy-start(f32[256]{0:T(256)S(1)} %get-tuple-element.1250) | copy-start | bytes 3076
  12.7 52.7 %copy-start.53 = (f32[256]{0:T(256)}, f32[256]{0:T(256)S(1)}, u32[]{:S(2)}) copy-start(f32[256]{0:T(256)S(1)} %get-tuple-element.1251) | copy-start | bytes 3076
  12.7 433.3 %copy-start.31 = (f32[256]{0:T(256)}, f32[256]{0:T(256)S(1)}, u32[]{:S(2)}) copy-start(f32[256]{0:T(256)S(1)} %add_rsqrt_fusion.1) | copy-start | bytes 3076
  13.6 51.7 %copy-start.34 = (f32[1,1024]{1,0:T(1,128)}, f32[1,1024]{1,0:T(1,128)S(1)}, u32[]{:S(2)}) copy-start(f32[1,1024]{1,0:T(1,128)S(1)} %get-tuple-element.1243) | copy-start | bytes 12292
  13.6 51.7 %copy-start.36 = (f32[1,1024]{1,0:T(1,128)}, f32[1,1024]{1,0:T(1,128)S(1)}, u32[]{:S(2)}) copy-start(f32[1,1024]{1,0:T(1,128)S(1)} %get-tuple-element.1244) | copy-start | bytes 12292
  13.7 51.7 %copy-start.38 = (f32[1,1024]{1,0:T(1,128)}, f32[1,1024]{1,0:T(1,128)S(1)}, u32[]{:S(2)}) copy-start(f32[1,1024]{1,0:T(1,128)S(1)} %get-tuple-element.1245) | copy-start | bytes 12292
  13.7 51.7 %copy-start.40 = (f32[1,1024]{1,0:T(1,128)}, f32[1,1024]{1,0:T(1,128)S(1)}, u32[]{:S(2)}) copy-start(f32[1,1024]{1,0:T(1,128)S(1)} %get-tuple-element.1246) | copy-start | bytes 12292
  13.7 41.8 %copy-start.33 = (bf16[20,1024]{1,0:T(8,128)(2,1)S(1)}, bf16[20,1024]{1,0:T(8,128)(2,1)}, u32[]{:S(2)}) copy-start(bf16[20,1024]{1,0:T(8,128)(2,1)} %param.34) | copy-start | bytes 122884
  53.2 12.2 copy-start.44
  53.3 11.9 collective-permute-start
  67.2 378.8 %copy-start.5 = (bf16[256,1024]{1,0:T(8,128)(2,1)}, bf16[256,1024]{1,0:T(8,128)(2,1)S(1)}, u32[]{:S(2)}) copy-start(bf16[256,1024]{1,0:T(8,128)(2,1)S(1)} %get-tuple-element.1012) | copy-start | bytes 1572868
  67.2 35.9 %copy-start.62 = (f32[1024]{0:T(1024)S(1)}, f32[1024]{0:T(1024)}, u32[]{:S(2)}) copy-start(f32[1024]{0:T(1024)} %param.36) | copy-start | bytes 12292
  68.3 377.8 %all-gather.13.cloned.1.call-start = ((), (), s32[]{:S(2)}) async-start(), calls=%async_computation.9 | async-start | bytes 4718592 | tf_op jit(solution)/shard_map/all_gather | solution.py:97
  69.0 382.0 %all-gather.15.cloned.1.call-start = ((), (), s32[]{:S(2)}) async-start(), calls=%async_computation.10 | async-start | bytes 4718592 | tf_op jit(solution)/shard_map/all_gather | solution.py:100
  69.6 471.9 %all-reduce.15.cloned.1.call-start = ((), (), s32[]{:S(2)}) async-start(), calls=%async_computation.11 | async-start | bytes 4194304 | tf_op jit(solution)/shard_map/psum | solution.py:168
  79.3 25.5 %copy-start.20 = (bf16[128,1024]{1,0:T(8,128)(2,1)}, bf16[128,1024]{1,0:T(8,128)(2,1)S(1)}, u32[]{:S(2)}) copy-start(bf16[128,1024]{1,0:T(8,128)(2,1)S(1)} %all_gather.54) | copy-start | bytes 786436
  104.8 15.4 copy-start.12
  141.3 304.8 %copy-start = (bf16[256,2048]{1,0:T(8,128)(2,1)S(1)}, bf16[256,2048]{1,0:T(8,128)(2,1)}, u32[]{:S(2)}) copy-start(bf16[256,2048]{1,0:T(8,128)(2,1)} %param.26) | copy-start | bytes 3145732
  141.3 304.8 %copy-start.22 = (f32[2048]{0:T(1024)S(1)}, f32[2048]{0:T(1024)}, u32[]{:S(2)}) copy-start(f32[2048]{0:T(1024)} %param.29) | copy-start | bytes 24580
  141.3 304.8 %copy-start.45 = (f32[1024]{0:T(1024)S(1)}, f32[1024]{0:T(1024)}, u32[]{:S(2)}) copy-start(f32[1024]{0:T(1024)} %param.38) | copy-start | bytes 12292
  446.0 5.0 copy-start.26
  451.0 5.0 copy-start.23
  456.0 140.6 %all-gather.17.cloned.1.call-start = ((), (), s32[]{:S(2)}) async-start(), calls=%async_computation.12 | async-start | bytes 9437184 | tf_op jit(solution)/shard_map/all_gather | solution.py:101
  456.6 196.3 %all-gather.19.cloned.1.call-start = ((), (), s32[]{:S(2)}) async-start(), calls=%async_computation.13 | async-start | bytes 9437184 | tf_op jit(solution)/shard_map/all_gather | solution.py:102
  457.3 251.9 %all-gather.21.cloned.1.call-start = ((), (), s32[]{:S(2)}) async-start(), calls=%async_computation.14 | async-start | bytes 9437184 | tf_op jit(solution)/shard_map/all_gather | solution.py:103
  458.1 85.3 %copy-start.30 = (f32[2048]{0:T(1024)S(1)}, f32[2048]{0:T(1024)}, u32[]{:S(2)}) copy-start(f32[2048]{0:T(1024)} %param.40) | copy-start | bytes 24580
  458.1 356.8 %all-reduce.19.cloned.1.call-start = ((), (), s32[]{:S(2)}) async-start(), calls=%async_computation.16 | async-start | bytes 4194304 | tf_op jit(solution)/shard_map/psum | solution.py:198
  718.0 6.6 copy-start.19
  718.0 6.6 copy-start.18
  718.0 6.6 copy-start.59
  728.3 140.4 %all-reduce.17.cloned.1.call-start = ((), (), s32[]{:S(2)}) async-start(), calls=%async_computation.15 | async-start | bytes 2097152 | tf_op jit(solution)/shard_map/psum | solution.py:177
  747.4 866.6 %all-reduce.21.cloned.1.call-start = ((), (), s32[]{:S(2)}) async-start(), calls=%async_computation.17 | async-start | bytes 4194304 | tf_op jit(solution)/shard_map/psum | solution.py:284
  868.6 4.0 copy-start.6
  868.6 4.0 copy-start.21
  868.6 4.0 copy-start.61
  868.6 4.6 copy-start.63
  1491.2 23.7 %copy-start.2 = (f32[259,1024]{1,0:T(8,128)S(1)}, f32[259,1024]{1,0:T(8,128)}, u32[]{:S(2)}) copy-start(f32[259,1024]{1,0:T(8,128)} %copy-done.1) | copy-start | bytes 3182596
  1491.2 23.7 %copy-start.50 = (f32[256]{0:T(256)S(1)}, f32[256]{0:T(256)}, u32[]{:S(2)}) copy-start(f32[256]{0:T(256)} %copy-done.49) | copy-start | bytes 3076
  1491.2 23.7 %copy-start.52 = (f32[256]{0:T(256)S(1)}, f32[256]{0:T(256)}, u32[]{:S(2)}) copy-start(f32[256]{0:T(256)} %copy-done.51) | copy-start | bytes 3076
  1491.3 23.7 %copy-start.54 = (f32[256]{0:T(256)S(1)}, f32[256]{0:T(256)}, u32[]{:S(2)}) copy-start(f32[256]{0:T(256)} %copy-done.53) | copy-start | bytes 3076
  1491.3 23.7 %copy-start.17 = (bf16[160,1024]{1,0:T(8,128)(2,1)S(1)}, bf16[160,1024]{1,0:T(8,128)(2,1)}, u32[]{:S(2)}) copy-start(bf16[160,1024]{1,0:T(8,128)(2,1)} %copy-done.16) | copy-start | bytes 983044
  1514.9 6.1 copy-start.35
  1515.0 6.1 copy-start.37
  1515.0 6.1 copy-start.39
  1515.0 6.1 copy-start.41
  1515.0 6.1 copy-start.46
  1515.0 6.1 copy-start.47
  1515.0 6.1 copy-start.48
  1517.9 3.1 collective-permute-start.1
  1528.4 204.3 %reduce-scatter.22.cloned.1.call-start = ((), (), s32[]{:S(2)}) async-start(), calls=%async_computation.25 | async-start | bytes 18874368 | tf_op jit(solution)/shard_map/reduce_scatter | solution.py:299
  1539.0 250.2 %all-reduce.23.cloned.1.call-start = ((), (), s32[]{:S(2)}) async-start(), calls=%async_computation.21 | async-start | bytes 131072 | tf_op jit(solution)/shard_map/psum | solution.py:301
  1540.4 285.8 %reduce-scatter.14.cloned.1.call-start = ((), (), s32[]{:S(2)}) async-start(), calls=%async_computation.20 | async-start | bytes 589824 | tf_op jit(solution)/shard_map/reduce_scatter | solution.py:295
  1541.6 360.2 %reduce-scatter.12.cloned.1.call-start = ((), (), s32[]{:S(2)}) async-start(), calls=%async_computation.19 | async-start | bytes 9437184 | tf_op jit(solution)/shard_map/reduce_scatter | solution.py:293
  1546.3 430.7 %reduce-scatter.16.cloned.1.call-start = ((), (), s32[]{:S(2)}) async-start(), calls=%async_computation.22 | async-start | bytes 9437184 | tf_op jit(solution)/shard_map/reduce_scatter | solution.py:296
  1553.4 499.2 %reduce-scatter.10.cloned.1.call-start = ((), (), s32[]{:S(2)}) async-start(), calls=%async_computation.18 | async-start | bytes 9437184 | tf_op jit(solution)/shard_map/reduce_scatter | solution.py:292
  1559.1 613.5 %reduce-scatter.18.cloned.1.call-start = ((), (), s32[]{:S(2)}) async-start(), calls=%async_computation.23 | async-start | bytes 18874368 | tf_op jit(solution)/shard_map/reduce_scatter | solution.py:297
  1568.8 723.9 %reduce-scatter.20.cloned.1.call-start = ((), (), s32[]{:S(2)}) async-start(), calls=%async_computation.24 | async-start | bytes 18874368 | tf_op jit(solution)/shard_map/reduce_scatter | solution.py:298
  1603.5 12.7 copy-start.42
  1603.5 12.7 copy-start.56
  1603.6 4.7 collective-permute-start.2
  1605.5 2.8 collective-permute-start.3
  (23 other events, 48.8 us)
Sparse Core Ops, SparseCore 0:
  9.9 39.4 all-gather.10
  68.4 34.6 all-reduce.12
  105.2 39.1 all-gather.12
  146.2 36.7 all-gather.14
  456.1 85.3 all-reduce.14
  543.2 53.3 all-gather.16
  598.5 54.3 all-gather.18
  654.8 54.3 all-gather.20
  728.4 86.4 all-reduce.18
  817.8 50.7 all-reduce.16
  1528.5 85.3 all-reduce.20
  1617.8 114.9 reduce-scatter.21
  1736.6 52.4 all-reduce.22
  1792.7 33.5 reduce-scatter.13
  1830.5 71.2 reduce-scatter.11
  1905.7 71.2 reduce-scatter.15
  1981.2 71.2 reduce-scatter.9
  2056.5 115.9 reduce-scatter.17
  2176.7 115.9 reduce-scatter.19
where the time goes:
time: 2330 us; the launch traced here: 2300 us
  waiting for transfers between devices  1060 us (45%)
  other arithmetic  346 us (15%)
  loops' own time  322 us (14%)
  local copies, waits for them, and re-layouts  299 us (13%)
  blocking collectives  118 us (5%)
  matrix products  116 us (5%)
    reduce_sum x112, other arithmetic, backward_step(): d_step_t = along * input_t + jnp.sum(through_decay * decay, axis=0)  198 us
    another operation x1, loops' own time, local(): lax.scan(forward_step, carried_in, (step_size, mixed_f, write_vec, read_v...  163 us
    another operation x1, loops' own time, local(): lax.scan(backward_step, (carried_back, jnp.zeros_like(decay)), (step_size...  159 us
    reduce_scatter x1, waiting for transfers between devices, local(): lax.psum_scatter(summed_ffn[1], 'seq', scatter_dimension=0, tiled=True)  120 us
    reduce_scatter x1, waiting for transfers between devices, local(): lax.psum_scatter(summed_ffn[0], 'seq', scatter_dimension=0, tiled=True)  120 us
    dot_general x24, matrix products, contract(): jnp.einsum(pattern, left_op, right_op, preferred_element_type=jnp.float32)  116 us
    reduce_scatter x1, waiting for transfers between devices, local(): lax.psum_scatter(summed_ffn[2], 'seq', scatter_dimension=0, tiled=True)  88 us
    psum x1, waiting for transfers between devices, local(): residual = token_vals + lax.psum(contract(gated, w_mix, 'tc,dc->td'), 'wt')  83.3 us
  transfers between devices with their start and end apart: 23, of which 19 were waited for; matrix products, arithmetic and copies ran while one was open for 12% of the time, Pallas kernels for 0%

commit v1 on v0

v1 whole, which is shorter than its diff:
```python
import functools

import jax
import jax.numpy as jnp
from jax import lax
from jax.experimental import pallas as pl
from jax.experimental.pallas import tpu as pltpu
from jax.sharding import PartitionSpec as P

NS = 16
R = 128
KC = 4
EPS = 1e-05
F32 = jnp.float32
BF16 = jnp.bfloat16
LOG2E = 1.4426950408889634
FAR = 1e30
MESH = pl.DeviceIdType.MESH
VMEM = pl.BlockSpec(memory_space=pltpu.VMEM)
SMEM = pl.BlockSpec(memory_space=pltpu.SMEM)
MIB = 2**20


def greet(axes):
    barrier = pltpu.get_barrier_semaphore()
    total = 0
    for axis in axes:
        n, me = lax.axis_size(axis), lax.axis_index(axis)
        for k in range(1, n):
            pl.semaphore_signal(
                barrier, inc=1, device_id={axis: lax.rem(me + k, n)}, device_id_type=MESH
            )
        total += n - 1
    pl.semaphore_wait(barrier, total)


def remote(src, dst, sems, slot, axis, peer):
    return pltpu.make_async_remote_copy(
        src_ref=src,
        dst_ref=dst,
        send_sem=sems.at[0, slot],
        recv_sem=sems.at[1, slot],
        device_id={axis: peer},
        device_id_type=MESH,
    )


def send(src, dst, sems, slot, axis, peer):
    copy = remote(src, dst, sems, slot, axis, peer)
    copy.start()
    return copy


def scatter_start(part, recv, sems, axis):
    n, me = lax.axis_size(axis), lax.axis_index(axis)
    rows = recv.shape[1]
    copies = []
    for k in range(1, n):
        peer = lax.rem(me + k, n)
        copies.append(
            send(part.at[pl.ds(peer * rows, rows)], recv.at[k - 1], sems, k - 1, axis, peer)
        )
    return copies


def gather_start(whole, rows, sems, axis):
    n, me = lax.axis_size(axis), lax.axis_index(axis)
    mine = whole.at[pl.ds(me * rows, rows)]
    return [send(mine, mine, sems, k - 1, axis, lax.rem(me + k, n)) for k in range(1, n)]


def arrived(copies):
    for copy in copies:
        copy.wait_recv()


def left(copies):
    for copy in copies:
        copy.wait_send()


def pair_sems(n):
    return pltpu.SemaphoreType.DMA((2, n - 1))


def summed(part, recv, at, step, row0):
    total = part[pl.ds(row0 + at, step)].astype(F32)
    for k in range(recv.shape[0]):
        total = total + recv[k, pl.ds(at, step)].astype(F32)
    return total


def step_rows(rows, step, body):
    def run(i, carry):
        body(pl.multiple_of(i * step, step))
        return carry

    lax.fori_loop(0, rows // step, run, 0)


def wt_sum_kernel(part, out, recv, s_scatter, s_gather):
    me = lax.axis_index("wt")
    rows = recv.shape[1]
    greet(("wt",))
    first = scatter_start(part, recv, s_scatter, "wt")
    arrived(first)
    out[pl.ds(me * rows, rows)] = summed(part, recv, 0, rows, me * rows)
    second = gather_start(out, rows, s_gather, "wt")
    arrived(second)
    left(first)
    left(second)


def wt_sum(part, n_wt, ident):
    rows, cols = part.shape
    return pl.pallas_call(
        wt_sum_kernel,
        out_shape=jax.ShapeDtypeStruct((rows, cols), F32),
        in_specs=[VMEM],
        out_specs=VMEM,
        scratch_shapes=[
            pltpu.VMEM((n_wt - 1, rows // n_wt, cols), F32),
            pair_sems(n_wt),
            pair_sems(n_wt),
        ],
        compiler_params=pltpu.CompilerParams(collective_id=ident, has_side_effects=True),
        cost_estimate=pl.CostEstimate(flops=10**5, bytes_accessed=10**6, transcendentals=0),
    )(part)


def second_norm_kernel(part, tok, gain, out, res, recv, s_scatter, s_gather):
    me = lax.axis_index("wt")
    rows = recv.shape[1]
    greet(("wt",))
    first = scatter_start(part, recv, s_scatter, "wt")
    arrived(first)
    row0 = me * rows

    def body(at):
        r = tok[pl.ds(at, 16)] + summed(part, recv, at, 16, row0)
        res[pl.ds(at, 16)] = r
        inverse = lax.rsqrt(jnp.mean(r * r, axis=-1, keepdims=True) + EPS)
        out[pl.ds(pl.multiple_of(row0 + at, 16), 16)] = (r * inverse * gain[...]).astype(BF16)

    step_rows(rows, 16, body)
    second = gather_start(out, rows, s_gather, "wt")
    arrived(second)
    left(first)
    left(second)


def second_norm(part, tok_own, gain, n_wt, ident):
    rows, cols = part.shape
    own = rows // n_wt
    return pl.pallas_call(
        second_norm_kernel,
        out_shape=[
            jax.ShapeDtypeStruct((rows, cols), BF16),
            jax.ShapeDtypeStruct((own, cols), F32),
        ],
        in_specs=[VMEM] * 3,
        out_specs=[VMEM] * 2,
        scratch_shapes=[
            pltpu.VMEM((n_wt - 1, own, cols), BF16),
            pair_sems(n_wt),
            pair_sems(n_wt),
        ],
        compiler_params=pltpu.CompilerParams(collective_id=ident, has_side_effects=True),
        cost_estimate=pl.CostEstimate(flops=10**6, bytes_accessed=10**8, transcendentals=0),
    )(part, tok_own, gain[None])


def norm_back_rows(grad, vals, gain):
    inverse = lax.rsqrt(jnp.mean(vals * vals, axis=-1, keepdims=True) + EPS)
    normed = vals * inverse
    scaled = grad * gain
    mean = jnp.mean(scaled * normed, axis=-1, keepdims=True)
    return inverse * (scaled - normed * mean), grad * normed


def second_back_kernel(part, res, cot, gain, out, d_res, gain_grad, recv, s_scatter, s_gather):
    me = lax.axis_index("wt")
    rows = recv.shape[1]
    greet(("wt",))
    first = scatter_start(part, recv, s_scatter, "wt")
    gain_grad[...] = jnp.zeros_like(gain_grad)
    arrived(first)
    row0 = me * rows

    def body(at):
        grad = summed(part, recv, at, 16, row0)
        back, prod = norm_back_rows(grad, res[pl.ds(at, 16)], gain[...])
        gain_grad[...] += prod[:8] + prod[8:]
        d = cot[pl.ds(at, 16)] + back
        d_res[pl.ds(at, 16)] = d
        out[pl.ds(pl.multiple_of(row0 + at, 16), 16)] = d.astype(BF16)

    step_rows(rows, 16, body)
    second = gather_start(out, rows, s_gather, "wt")
    arrived(second)
    left(first)
    left(second)


def second_back(part, res, cot_own, gain, n_wt, ident):
    rows, cols = part.shape
    own = rows // n_wt
    return pl.pallas_call(
        second_back_kernel,
        out_shape=[
            jax.ShapeDtypeStruct((rows, cols), BF16),
            jax.ShapeDtypeStruct((own, cols), F32),
            jax.ShapeDtypeStruct((8, cols), F32),
        ],
        in_specs=[VMEM] * 4,
        out_specs=[VMEM] * 3,
        scratch_shapes=[
            pltpu.VMEM((n_wt - 1, own, cols), BF16),
            pair_sems(n_wt),
            pair_sems(n_wt),
        ],
        compiler_params=pltpu.CompilerParams(collective_id=ident, has_side_effects=True),
        cost_estimate=pl.CostEstimate(flops=10**6, bytes_accessed=10**8, transcendentals=0),
    )(part, res, cot_own, gain[None])


def last_kernel(
    part, tok, d_res, gain, rows_small, by_chan, gain_grad2,
    out, small_out, chan_out, gains_out,
    recv, recv_small, recv_chan, gain_buf, recv_gz, recv_gs,
    s_scatter, s_gather, s_small, s_chan, s_gz, s_gs,
):
    me = lax.axis_index("wt")
    seq, n_seq = lax.axis_index("seq"), lax.axis_size("seq")
    rows = recv.shape[1]
    greet(("wt", "seq"))
    first = scatter_start(part, recv, s_scatter, "wt")
    smalls, chans = [], []
    for k in range(1, n_seq):
        peer = lax.rem(seq + k, n_seq)
        smalls.append(
            send(rows_small.at[peer], recv_small.at[k - 1], s_small, k - 1, "seq", peer)
        )
        chans.append(send(by_chan, recv_chan.at[k - 1], s_chan, k - 1, "seq", peer))
    gain_buf[1] = gain_grad2[...]
    gain_buf[0] = jnp.zeros_like(gain_grad2)
    arrived(smalls)
    total = rows_small[seq]
    for k in range(n_seq - 1):
        total = total + recv_small[k]
    small_out[...] = total
    arrived(chans)
    total = jnp.zeros_like(chan_out)
    for pos in range(n_seq):
        slot = lax.rem(seq - pos + n_seq, n_seq)
        other = recv_chan[jnp.maximum(slot - 1, 0)]
        total = total + jnp.where(slot == 0, by_chan[...], other)
    chan_out[...] = total
    arrived(first)
    row0 = me * rows

    def body(at):
        grad = summed(part, recv, at, 16, row0)
        back, prod = norm_back_rows(grad, tok[pl.ds(at, 16)], gain[...])
        gain_buf[0] += prod[:8] + prod[8:]
        out[pl.ds(pl.multiple_of(row0 + at, 16), 16)] = (d_res[pl.ds(at, 16)] + back).astype(BF16)

    step_rows(rows, 16, body)
    second = gather_start(out, rows, s_gather, "wt")
    n_wt = lax.axis_size("wt")
    zs = [
        send(gain_buf, recv_gz.at[me], s_gz, k - 1, "wt", lax.rem(me + k, n_wt))
        for k in range(1, n_wt)
    ]
    recv_gz[me] = gain_buf[...]
    arrived(zs)
    total = recv_gz[0]
    for pos in range(1, n_wt):
        total = total + recv_gz[pos]
    recv_gs[seq] = total
    mine = recv_gs.at[seq]
    ss = [
        send(mine, mine, s_gs, k - 1, "seq", lax.rem(seq + k, n_seq)) for k in range(1, n_seq)
    ]
    arrived(ss)
    total = recv_gs[0]
    for pos in range(1, n_seq):
        total = total + recv_gs[pos]
    gains_out[...] = jnp.sum(total, axis=1, keepdims=True)
    arrived(second)
    for group in (first, second, smalls, chans, zs, ss):
        left(group)


def last(part, tok_own, d_res, gain, rows_small, by_chan, gain_grad2, n_wt, n_seq, ident):
    rows, cols = part.shape
    own = rows // n_wt
    return pl.pallas_call(
        last_kernel,
        out_shape=[
            jax.ShapeDtypeStruct((rows, cols), BF16),
            jax.ShapeDtypeStruct(rows_small.shape[1:], F32),
            jax.ShapeDtypeStruct(by_chan.shape, F32),
            jax.ShapeDtypeStruct((2, 1, cols), F32),
        ],
        in_specs=[VMEM] * 7,
        out_specs=[VMEM] * 4,
        scratch_shapes=[
            pltpu.VMEM((n_wt - 1, own, cols), BF16),
            pltpu.VMEM((n_seq - 1,) + rows_small.shape[1:], F32),
            pltpu.VMEM((n_seq - 1,) + by_chan.shape, F32),
            pltpu.VMEM((2, 8, cols), F32),
            pltpu.VMEM((n_wt, 2, 8, cols), F32),
            pltpu.VMEM((n_seq, 2, 8, cols), F32),
            pair_sems(n_wt),
            pair_sems(n_wt),
            pair_sems(n_seq),
            pair_sems(n_seq),
            pair_sems(n_wt),
            pair_sems(n_seq),
        ],
        compiler_params=pltpu.CompilerParams(
            collective_id=ident, has_side_effects=True, vmem_limit_bytes=40 * MIB
        ),
        cost_estimate=pl.CostEstimate(flops=10**6, bytes_accessed=10**8, transcendentals=0),
    )(part, tok_own, d_res, gain[None], rows_small, by_chan, gain_grad2)


def load(ref):
    return tuple(ref[n] for n in range(NS))


def store(ref, values):
    for n in range(NS):
        ref[n] = values[n]


def fold(mine, box, recv, a2, carried, backward):
    n, me = lax.axis_size("seq"), lax.axis_index("seq")
    carried[...] = jnp.zeros_like(carried)
    for k in range(n - 1, 0, -1):

        @pl.when((me + k < n) if backward else (me >= k))
        def _():
            giver = me + k if backward else me - k
            remote(mine, recv.at[k - 1], box, k - 1, "seq", giver).wait_recv()
            through = recv[k - 1, NS]
            for s in range(NS):
                carried[s] = (
                    jnp.exp2(a2[s] * through) * carried[s] + recv[k - 1, s]
                )


def hand_on(mine, recv, box, backward):
    n, me = lax.axis_size("seq"), lax.axis_index("seq")
    for k in range(1, n):

        @pl.when((me >= k) if backward else (me + k < n))
        def _():
            peer = me - k if backward else me + k
            send(mine, recv.at[k - 1], box, k - 1, "seq", peer)


def handed(mine, recv, box, backward):
    n, me = lax.axis_size("seq"), lax.axis_index("seq")
    for k in range(1, n):

        @pl.when((me >= k) if backward else (me + k < n))
        def _():
            peer = me - k if backward else me + k
            remote(mine, recv.at[k - 1], box, k - 1, "seq", peer).wait_send()


def fwd_kernel(sa, dx, w, r, a2, y, h0, mine, recv, box):
    tok = sa.shape[0]
    greet(("seq",))

    def end(t, carry):
        s, d = sa[t], dx[t]
        h, total = carry
        return (
            tuple(jnp.exp2(s * a2[n]) * h[n] + w[t, n] * d for n in range(NS)),
            total + s,
        )

    zero = jnp.zeros(sa.shape[1:], F32)
    ends, total = lax.fori_loop(0, tok, end, ((zero,) * NS, zero), unroll=4)
    store(mine, ends)
    mine[NS] = total
    hand_on(mine, recv, box, False)
    fold(mine, box, recv, a2, h0, False)

    def body(t, h):
        s, d = sa[t], dx[t]
        new, sums = [], [None] * 4
        for n in range(NS):
            hn = jnp.exp2(s * a2[n]) * h[n] + w[t, n] * d
            new.append(hn)
            c = r[t, n] * hn
            sums[n % 4] = c if sums[n % 4] is None else sums[n % 4] + c
        y[t] = (sums[0] + sums[1]) + (sums[2] + sums[3])
        return tuple(new)

    lax.fori_loop(0, tok, body, load(h0), unroll=4)
    handed(mine, recv, box, False)


def fwd_scan(sa, dx, w, r, a2, n_seq, ident):
    tok, high = sa.shape[:2]
    return pl.pallas_call(
        fwd_kernel,
        out_shape=[
            jax.ShapeDtypeStruct((tok, high, 128), F32),
            jax.ShapeDtypeStruct((NS, high, 128), F32),
        ],
        in_specs=[VMEM, VMEM, SMEM, SMEM, VMEM],
        out_specs=[VMEM] * 2,
        scratch_shapes=[
            pltpu.VMEM((NS + 1, high, 128), F32),
            pltpu.VMEM((n_seq - 1, NS + 1, high, 128), F32),
            pair_sems(n_seq),
        ],
        compiler_params=pltpu.CompilerParams(
            collective_id=ident, has_side_effects=True, vmem_limit_bytes=32 * MIB
        ),
        cost_estimate=pl.CostEstimate(
            flops=10**8, bytes_accessed=8 * 10**7, transcendentals=2 * tok * NS * 1024
        ),
    )(sa, dx, w, r, a2)


def bwd_kernel(
    sa, dx, w, r, do, a2, h0, part, res,
    along, ds2, grad_a, pw, pr, out,
    hs, qw, qr, g0, mine, recv, recv_z, box, s_scatter, s_gather,
):
    tok = sa.shape[0]
    chunk = qw.shape[0] // (NS * 8)
    greet(("wt", "seq"))
    first = scatter_start(part, recv_z, s_scatter, "wt")

    def end(i, carry):
        t = tok - 1 - i
        s, d = sa[t], do[t]
        g, total = carry
        return (
            tuple(jnp.exp2(s * a2[n]) * (g[n] + r[t, n] * d) for n in range(NS)),
            total + s,
        )

    zero = jnp.zeros(sa.shape[1:], F32)
    ends, total = lax.fori_loop(0, tok, end, ((zero,) * NS, zero), unroll=4)
    store(mine, ends)
    mine[NS] = total
    hand_on(mine, recv, box, True)

    def again(t, h):
        s, d = sa[t], dx[t]
        new = []
        for n in range(NS):
            hs[t, n] = h[n]
            new.append(jnp.exp2(s * a2[n]) * h[n] + w[t, n] * d)
        return tuple(new)

    lax.fori_loop(0, tok, again, load(h0), unroll=2)

    arrived(first)
    me = lax.axis_index("wt")
    rows = recv_z.shape[1]
    row0 = me * rows

    def block_rows(at):
        total = res[pl.ds(at, 16)] + summed(part, recv_z, at, 16, row0)
        out[pl.ds(pl.multiple_of(row0 + at, 16), 16)] = total.astype(BF16)

    step_rows(rows, 16, block_rows)
    second = gather_start(out, rows, s_gather, "wt")

    fold(mine, box, recv, a2, g0, True)
    grad_a[...] = jnp.zeros_like(grad_a)

    def one_chunk(j, g):
        base = (tok // chunk - 1 - j) * chunk

        def body(i, g):
            at = chunk - 1 - i
            t = base + at
            s, d, o = sa[t], dx[t], do[t]
            al = d2 = None
            new = []
            for n in range(NS):
                hp = hs[t, n]
                f = jnp.exp2(s * a2[n])
                hn = f * hp + w[t, n] * d
                gn = r[t, n] * o + g[n]
                adj = f * gn
                new.append(adj)
                th = adj * hp
                grad_a[n] += th * s
                x = w[t, n] * gn
                al = x if al is None else al + x
                x = a2[n] * th
                d2 = x if d2 is None else d2 + x
                row = pl.multiple_of((at * NS + n) * 8, 8)
                qw[pl.ds(row, 8), :] = gn * d
                qr[pl.ds(row, 8), :] = hn * o
            along[t] = al
            ds2[t] = d2
            return tuple(new)

        g = lax.fori_loop(0, chunk, body, g)

        def lanes(i, carry):
            for q, p in ((qw, pw), (qr, pr)):
                acc = q[pl.ds(i * NS * 8, NS, stride=8), :]
                for s in range(1, 8):
                    acc = acc + q[pl.ds(i * NS * 8 + s, NS, stride=8), :]
                p[base + i] = acc
            return carry

        lax.fori_loop(0, chunk, lanes, 0, unroll=4)
        return g

    lax.fori_loop(0, tok // chunk, one_chunk, load(g0))
    handed(mine, recv, box, True)
    arrived(second)
    left(first)
    left(second)


def bwd_scan(sa, dx, w, r, do, a2, h0, part, res, n_wt, n_seq, ident):
    tok, high = sa.shape[:2]
    rows, cols = part.shape
    chunk = 32
    return pl.pallas_call(
        bwd_kernel,
        out_shape=[
            jax.ShapeDtypeStruct((tok, high, 128), F32),
            jax.ShapeDtypeStruct((tok, high, 128), F32),
            jax.ShapeDtypeStruct((NS, high, 128), F32),
            jax.ShapeDtypeStruct((tok, NS, 128), F32),
            jax.ShapeDtypeStruct((tok, NS, 128), F32),
            jax.ShapeDtypeStruct((rows, cols), BF16),
        ],
        in_specs=[VMEM, VMEM, SMEM, SMEM] + [VMEM] * 5,
        out_specs=[VMEM] * 6,
        scratch_shapes=[
            pltpu.VMEM((tok, NS, high, 128), F32),
            pltpu.VMEM((chunk * NS * 8, 128), F32),
            pltpu.VMEM((chunk * NS * 8, 128), F32),
            pltpu.VMEM((NS, high, 128), F32),
            pltpu.VMEM((NS + 1, high, 128), F32),
            pltpu.VMEM((n_seq - 1, NS + 1, high, 128), F32),
            pltpu.VMEM((n_wt - 1, rows // n_wt, cols), BF16),
            pair_sems(n_seq),
            pair_sems(n_wt),
            pair_sems(n_wt),
        ],
        compiler_params=pltpu.CompilerParams(
            collective_id=ident, has_side_effects=True, vmem_limit_bytes=56 * MIB
        ),
        cost_estimate=pl.CostEstimate(
            flops=10**8, bytes_accessed=15 * 10**7, transcendentals=3 * tok * NS * 1024
        ),
    )(sa, dx, w, r, do, a2, h0, part, res)


def gather(block):
    return lax.all_gather(block, "seq", axis=0, tiled=True)


def from_behind(block, axis, distance):
    devices = range(lax.axis_size(axis))
    route = [(i - distance, i) for i in devices if i - distance in devices]
    return lax.ppermute(block, axis, route)


def contract(left_op, right_op, pattern):
    return jnp.einsum(pattern, left_op, right_op, preferred_element_type=F32)


def silu_slope(values):
    sigma = jax.nn.sigmoid(values)
    return sigma * (1.0 + values * (1.0 - sigma))


def tiles(rows):
    return rows.reshape(rows.shape[0], rows.shape[1] // 128, 128)


def flat(rows):
    return rows.reshape(rows.shape[0], rows.shape[1] * rows.shape[2])


def local(
    tokens,
    cotangent,
    doc_start,
    premix_gain,
    inner_proj,
    switch_proj,
    conv_taps,
    conv_bias,
    select_proj,
    step_proj,
    step_bias,
    decay_log,
    skip_gain,
    mixer_out,
    preffn_gain,
    ffn_gate,
    ffn_up,
    ffn_down,
):
    tok_count, width = tokens.shape
    chan = inner_proj.shape[1]
    units = ffn_gate.shape[1]
    edge = KC - 1
    n_seq, n_wt = lax.axis_size("seq"), lax.axis_size("wt")
    z = lax.axis_index("wt")
    own = tok_count // n_wt
    gather_acts = n_seq * tok_count <= width

    w_mixer = gather(jnp.concatenate([inner_proj, switch_proj, mixer_out], axis=1))
    w_first, w_mix = w_mixer[:, : 2 * chan], w_mixer[:, 2 * chan :]
    w_small = lax.all_gather(jnp.concatenate([select_proj, step_proj], axis=0), "seq", axis=0)
    w_select = w_small[:, : select_proj.shape[0]].reshape(-1, chan)
    w_step = w_small[:, select_proj.shape[0] :].reshape(-1, chan)
    w_all = gather(jnp.concatenate([ffn_gate, ffn_up, ffn_down], axis=1))
    w_ffn, w_down = w_all[:, : 2 * units], w_all[:, 2 * units :]

    token_vals = tokens.astype(F32)
    first_inv = lax.rsqrt(jnp.mean(token_vals * token_vals, axis=-1, keepdims=True) + EPS)
    first_in = (token_vals * first_inv * premix_gain).astype(BF16)
    both = contract(first_in, w_first, "td,dc->tc")
    inner_act = both[:, :chan].astype(BF16)
    switch = both[:, chan:]

    counts = jnp.cumsum(doc_start)
    last_count = counts[-1]
    head_keep = (counts == 0).astype(F32)
    tail_keep = (counts == last_count).astype(F32)
    tail_rows = jnp.where(
        tail_keep[-edge:, None] > 0, inner_act[-edge:], jnp.zeros_like(inner_act[-edge:])
    )
    prev_rows = from_behind(tail_rows, "seq", 1)
    extended = jnp.concatenate([prev_rows, inner_act], axis=0).astype(F32)
    ext_counts = jnp.concatenate([jnp.zeros((edge,), jnp.int32), counts])
    conv_out = jnp.zeros((tok_count, chan), F32) + conv_bias[None, :]
    for offset in range(KC):
        same_doc = (counts == ext_counts[edge - offset : edge - offset + tok_count]).astype(F32)
        conv_out = (
            conv_out
            + conv_taps[offset][None, :]
            * extended[edge - offset : edge - offset + tok_count]
            * same_doc[:, None]
        )
    mixed_in = jax.nn.silu(conv_out).astype(BF16)
    mixed_f = mixed_in.astype(F32)
    select = wt_sum(contract(w_select, mixed_in, "jc,tc->jt"), n_wt, 0)
    low_rank = select[:R].astype(BF16)
    write_vec = select[R : R + NS].T
    read_vec = select[R + NS :].T
    step_pre = contract(low_rank, w_step, "rt,rc->tc") + step_bias[None, :]
    step_size = jax.nn.softplus(step_pre)
    decay = -jnp.exp(decay_log)
    decay2 = tiles(decay * LOG2E)
    step_a = tiles(jnp.where(doc_start[:, None] > 0, FAR, step_size))
    drive = tiles(step_size * mixed_f)
    scan_out, carried_in = fwd_scan(step_a, drive, write_vec, read_vec, decay2, n_seq, 1)

    scanned = flat(scan_out) + skip_gain[None, :] * mixed_f
    switch_act = jax.nn.silu(switch)
    gated = (scanned * switch_act).astype(BF16)
    mix_part = contract(gated, w_mix, "tc,dc->td").astype(BF16)
    tokens_own = lax.dynamic_slice_in_dim(tokens, z * own, own, 0).astype(F32)
    cot_own = lax.dynamic_slice_in_dim(cotangent, z * own, own, 0).astype(F32)
    second_in, residual = second_norm(mix_part, tokens_own, preffn_gain, n_wt, 2)
    gate_up = contract(second_in, w_ffn, "td,df->tf")
    gate_pre, up_pre = gate_up[:, :units], gate_up[:, units:]
    gate_act = jax.nn.silu(gate_pre)
    hidden = (gate_act * up_pre).astype(BF16)

    d_hidden = contract(cotangent, w_down, "td,df->tf")
    d_gate = (d_hidden * up_pre * silu_slope(gate_pre)).astype(BF16)
    d_up = (d_hidden * gate_act).astype(BF16)
    d_ffn = jnp.concatenate([d_gate, d_up], axis=1)
    d_second = contract(d_ffn, w_ffn, "tf,df->td").astype(BF16)
    d_branch, d_residual, grad_preffn = second_back(d_second, residual, cot_own, preffn_gain, n_wt, 3)
    down_part = contract(hidden, w_down, "tf,df->td").astype(BF16)
    d_gated = contract(d_branch, w_mix, "td,dc->tc")
    d_scanned = d_gated * switch_act
    d_switch = (d_gated * scanned * silu_slope(switch)).astype(BF16)
    grad_skip = jnp.sum(d_scanned * mixed_f, axis=0)
    along, through_sum, grad_decay, write_lanes, read_lanes, block_out = bwd_scan(
        step_a, drive, write_vec, read_vec, tiles(d_scanned), decay2, carried_in,
        down_part, residual, n_wt, n_seq, 4,
    )
    along = flat(along)
    d_step = along * mixed_f + flat(through_sum) * (1.0 / LOG2E)
    grad_decay_log = flat(grad_decay) * decay
    d_pre = d_step * jax.nn.sigmoid(step_pre)
    grad_step_bias = jnp.sum(d_pre, axis=0)
    d_pre_low = d_pre.astype(BF16)
    grad_step = contract(low_rank, d_pre_low, "rt,tc->rc")
    d_select = wt_sum(
        jnp.concatenate(
            [
                contract(w_step, d_pre_low, "rc,tc->rt"),
                jnp.sum(write_lanes, axis=-1).T,
                jnp.sum(read_lanes, axis=-1).T,
            ],
            axis=0,
        ),
        n_wt,
        5,
    ).astype(BF16)
    grad_select = contract(d_select, mixed_in, "jt,tc->jc")
    d_mixed = (
        along * step_size
        + skip_gain[None, :] * d_scanned
        + contract(d_select, w_select, "jt,jc->tc")
    )
    d_conv = (d_mixed * silu_slope(conv_out)).astype(BF16)
    d_conv_f = d_conv.astype(F32)
    grad_conv_bias = jnp.sum(d_conv_f, axis=0)
    head_rows = jnp.where(head_keep[:edge, None] > 0, d_conv[:edge], jnp.zeros_like(d_conv[:edge]))
    next_rows = from_behind(head_rows, "seq", -1)
    ext_grad = jnp.concatenate([d_conv, next_rows], axis=0).astype(F32)
    ext_after = jnp.concatenate([counts, jnp.zeros((edge,), jnp.int32) + last_count])
    d_inner = jnp.zeros_like(d_conv_f)
    taps_rows = []
    for offset in range(KC):
        same_doc = (counts == ext_counts[edge - offset : edge - offset + tok_count]).astype(F32)
        taps_rows.append(
            jnp.sum(
                d_conv_f * extended[edge - offset : edge - offset + tok_count] * same_doc[:, None],
                axis=0,
            )
        )
        later_same = (ext_after[offset : offset + tok_count] == counts).astype(F32)
        d_inner = (
            d_inner
            + conv_taps[offset][None, :]
            * ext_grad[offset : offset + tok_count]
            * later_same[:, None]
        )
    d_inner_low = d_inner.astype(BF16)
    d_first = contract(
        jnp.concatenate([d_inner_low, d_switch], axis=1), w_first, "tc,dc->td"
    ).astype(BF16)
    small = jnp.concatenate(
        [grad_select.reshape(n_seq, -1, chan), grad_step.reshape(n_seq, -1, chan)], axis=1
    )
    by_chan = jnp.concatenate(
        [
            jnp.stack(taps_rows, axis=0),
            grad_decay_log,
            grad_conv_bias[None],
            grad_step_bias[None],
            grad_skip[None],
            jnp.zeros((1, chan), F32),
        ],
        axis=0,
    )
    tokens_grad, small, by_chan, gains = last(
        d_first, tokens_own, d_residual, premix_gain, small, by_chan, grad_preffn, n_wt, n_seq, 6
    )

    if gather_acts:
        ffn_all = gather(jnp.concatenate([hidden, d_ffn], axis=1))
        mix_all = gather(jnp.concatenate([gated, d_switch, d_inner_low], axis=1))
        blocks = lambda v: v.reshape(tok_count, n_seq, 1, width // n_seq)
        early = jnp.concatenate([blocks(cotangent), blocks(first_in)], axis=2)
        late = jnp.concatenate([blocks(second_in), blocks(d_branch)], axis=2)
        early = lax.all_to_all(early, "seq", 1, 0, tiled=True).reshape(n_seq * tok_count, -1)
        late = lax.all_to_all(late, "seq", 1, 0, tiled=True).reshape(n_seq * tok_count, -1)
        piece = width // n_seq
        cot_f, first_f = early[:, :piece], early[:, piece:]
        second_f, branch_f = late[:, :piece], late[:, piece:]
        out_down = contract(cot_f, ffn_all[:, :units], "td,tf->df")
        out_gate = contract(second_f, ffn_all[:, units : 2 * units], "td,tf->df")
        out_up = contract(second_f, ffn_all[:, 2 * units :], "td,tf->df")
        out_mix = contract(branch_f, mix_all[:, :chan], "td,tc->dc")
        out_switch = contract(first_f, mix_all[:, chan : 2 * chan], "td,tc->dc")
        out_inner = contract(first_f, mix_all[:, 2 * chan :], "td,tc->dc")
    else:
        scatter = lambda v: lax.psum_scatter(v, "seq", scatter_dimension=0, tiled=True)
        out_down = scatter(contract(cotangent, hidden, "td,tf->df"))
        out_gate = scatter(contract(second_in, d_gate, "td,tf->df"))
        out_up = scatter(contract(second_in, d_up, "td,tf->df"))
        out_mix = scatter(contract(d_branch, gated, "td,tc->dc"))
        out_switch = scatter(contract(first_in, d_switch, "td,tc->dc"))
        out_inner = scatter(contract(first_in, d_inner_low, "td,tc->dc"))
    rows_sel = select_proj.shape[0]
    return (
        block_out,
        tokens_grad,
        gains[0, 0],
        out_inner,
        out_switch,
        by_chan[:KC],
        by_chan[KC + NS],
        small[:rows_sel],
        small[rows_sel:],
        by_chan[KC + NS + 1],
        by_chan[KC : KC + NS],
        by_chan[KC + NS + 2],
        out_mix,
        gains[1, 0],
        out_gate,
        out_up,
        out_down,
    )


def solution(mesh):
    placed = (
        P("seq", None),
        P("seq", None),
        P("seq"),
        P(),
        P("seq", "wt"),
        P("seq", "wt"),
        P(None, "wt"),
        P("wt"),
        P("seq", "wt"),
        P("seq", "wt"),
        P("wt"),
        P(None, "wt"),
        P("wt"),
        P("seq", "wt"),
        P(),
        P("seq", "wt"),
        P("seq", "wt"),
        P("seq", "wt"),
    )
    return jax.shard_map(
        local,
        mesh=mesh,
        in_specs=placed,
        out_specs=(
            P("seq", None),
            P("seq", None),
            P(),
            P("seq", "wt"),
            P("seq", "wt"),
            P(None, "wt"),
            P("wt"),
            P("seq", "wt"),
            P("seq", "wt"),
            P("wt"),
            P(None, "wt"),
            P("wt"),
            P("seq", "wt"),
            P(),
            P("seq", "wt"),
            P("seq", "wt"),
            P("seq", "wt"),
        ),
        check_vma=False,
    )
```

time: 2330 us -> 740 us (0.32)
  waiting for transfers between devices: 1060 us -> 149 us
  Pallas kernels: 0 us -> 336 us
  loops' own time: 322 us -> 0 us
  other arithmetic: 346 us -> 30.4 us
  local copies, waits for them, and re-layouts: 299 us -> 27.5 us
  blocking collectives: 118 us -> 57.4 us
    reduce_scatter x7 -> x0, waiting for transfers between devices: 592 us -> none  [the longest x1 120 us: local(): lax.psum_scatter(summed_ffn[1], 'seq', scatter_dimension=0, tiled=True)]
    pallas_call x0 -> x7, Pallas kernels: none -> 336 us  [the longest x1 119 us: last(): pl.pallas_call(last_kernel, out_shape=[jax.ShapeDtypeStruct((rows, cols),...]
    another operation x4 -> x0, loops' own time: 322 us -> none  [the longest x1 163 us: local(): lax.scan(forward_step, carried_in, (step_size, mixed_f, write_vec, read_v...]
    psum x6 -> x0, waiting for transfers between devices: 279 us -> none  [the longest x1 83.3 us: local(): residual = token_vals + lax.psum(contract(gated, w_mix, 'tc,dc->td'), 'wt')]
    reduce_sum x214 -> x3, other arithmetic: 253 us -> 4.89 us  [the longest x1 2.31 us: local(): jnp.sum(write_lanes, axis=-1)]
    slice x116 -> x13, local copies, waits for them, and re-layouts: 111 us -> 4.97 us  [the longest x2 0.92 us: local(): read_vec = select[R + NS:].T]
    concatenate x80 -> x1, local copies, waits for them, and re-layouts: 51.9 us -> 0.23 us  [local(): jnp.concatenate([jnp.stack(taps_rows, axis=0), grad_decay_log, grad_conv_...]
    mul x64 -> x0, local copies, waits for them, and re-layouts: 51.2 us -> none  [the longest x16 17.1 us: backward_step(): along = jnp.sum(total_adj * write_t[:, None], axis=0)]
  transfers between devices with their start and end apart: 23 -> 7, of which waited for: 19 -> 4; matrix products, arithmetic and copies ran while one was open for 12% -> 10% of each run, Pallas kernels for 0% -> 28%
where the time goes in v1:
time: 740 us; the launch traced here: 732 us
  Pallas kernels  336 us (45%)
  waiting for transfers between devices  149 us (20%)
  matrix products  109 us (15%)
  blocking collectives  57.4 us (8%)
  other arithmetic  30.4 us (4%)
  local copies, waits for them, and re-layouts  27.5 us (4%)
  between operations  15.3 us (2%)
    all_gather x4, waiting for transfers between devices, gather(): return lax.all_gather(block, 'seq', axis=0, tiled=True)  147 us
    pallas_call x1, Pallas kernels, last(): pl.pallas_call(last_kernel, out_shape=[jax.ShapeDtypeStruct((rows, cols),...  119 us
    dot_general x20, matrix products, contract(): return jnp.einsum(pattern, left_op, right_op, preferred_element_type=F32)  109 us
    pallas_call x1, Pallas kernels, bwd_scan(): pl.pallas_call(bwd_kernel, out_shape=[jax.ShapeDtypeStruct((tok, high, 12...  62.5 us
    pallas_call x1, Pallas kernels, second_back(): pl.pallas_call(second_back_kernel, out_shape=[jax.ShapeDtypeStruct((rows,...  47 us
    pallas_call x1, Pallas kernels, second_norm(): pl.pallas_call(second_norm_kernel, out_shape=[jax.ShapeDtypeStruct((rows,...  45.4 us
    all_to_all x1, blocking collectives, local(): lax.all_to_all(early, 'seq', 1, 0, tiled=True)  43.9 us
    pallas_call x2, Pallas kernels, wt_sum(): pl.pallas_call(wt_sum_kernel, out_shape=jax.ShapeDtypeStruct((rows, cols)...  39.1 us
  transfers between devices with their start and end apart: 7, of which 4 were waited for; matrix products, arithmetic and copies ran while one was open for 10% of the time, Pallas kernels for 28%

profile of v1, /device:TPU:0, one launch (start us, length us, event | category | flops | bytes accessed | tf_op | source)
XLA Modules:
  0.0 732.0 jit_solution(6347006374969990056)
XLA Ops:
  7.3 2.8 pad_maximum_fusion.4
  10.1 1.8 pad_maximum_fusion
  14.6 1.3 compare_convert_fusion.2
  17.2 0.8 dynamic-slice_convert_fusion.1.tok
  18.1 1.8 dynamic-slice_convert_fusion.cot
  20.2 65.2 %all-gather.7.cloned.1.call-done = bf16[2048,3072]{1,0:T(8,128)(2,1)} async-done(((bf16[256,3072]{1,0:T(8,128)(2,1)}), bf16[2048,3072]{1,0:T(8,128)(2,1)}) %all-gather.7.cloned.1.call-update) | async-done | bytes 12582928 | tf_op jit(solution)/shard_map/all_gather | solution.py:569
  85.4 7.0 fusion.101
  92.5 2.2 collective-permute-start
  94.7 13.4 %all-gather.1 = bf16[8,36,1024]{2,1,0:T(8,128)(2,1)S(1)} all-gather(bf16[1,36,1024]{2,1,0:T(8,128)(2,1)S(1)} %maximum_bitcast_fusion), channel_id=2, replica_groups=mesh['seq'=8,'wt'=4] {'seq'}, dimensions={0}, use_global_device_ids=true | all-gather | bytes 663552 | tf_op jit(solution)/shard_map/all_gather | solution.py:626
  108.9 1.8 multiply_convert_fusion.5
  110.7 1.0 fusion.102.part
  111.8 14.7 %shard_map.305 = f32[160,256]{1,0:T(8,128)} custom-call(f32[160,256]{1,0:T(8,128)} %fusion.102.part), custom_call_target="tpu_custom_call" | custom-call | flops 100000 | bytes 1000000 | tf_op jit(solution)/shard_map/pallas_call | solution.py:116
  126.5 1.2 convolution_add_fusion.1
  127.8 0.7 fusion.52
  129.1 0.8 fusion.97
  130.2 22.7 %shard_map.306 = (f32[256,8,128]{2,1,0:T(8,128)S(1)}, f32[16,8,128]{2,1,0:T(8,128)S(1)}) custom-call(f32[256,8,128]{2,1,0:T(8,128)S(1)} %bitcast.101, f32[256,8,128]{2,1,0:T(8,128)S(1)} %bitcast.103, f32[256,16]{1,0:T(8,128)S(1)} %bitcast.107, f32[256,16]{1,0:T(8,128)S(1)} %bitcast.109, f32[16,8,128]{2,1,0:T(8,128)S(1)} %bitcast.111), custom_call_target="tpu_custom_call" | custom-call | flops 100000000 | bytes 80000000 | tf_op jit(solution)/shard_map/pallas_call | solution.py:410
  153.5 4.6 fusion.34.part
  158.1 45.4 %shard_map.307 = (bf16[256,2048]{1,0:T(8,128)(2,1)}, f32[64,2048]{1,0:T(8,128)}) custom-call(bf16[256,2048]{1,0:T(8,128)(2,1)} %fusion.34.part, f32[64,2048]{1,0:T(8,128)} %dynamic-slice_convert_fusion.1.tok, f32[1,2048]{1,0:T(1,128)} %bitcast.147), custom_call_target="tpu_custom_call" | custom-call | flops 1000000 | bytes 100000000 | tf_op jit(solution)/shard_map/pallas_call | solution.py:155
  203.6 10.9 %all-gather.9.cloned.1.call-done = bf16[2048,6144]{1,0:T(8,128)(2,1)} async-done(((bf16[256,6144]{1,0:T(8,128)(2,1)}), bf16[2048,6144]{1,0:T(8,128)(2,1)}) %all-gather.9.cloned.1.call-update) | async-done | bytes 25165840 | tf_op jit(solution)/shard_map/all_gather | solution.py:569
  214.5 14.8 %fusion.2 = f32[256,4096]{0,1:T(8,128)} fusion(bf16[256,2048]{1,0:T(8,128)(2,1)} %get-tuple-element.35, bf16[2048,6144]{1,0:T(8,128)(2,1)} %all-gather.9.cloned.1.call-done), kind=kOutput, calls=%fused_computation.2 | convolution fusion | flops 4294967296 | bytes 22020096 | tf_op jit(solution)/shard_map/td,df->tf/dot_general | solution.py:579
  229.3 9.2 %multiply_convert_fusion.2 = (bf16[256,2048]{0,1:T(8,128)(2,1)S(1)}, bf16[256,2048]{0,1:T(8,128)(2,1)}, bf16[256,2048]{0,1:T(8,128)(2,1)}) fusion(f32[256,4096]{0,1:T(8,128)} %fusion.2, bf16[256,2048]{1,0:T(8,128)(2,1)S(1)} %copy-done.30, bf16[2048,6144]{1,0:T(8,128)(2,1)} %all-gather.9.cloned.1.call-done), kind=kOutput, calls=%fused_computation.53 | convolution fusion | flops 2155347968 | bytes 16777216 | tf_op jit(solution)/shard_map/td,df->tf/dot_general | solution.py:579
  238.5 1.0 copy-done.40
  239.6 11.8 %fusion.31.part = bf16[256,2048]{1,0:T(8,128)(2,1)} fusion(bf16[2048,6144]{1,0:T(8,128)(2,1)} %all-gather.9.cloned.1.call-done, bf16[256,2048]{0,1:T(8,128)(2,1)} %get-tuple-element.65, bf16[256,2048]{0,1:T(8,128)(2,1)S(1)} %get-tuple-element.64), kind=kOutput, calls=%fused_computation.34 | convolution fusion | flops 4299685888 | bytes 19922944 | tf_op jit(solution)/shard_map/tf,df->td/dot_general | solution.py:579
  251.4 47.0 %shard_map.308 = (bf16[256,2048]{1,0:T(8,128)(2,1)}, f32[64,2048]{1,0:T(8,128)}, f32[8,2048]{1,0:T(8,128)}) custom-call(bf16[256,2048]{1,0:T(8,128)(2,1)} %fusion.31.part, f32[64,2048]{1,0:T(8,128)} %get-tuple-element.36.res, f32[64,2048]{1,0:T(8,128)} %dynamic-slice_convert_fusion.cot, f32[1,2048]{1,0:T(1,128)} %bitcast.148), custom_call_target="tpu_custom_call" | custom-call | flops 1000000 | bytes 100000000 | tf_op jit(solution)/shard_map/pallas_call | solution.py:208
  298.5 5.9 fusion.56
  304.4 1.0 copy-done.35
  305.5 1.2 copy.66
  306.6 6.7 fusion.40.part
  313.4 62.5 %shard_map.309 = (f32[256,8,128]{2,1,0:T(8,128)}, f32[256,8,128]{2,1,0:T(8,128)}, f32[16,8,128]{2,1,0:T(8,128)}, f32[256,16,128]{2,1,0:T(8,128)}, f32[256,16,128]{2,1,0:T(8,128)}, /*index=5*/bf16[256,2048]{1,0:T(8,128)(2,1)}) custom-call(f32[256,8,128]{2,1,0:T(8,128)} %bitcast.102, f32[256,8,128]{2,1,0:T(8,128)} %bitcast.104, f32[256,16]{1,0:T(8,128)} %bitcast.108, ...), custom_call_target="tpu_custom_call" | custom-call | flops 100000000 | bytes 150000000 | tf_op jit(solution)/shard_map/pallas_call | solution.py:535
  375.9 2.3 reduce_sum.92
  378.3 2.3 reduce_sum.91
  380.8 2.6 fusion.95
  383.7 0.7 pad_maximum_fusion.7.part
  384.4 24.3 %shard_map.310 = f32[160,256]{1,0:T(8,128)} custom-call(f32[160,256]{1,0:T(8,128)} %pad_maximum_fusion.7.part), custom_call_target="tpu_custom_call" | custom-call | flops 100000 | bytes 1000000 | tf_op jit(solution)/shard_map/pallas_call | solution.py:116
  408.8 4.5 fusion.63
  413.4 1.3 collective-permute-start.1
  414.7 1.8 collective-permute-done.1
  417.9 1.2 pad_maximum_fusion.5
  419.6 0.8 copy-done.42
  420.4 2.9 pad_maximum_fusion.1
  423.3 1.2 copy-done.21
  425.0 1.6 copy.53
  426.8 43.9 %all_to_all.30 = bf16[256,8,2,256]{0,3,2,1:T(8,128)(2,1)S(1)} all-to-all(bf16[256,8,2,256]{0,3,2,1:T(8,128)(2,1)S(1)} %pad_maximum_fusion.2), channel_id=1, replica_groups=mesh['seq'=8,'wt'=4] {'seq'}, dimensions={1} | all-to-all | bytes 4194304 | tf_op jit(solution)/shard_map/all_to_all | solution.py:776
  470.7 1.2 copy.55
  471.9 2.0 copy.70
  474.5 1.5 copy.61
  476.2 0.9 reshape.138
  477.2 1.5 pad_maximum_fusion.3
  478.8 3.7 all-to-all-start.1
  483.1 1.3 pad_maximum_fusion.6.rows_small
  484.4 6.2 fusion.37.part
  490.6 119.3 %shard_map.311 = (bf16[256,2048]{1,0:T(8,128)(2,1)S(1)}, f32[36,1024]{1,0:T(8,128)S(1)}, f32[24,1024]{1,0:T(8,128)S(1)}, f32[2,1,2048]{2,1,0:T(1,128)S(1)}) custom-call(bf16[256,2048]{1,0:T(8,128)(2,1)S(1)} %fusion.37.part, f32[64,2048]{1,0:T(8,128)S(1)} %copy-done, f32[64,2048]{1,0:T(8,128)S(1)} %copy-done.3, f32[1,2048]{1,0:T(1,128)S(1)} %bitcast.113, ...), custom_call_target="tpu_custom_call" | custom-call | flops 1000000 | bytes 100000000 | tf_op jit(solution)/shard_map/pallas_call | solution.py:298
  609.9 0.6 slice.238
  613.7 1.2 copy.58
  614.8 2.0 copy.71
  616.9 4.4 fusion.22
  621.3 4.6 fusion.20
  625.8 4.8 fusion.18
  630.6 70.7 %all-gather.13.cloned.1.call-done = bf16[2048,6144]{0,1:T(8,128)(2,1)} async-done(((bf16[256,6144]{0,1:T(8,128)(2,1)}), bf16[2048,6144]{0,1:T(8,128)(2,1)}) %all-gather.13.cloned.1.call-update) | async-done | bytes 25165840 | tf_op jit(solution)/shard_map/all_gather | solution.py:569
  701.3 7.5 %fusion.8 = f32[256,2048]{1,0:T(8,128)} fusion(bf16[2048,6144]{0,1:T(8,128)(2,1)} %all-gather.13.cloned.1.call-done, bf16[2048,512]{0,1:T(8,128)(2,1)} %bitcast.129), kind=kOutput, calls=%fused_computation.8 | convolution fusion | flops 2147483648 | bytes 11534336 | tf_op jit(solution)/shard_map/td,tf->df/dot_general | solution.py:579
  708.8 7.1 fusion.6
  715.9 7.2 fusion.4
  723.1 1.0 copy.85
  724.0 1.0 copy.86
  (208 shorter events, 14.1 us)
Async XLA Ops:
  7.2 2.9 copy-start.37
  7.2 2.9 copy-start.38
  7.2 2.9 copy-start.39
  7.2 78.2 %all-gather.7.cloned.1.call-start = ((), (), s32[]{:S(2)}) async-start(), calls=%async_computation.2 | async-start | bytes 14155776 | tf_op jit(solution)/shard_map/all_gather | solution.py:569
  10.1 204.4 %all-gather.9.cloned.1.call-start = ((), (), s32[]{:S(2)}) async-start(), calls=%async_computation.3 | async-start | bytes 28311552 | tf_op jit(solution)/shard_map/all_gather | solution.py:569
  11.9 4.6 copy-start.57
  11.9 4.6 copy-start.47
  12.0 7.9 %copy-start.8 = (f32[2048]{0:T(1024)S(1)}, f32[2048]{0:T(1024)}, u32[]{:S(2)}) copy-start(f32[2048]{0:T(1024)} %param.21) | copy-start | bytes 24580
  12.0 604.9 %all-gather.11.cloned.1.call-start = ((), (), s32[]{:S(2)}) async-start(), calls=%async_computation.4 | async-start | bytes 14155776 | tf_op jit(solution)/shard_map/all_gather | solution.py:569
  15.9 92.6 %copy-start.65 = (f32[256]{0:T(256)}, f32[256]{0:T(256)S(1)}, u32[]{:S(2)}) copy-start(f32[256]{0:T(256)S(1)} %get-tuple-element.83) | copy-start | bytes 3076
  15.9 92.6 %copy-start.66 = (f32[256]{0:T(256)}, f32[256]{0:T(256)S(1)}, u32[]{:S(2)}) copy-start(f32[256]{0:T(256)S(1)} %get-tuple-element.84) | copy-start | bytes 3076
  15.9 92.6 %copy-start.67 = (f32[256]{0:T(256)}, f32[256]{0:T(256)S(1)}, u32[]{:S(2)}) copy-start(f32[256]{0:T(256)S(1)} %get-tuple-element.85) | copy-start | bytes 3076
  16.6 92.0 %copy-start.51 = (f32[1,1024]{1,0:T(1,128)}, f32[1,1024]{1,0:T(1,128)S(1)}, u32[]{:S(2)}) copy-start(f32[1,1024]{1,0:T(1,128)S(1)} %get-tuple-element.79) | copy-start | bytes 12292
  16.6 92.0 %copy-start.53 = (f32[1,1024]{1,0:T(1,128)}, f32[1,1024]{1,0:T(1,128)S(1)}, u32[]{:S(2)}) copy-start(f32[1,1024]{1,0:T(1,128)S(1)} %get-tuple-element.80) | copy-start | bytes 12292
  20.2 72.2 %copy-start.20 = (bf16[256,2048]{1,0:T(8,128)(2,1)}, bf16[256,2048]{1,0:T(8,128)(2,1)S(1)}, u32[]{:S(2)}) copy-start(bf16[256,2048]{1,0:T(8,128)(2,1)S(1)} %fusion.45) | copy-start | bytes 3145732
  92.5 15.9 %collective-permute-start = (bf16[3,1024]{1,0:T(4,128)(2,1)S(1)}, bf16[3,1024]{1,0:T(4,128)(2,1)S(1)}, u32[]{:S(2)}, u32[]{:S(2)}) collective-permute-start(bf16[3,1024]{1,0:T(4,128)(2,1)S(1)} %slice_select_fusion.1), channel_id=1, source_target_pairs={{0,4},{4,8},{8,12},{12,16},{16,20},{20,24},{24,28},{1,5},{5,9},{9,... | collective-permute-start | bytes 18440 | tf_op jit(solution)/shard_map/ppermute | solution.py:575
  108.2 18.3 %copy-start.22 = (bf16[8,16,1024]{2,1,0:T(8,128)(2,1)}, bf16[8,16,1024]{2,1,0:T(8,128)(2,1)S(1)}, u32[]{:S(2)}) copy-start(bf16[8,16,1024]{2,1,0:T(8,128)(2,1)S(1)} %slice.260) | copy-start | bytes 786436
  108.9 2.8 copy-start.48
  108.9 17.6 %copy-start.59 = (f32[1024]{0:T(1024)S(1)}, f32[1024]{0:T(1024)}, u32[]{:S(2)}) copy-start(f32[1024]{0:T(1024)} %param.28) | copy-start | bytes 12292
  110.7 17.7 %copy-start.12 = (bf16[256,1024]{1,0:T(8,128)(2,1)}, bf16[256,1024]{1,0:T(8,128)(2,1)S(1)}, u32[]{:S(2)}) copy-start(bf16[256,1024]{1,0:T(8,128)(2,1)S(1)} %get-tuple-element.62) | copy-start | bytes 1572868
  110.7 17.0 %copy-start.76 = (pred[256]{0:T(512)(128)(4,1)S(1)}, pred[256]{0:T(512)(128)(4,1)}, u32[]{:S(2)}) copy-start(pred[256]{0:T(512)(128)(4,1)} %broadcast_compare_fusion.2) | copy-start | bytes 772
  111.7 18.4 %copy-start.7 = (f32[2,8,8,128]{3,2,1,0:T(8,128)}, f32[2,8,8,128]{3,2,1,0:T(8,128)S(1)}, u32[]{:S(2)}) copy-start(f32[2,8,8,128]{3,2,1,0:T(8,128)S(1)} %copy.64) | copy-start | bytes 196612
  128.9 24.0 %copy-start.1 = (f32[32,8,8,128]{3,2,1,0:T(8,128)}, f32[32,8,8,128]{3,2,1,0:T(8,128)S(1)}, u32[]{:S(2)}) copy-start(f32[32,8,8,128]{3,2,1,0:T(8,128)S(1)} %copy.62) | copy-start | bytes 3145732
  129.1 23.8 %copy-start.2 = (f32[32,8,8,128]{3,2,1,0:T(8,128)}, f32[32,8,8,128]{3,2,1,0:T(8,128)S(1)}, u32[]{:S(2)}) copy-start(f32[32,8,8,128]{3,2,1,0:T(8,128)S(1)} %copy.63) | copy-start | bytes 3145732
  130.1 22.9 %copy-start.4 = (f32[16,256]{0,1:T(8,128)}, f32[16,256]{0,1:T(8,128)S(1)}, u32[]{:S(2)}) copy-start(f32[16,256]{0,1:T(8,128)S(1)} %copy.47) | copy-start | bytes 49156
  130.2 22.8 %copy-start.5 = (f32[16,256]{0,1:T(8,128)}, f32[16,256]{0,1:T(8,128)S(1)}, u32[]{:S(2)}) copy-start(f32[16,256]{0,1:T(8,128)S(1)} %copy.48) | copy-start | bytes 49156
  130.2 22.8 %copy-start.13 = (bf16[256,1024]{1,0:T(8,128)(2,1)S(1)}, bf16[256,1024]{1,0:T(8,128)(2,1)}, u32[]{:S(2)}) copy-start(bf16[256,1024]{1,0:T(8,128)(2,1)} %copy-done.12) | copy-start | bytes 1572868
  130.2 22.8 %copy-start.45 = (f32[256,2048]{1,0:T(8,128)S(1)}, f32[256,2048]{1,0:T(8,128)}, u32[]{:S(2)}) copy-start(f32[256,2048]{1,0:T(8,128)} %get-tuple-element.89) | copy-start | bytes 6291460
  130.2 22.8 %copy-start.60 = (f32[1024]{0:T(1024)S(1)}, f32[1024]{0:T(1024)}, u32[]{:S(2)}) copy-start(f32[1024]{0:T(1024)} %param.30) | copy-start | bytes 12292
  153.0 5.2 copy-start.9
  153.5 4.7 copy-start.28
  214.5 14.8 %copy-start.30 = (bf16[256,2048]{1,0:T(8,128)(2,1)S(1)}, bf16[256,2048]{1,0:T(8,128)(2,1)}, u32[]{:S(2)}) copy-start(bf16[256,2048]{1,0:T(8,128)(2,1)} %param.19) | copy-start | bytes 3145732
  251.4 47.1 %copy-start.14 = (bf16[256,1024]{1,0:T(8,128)(2,1)S(1)}, bf16[256,1024]{1,0:T(8,128)(2,1)}, u32[]{:S(2)}) copy-start(bf16[256,1024]{1,0:T(8,128)(2,1)} %copy-done.12) | copy-start | bytes 1572868
  251.4 47.1 %copy-start.61 = (f32[1024]{0:T(1024)S(1)}, f32[1024]{0:T(1024)}, u32[]{:S(2)}) copy-start(f32[1024]{0:T(1024)} %param.30) | copy-start | bytes 12292
  375.9 4.8 copy-start.36
  378.3 2.5 copy-start.16
  380.8 2.7 copy-start.23
  380.8 3.6 copy-start.75
  380.8 28.0 %copy-start.11 = (f32[259,1024]{1,0:T(8,128)S(1)}, f32[259,1024]{1,0:T(8,128)}, u32[]{:S(2)}) copy-start(f32[259,1024]{1,0:T(8,128)} %copy-done.10) | copy-start | bytes 3182596
  383.4 29.9 %copy-start.18 = (bf16[256,1024]{1,0:T(8,128)(2,1)}, bf16[256,1024]{1,0:T(8,128)(2,1)S(1)}, u32[]{:S(2)}) copy-start(bf16[256,1024]{1,0:T(8,128)(2,1)S(1)} %get-tuple-element.59) | copy-start | bytes 1572868
  408.8 7.8 %copy-start.52 = (f32[1,1024]{1,0:T(1,128)S(1)}, f32[1,1024]{1,0:T(1,128)}, u32[]{:S(2)}) copy-start(f32[1,1024]{1,0:T(1,128)} %copy-done.51) | copy-start | bytes 12292
  408.8 7.8 %copy-start.54 = (f32[1,1024]{1,0:T(1,128)S(1)}, f32[1,1024]{1,0:T(1,128)}, u32[]{:S(2)}) copy-start(f32[1,1024]{1,0:T(1,128)} %copy-done.53) | copy-start | bytes 12292
  408.8 7.8 %copy-start.62 = (f32[256]{0:T(256)S(1)}, f32[256]{0:T(256)}, u32[]{:S(2)}) copy-start(f32[256]{0:T(256)} %get-tuple-element.81) | copy-start | bytes 3076
  408.8 7.8 %copy-start.63 = (f32[256]{0:T(256)S(1)}, f32[256]{0:T(256)}, u32[]{:S(2)}) copy-start(f32[256]{0:T(256)} %get-tuple-element.82) | copy-start | bytes 3076
  408.8 7.8 %copy-start.64 = (f32[256]{0:T(256)S(1)}, f32[256]{0:T(256)}, u32[]{:S(2)}) copy-start(f32[256]{0:T(256)} %get-tuple-element.86) | copy-start | bytes 3076
  413.4 3.1 collective-permute-start.1
  419.1 282.2 %all-gather.13.cloned.1.call-start = ((), (), s32[]{:S(2)}) async-start(), calls=%async_computation.5 | async-start | bytes 28311552 | tf_op jit(solution)/shard_map/all_gather | solution.py:569
  478.7 3.8 copy-start.49
  478.7 3.9 copy-start.56
  478.7 3.9 copy-start.68
  478.7 3.9 copy-start.69
  478.7 3.9 copy-start.70
  478.7 3.9 copy-start.71
  478.7 3.9 copy-start.72
  478.7 3.9 copy-start.73
  478.7 4.1 copy-start.19
  478.7 4.1 copy-start.32
  478.8 134.9 %all-to-all-start.1 = ((bf16[256,8,2,256]{0,3,2,1:T(8,128)(2,1)}), bf16[256,8,2,256]{0,3,2,1:T(8,128)(2,1)S(1)}, u32[]{:S(2)}, u32[]{:S(2)}) async-start(bf16[256,8,2,256]{0,3,2,1:T(8,128)(2,1)} %pad_maximum_fusion.3), calls=%async_computation.1 | async-start | bytes 4194304 | tf_op jit(solution)/shard_map/all_to_all | solution.py:777
  484.4 6.2 copy-start
  484.4 6.2 copy-start.3
  484.4 6.2 copy-start.6
  621.3 4.6 copy-start.25
  701.3 7.5 %copy-start.26 = (bf16[64,8,8,256]{3,1,2,0:T(8,128)(2,1)S(1)}, bf16[64,8,8,256]{3,1,2,0:T(8,128)(2,1)}, u32[]{:S(2)}) copy-start(bf16[64,8,8,256]{3,1,2,0:T(8,128)(2,1)} %copy.71) | copy-start | bytes 6291460
  715.9 7.2 copy-start.33
  (20 other events, 32.8 us)
Sparse Core Ops, SparseCore 0:
  10.5 74.8 all-gather.6
  87.3 127.1 all-gather.8
  419.3 139.6 all-gather.10
  560.7 140.5 all-gather.12

commit v2 on v1

--- a/solution.py
+++ b/solution.py
@@ -18,6 +18,7 @@
 MESH = pl.DeviceIdType.MESH
 VMEM = pl.BlockSpec(memory_space=pltpu.VMEM)
 SMEM = pl.BlockSpec(memory_space=pltpu.SMEM)
+ANY = pl.BlockSpec(memory_space=pl.ANY)
 MIB = 2**20
 
 
@@ -98,34 +99,303 @@
     lax.fori_loop(0, rows // step, run, 0)
 
 
-def wt_sum_kernel(part, out, recv, s_scatter, s_gather):
+def flips():
+    seq = lax.axis_index("seq")
+    core, x, y = lax.rem(seq, 2), lax.rem(seq // 2, 2), seq // 4
+
+    def at(fy, fx, fc):
+        return (
+            (1 - y if fy else y) * 4 + (1 - x if fx else x) * 2 + (1 - core if fc else core)
+        )
+
+    return at
+
+
+def cube_sems():
+    return pltpu.SemaphoreType.DMA((2, 9))
+
+
+def cube_first(block, whole, sems):
+    at = flips()
+    mine = whole.at[at(0, 0, 0)]
+    return [
+        send(block, mine, sems, 0, "seq", at(0, 1, 0)),
+        send(block, mine, sems, 1, "seq", at(1, 0, 0)),
+        send(block, mine, sems, 2, "seq", at(0, 0, 1)),
+    ]
+
+
+def keep(block, whole, sem):
+    copy = pltpu.make_async_copy(block, whole.at[lax.axis_index("seq")], sem)
+    copy.start()
+    return copy
+
+
+def spread(src, dst, sems, own_sem):
+    seq, n_seq = lax.axis_index("seq"), lax.axis_size("seq")
+    piece = dst.shape[2]
+
+    def columns(peer):
+        return src.at[:, pl.ds(pl.multiple_of(peer * piece, piece), piece)]
+
+    out = []
+    for k in range(1, n_seq):
+        peer = lax.rem(seq + k, n_seq)
+        out.append(send(columns(peer), dst.at[seq], sems, k - 1, "seq", peer))
+    return out, keep(columns(seq), dst, own_sem)
+
+
+def cube_second(whole, sems, first):
+    at = flips()
+    half = whole.shape[1] // 2
+    first[0].wait_recv()
+    block = whole.at[at(0, 1, 0)]
+    top = block.at[pl.ds(0, half)]
+    sent = [
+        send(top, top, sems, 3, "seq", at(1, 0, 0)),
+        send(block, block, sems, 5, "seq", at(0, 0, 1)),
+    ]
+    first[1].wait_recv()
+    block = whole.at[at(1, 0, 0)]
+    low = block.at[pl.ds(half, half)]
+    sent += [
+        send(low, low, sems, 4, "seq", at(0, 1, 0)),
+        send(block, block, sems, 6, "seq", at(0, 0, 1)),
+    ]
+    return sent
+
+
+def cube_third(whole, sems, second):
+    at = flips()
+    half = whole.shape[1] // 2
+    block = whole.at[at(1, 1, 0)]
+    sent = []
+    for slot, came in ((0, second[0]), (1, second[2])):
+        came.wait_recv()
+        piece = block.at[pl.ds(slot * half, half)]
+        sent.append(send(piece, piece, sems, 7 + slot, "seq", at(0, 0, 1)))
+    return sent
+
+
+def cube_end(first, second, third):
+    first[2].wait_recv()
+    second[1].wait_recv()
+    second[3].wait_recv()
+    arrived(third)
+    for group in (first, second, third):
+        left(group)
+
+
+def first_kernel(
+    mixer, small, cot, act, w_mixer, w_small, cot_f, act_f,
+    s_big, s_small, s_own, s_cot, s_act, s_cz, s_az,
+):
+    seq, n_seq = lax.axis_index("seq"), lax.axis_size("seq")
+    z, n_wt = lax.axis_index("wt"), lax.axis_size("wt")
+    own, piece = cot_f.shape[2:]
+    kept = [keep(mixer, w_mixer, s_own.at[0]), keep(small, w_small, s_own.at[1])]
+    greet(("seq", "wt"))
+    little = cube_first(small, w_small, s_small)
+    sent, mine = [], []
+    for i, (src, dst, sems) in enumerate(((cot, cot_f, s_cot), (act, act_f, s_act))):
+        rows = src.at[pl.ds(pl.multiple_of(z * own, own), own)]
+
+        def columns(peer, rows=rows):
+            return rows.at[:, pl.ds(pl.multiple_of(peer * piece, piece), piece)]
+
+        for k in range(1, n_seq):
+            peer = lax.rem(seq + k, n_seq)
+            sent.append(send(columns(peer), dst.at[seq, z], sems, k - 1, "seq", peer))
+        mine.append(pltpu.make_async_copy(columns(seq), dst.at[seq, z], s_own.at[2 + i]))
+        mine[-1].start()
+    big = cube_first(mixer, w_mixer, s_big)
+    arrived(sent)
+    for copy in mine:
+        copy.wait()
+    along = []
+    for dst, sems in ((cot_f, s_cz), (act_f, s_az)):
+        lines = dst.at[:, z]
+        along += [
+            send(lines, lines, sems, k - 1, "wt", lax.rem(z + k, n_wt)) for k in range(1, n_wt)
+        ]
+    little2 = cube_second(w_small, s_small, little)
+    little3 = cube_third(w_small, s_small, little2)
+    big2 = cube_second(w_mixer, s_big, big)
+    big3 = cube_third(w_mixer, s_big, big2)
+    cube_end(little, little2, little3)
+    cube_end(big, big2, big3)
+    arrived(along)
+    left(along)
+    left(sent)
+    for copy in kept:
+        copy.wait()
+
+
+def first_gather(mixer, small, cot, act, n_wt, n_seq, ident):
+    tok, width = cot.shape
+    far = jax.ShapeDtypeStruct((n_seq, n_wt, tok // n_wt, width // n_seq), BF16)
+    return pl.pallas_call(
+        first_kernel,
+        out_shape=[
+            jax.ShapeDtypeStruct((n_seq,) + mixer.shape, BF16),
+            jax.ShapeDtypeStruct((n_seq,) + small.shape, BF16),
+            far,
+            far,
+        ],
+        in_specs=[ANY, ANY, VMEM, VMEM],
+        out_specs=[ANY] * 4,
+        scratch_shapes=[
+            cube_sems(),
+            cube_sems(),
+            pltpu.SemaphoreType.DMA((4,)),
+            pair_sems(n_seq),
+            pair_sems(n_seq),
+            pair_sems(n_wt),
+            pair_sems(n_wt),
+        ],
+        compiler_params=pltpu.CompilerParams(collective_id=ident, has_side_effects=True),
+        cost_estimate=pl.CostEstimate(flops=10**6, bytes_accessed=10**8, transcendentals=0),
+    )(mixer, small, cot, act)
+
+
+UNITS = 256
+
+
+def nt(left_op, right_op):
+    return lax.dot_general(
+        left_op, right_op, (((1,), (1,)), ((), ())), preferred_element_type=F32
+    )
+
+
+def ffn_kernel(x, c, wg, wu, wd, acts, down, d_second, acc_down, acc_second):
+    step = pl.program_id(0)
+
+    @pl.when(step == 0)
+    def _():
+        acc_down[...] = jnp.zeros_like(acc_down)
+        acc_second[...] = jnp.zeros_like(acc_second)
+
+    gate = jnp.dot(x[...], wg[...], preferred_element_type=F32)
+    up = jnp.dot(x[...], wu[...], preferred_element_type=F32)
+    d_hidden = jnp.dot(c[...], wd[...], preferred_element_type=F32)
+    sigma = jax.nn.sigmoid(gate)
+    act = gate * sigma
+    hidden = (act * up).astype(BF16)
+    d_gate = (d_hidden * up * (sigma * (1.0 + gate * (1.0 - sigma)))).astype(BF16)
+    d_up = (d_hidden * act).astype(BF16)
+    acts[:, :UNITS] = hidden
+    acts[:, UNITS : 2 * UNITS] = d_gate
+    acts[:, 2 * UNITS :] = d_up
+    acc_down[...] += nt(hidden, wd[...])
+    acc_second[...] += nt(d_gate, wg[...]) + nt(d_up, wu[...])
+
+    @pl.when(step == pl.num_programs(0) - 1)
+    def _():
+        down[...] = acc_down[...].astype(BF16)
+        d_second[...] = acc_second[...].astype(BF16)
+
+
+def ffn(x, c, w_all):
+    tok, width = x.shape
+    units = w_all.shape[1] // 3
+    steps = units // UNITS
+    whole = pl.BlockSpec((tok, width), lambda i: (0, 0))
+    tile = lambda part: pl.BlockSpec((width, UNITS), lambda i: (0, part * steps + i))
+    return pl.pallas_call(
+        ffn_kernel,
+        grid=(steps,),
+        in_specs=[whole, whole, tile(0), tile(1), tile(2)],
+        out_specs=[pl.BlockSpec((tok, 3 * UNITS), lambda i: (0, i)), whole, whole],
+        out_shape=[
+            jax.ShapeDtypeStruct((tok, 3 * units), BF16),
+            jax.ShapeDtypeStruct((tok, width), BF16),
+            jax.ShapeDtypeStruct((tok, width), BF16),
+        ],
+        scratch_shapes=[pltpu.VMEM((tok, width), F32)] * 2,
+        compiler_params=pltpu.CompilerParams(vmem_limit_bytes=40 * MIB),
+        cost_estimate=pl.CostEstimate(
+            flops=12 * tok * width * units, bytes_accessed=6 * width * units, transcendentals=0
+        ),
+    )(x, c, w_all, w_all, w_all)
+
+
+def grads_kernel(lefts, *refs):
+    n, m = max(lefts) + 1, len(lefts)
+    for which, act, out in zip(lefts, refs[n : n + m], refs[n + m :]):
+        out[...] = jnp.dot(refs[which][...], act[...], preferred_element_type=F32)
+
+
+def grads(left_ops, lefts, acts):
+    rows, tok = left_ops[0].shape
+    cols = acts[0].shape[1]
+    n = len(acts)
+    return pl.pallas_call(
+        functools.partial(grads_kernel, lefts),
+        grid=(cols // UNITS,),
+        in_specs=[pl.BlockSpec((rows, tok), lambda i: (0, 0))] * len(left_ops)
+        + [pl.BlockSpec((tok, UNITS), lambda i: (0, i))] * n,
+        out_specs=[pl.BlockSpec((rows, UNITS), lambda i: (0, i))] * n,
+        out_shape=[jax.ShapeDtypeStruct((rows, cols), F32)] * n,
+        compiler_params=pltpu.CompilerParams(vmem_limit_bytes=60 * MIB),
+        cost_estimate=pl.CostEstimate(
+            flops=2 * n * tok * rows * cols, bytes_accessed=2 * n * tok * cols, transcendentals=0
+        ),
+    )(*left_ops, *acts)
+
+
+def wt_sum_kernel(n_cube, n_spread, part, *refs):
+    n = n_cube + n_spread
+    srcs, out, dsts, refs = refs[:n], refs[n], refs[n + 1 : 2 * n + 1], refs[2 * n + 1 :]
+    recv, s_scatter, s_gather = refs[:3]
     me = lax.axis_index("wt")
     rows = recv.shape[1]
-    greet(("wt",))
+    greet(("wt", "seq") if n else ("wt",))
     first = scatter_start(part, recv, s_scatter, "wt")
+    sems = refs[3:]
+    cubes, sent, kept = [], [], []
+    for i in range(n):
+        if i < n_cube:
+            cubes.append(cube_first(srcs[i], dsts[i], sems[2 * i]))
+            kept.append(keep(srcs[i], dsts[i], sems[2 * i + 1]))
+        else:
+            new, own = spread(srcs[i], dsts[i], sems[2 * i], sems[2 * i + 1])
+            sent += new
+            kept.append(own)
     arrived(first)
     out[pl.ds(me * rows, rows)] = summed(part, recv, 0, rows, me * rows)
     second = gather_start(out, rows, s_gather, "wt")
+    cubes2 = [cube_second(dsts[i], sems[2 * i], cubes[i]) for i in range(n_cube)]
+    cubes3 = [cube_third(dsts[i], sems[2 * i], cubes2[i]) for i in range(n_cube)]
+    for one, two, three in zip(cubes, cubes2, cubes3):
+        cube_end(one, two, three)
+    for copy in kept:
+        copy.wait()
     arrived(second)
+    arrived(sent)
     left(first)
     left(second)
-
-
-def wt_sum(part, n_wt, ident):
+    left(sent)
+
+
+def wt_sum(part, blocks, srcs, n_wt, n_seq, ident):
     rows, cols = part.shape
     return pl.pallas_call(
-        wt_sum_kernel,
-        out_shape=jax.ShapeDtypeStruct((rows, cols), F32),
-        in_specs=[VMEM],
-        out_specs=VMEM,
+        functools.partial(wt_sum_kernel, len(blocks), len(srcs)),
+        out_shape=[jax.ShapeDtypeStruct((rows, cols), F32)]
+        + [jax.ShapeDtypeStruct((n_seq,) + a.shape, BF16) for a in blocks]
+        + [jax.ShapeDtypeStruct((n_seq, a.shape[0], a.shape[1] // n_seq), BF16) for a in srcs],
+        in_specs=[VMEM] + [ANY] * len(blocks) + [VMEM] * len(srcs),
+        out_specs=[VMEM] + [ANY] * len(blocks + srcs),
         scratch_shapes=[
             pltpu.VMEM((n_wt - 1, rows // n_wt, cols), F32),
             pair_sems(n_wt),
             pair_sems(n_wt),
-        ],
+        ]
+        + [cube_sems(), pltpu.SemaphoreType.DMA] * len(blocks)
+        + [pair_sems(n_seq), pltpu.SemaphoreType.DMA] * len(srcs),
         compiler_params=pltpu.CompilerParams(collective_id=ident, has_side_effects=True),
         cost_estimate=pl.CostEstimate(flops=10**5, bytes_accessed=10**6, transcendentals=0),
-    )(part)
+    )(part, *blocks, *srcs)
 
 
 def second_norm_kernel(part, tok, gain, out, res, recv, s_scatter, s_gather):
@@ -224,106 +494,173 @@
     )(part, res, cot_own, gain[None])
 
 
-def last_kernel(
-    part, tok, d_res, gain, rows_small, by_chan, gain_grad2,
-    out, small_out, chan_out, gains_out,
-    recv, recv_small, recv_chan, gain_buf, recv_gz, recv_gs,
-    s_scatter, s_gather, s_small, s_chan, s_gz, s_gs,
-):
-    me = lax.axis_index("wt")
+def last_kernel(cube, part, tok, d_res, gain, gain_grad2, sel, stp, taps, decays, bias3, *refs):
+    blocks, refs = refs[:cube], refs[cube:]
+    if cube:
+        cot_t, second_t, acts, refs = refs[0], refs[1], refs[2], refs[3:]
+    out, sel_out, stp_out, chan_out, gains_out = refs[:5]
+    wholes, refs = refs[5 : 5 + cube], refs[5 + cube :]
+    if cube:
+        grad_outs, refs = refs[:3], refs[3:]
+        tile, s_tile, refs = refs[0], refs[1], refs[2:]
+        width = tile.shape[2]
+        tiles = acts.shape[1] // width
+
+        def fetch(j, slot):
+            columns = acts.at[:, pl.ds(pl.multiple_of(j * width, width), width)]
+            return pltpu.make_async_copy(columns, tile.at[slot], s_tile.at[slot])
+
+        def one_tile(j, carry):
+            slot = lax.rem(j, 2)
+
+            @pl.when(j + 1 < tiles)
+            def _():
+                fetch(j + 1, 1 - slot).start()
+
+            fetch(j, slot).wait()
+            columns = pl.ds(pl.multiple_of(j * UNITS, UNITS), UNITS)
+            for i, left_op in enumerate((cot_t, second_t, second_t)):
+                grad_outs[i][:, columns] = jnp.dot(
+                    left_op[...],
+                    tile[slot, :, i * UNITS : (i + 1) * UNITS],
+                    preferred_element_type=F32,
+                )
+            return carry
+
+        fetch(0, 0).start()
+    recv, recv_sel, recv_stp, recv_chan, pack, gain_buf, recv_gz, recv_gs = refs[:8]
+    s_scatter, s_gather, s_sel, s_stp, s_chan, s_cg, s_gz, s_gs = refs[8:16]
+    me, n_wt = lax.axis_index("wt"), lax.axis_size("wt")
     seq, n_seq = lax.axis_index("seq"), lax.axis_size("seq")
     rows = recv.shape[1]
     greet(("wt", "seq"))
     first = scatter_start(part, recv, s_scatter, "wt")
-    smalls, chans = [], []
-    for k in range(1, n_seq):
-        peer = lax.rem(seq + k, n_seq)
-        smalls.append(
-            send(rows_small.at[peer], recv_small.at[k - 1], s_small, k - 1, "seq", peer)
-        )
-        chans.append(send(by_chan, recv_chan.at[k - 1], s_chan, k - 1, "seq", peer))
-    gain_buf[1] = gain_grad2[...]
-    gain_buf[0] = jnp.zeros_like(gain_grad2)
+    share = -(-(KC + NS + 3) // n_seq)
+    lines = [(taps, i) for i in range(KC)] + [(decays, i) for i in range(NS)]
+    lines += [(bias3, i) for i in range(3)]
+    for at, (ref, i) in enumerate(lines):
+        pack[at // share, at % share : at % share + 1] = ref[i : i + 1]
+    smalls = []
+    for src, dst, sems in ((sel, recv_sel, s_sel), (stp, recv_stp, s_stp), (pack, recv_chan, s_chan)):
+        for k in range(1, n_seq):
+            peer = lax.rem(seq + k, n_seq)
+            smalls.append(send(src.at[peer], dst.at[k - 1], sems, k - 1, "seq", peer))
+    cubes = []
+    for i in range(cube):
+        s_cube, s_own = refs[16 + 2 * i : 18 + 2 * i]
+        cubes.append([cube_first(blocks[i], wholes[i], s_cube), s_cube, wholes[i]])
+        cubes[-1].append(keep(blocks[i], wholes[i], s_own))
+    if cube:
+        lax.fori_loop(0, tiles // 2, one_tile, 0)
     arrived(smalls)
-    total = rows_small[seq]
+    for src, recv_one, one_out in ((sel, recv_sel, sel_out), (stp, recv_stp, stp_out)):
+        total = src[seq].astype(F32)
+        for k in range(n_seq - 1):
+            total = total + recv_one[k].astype(F32)
+        one_out[...] = total
+    total = pack[seq]
     for k in range(n_seq - 1):
-        total = total + recv_small[k]
-    small_out[...] = total
-    arrived(chans)
-    total = jnp.zeros_like(chan_out)
-    for pos in range(n_seq):
-        slot = lax.rem(seq - pos + n_seq, n_seq)
-        other = recv_chan[jnp.maximum(slot - 1, 0)]
-        total = total + jnp.where(slot == 0, by_chan[...], other)
-    chan_out[...] = total
+        total = total + recv_chan[k]
+    chan_out[seq] = total
+    mine = chan_out.at[seq]
+    chans = [
+        send(mine, mine, s_cg, k - 1, "seq", lax.rem(seq + k, n_seq)) for k in range(1, n_seq)
+    ]
     arrived(first)
     row0 = me * rows
+    gain_buf[...] = jnp.zeros_like(gain_buf)
 
     def body(at):
         grad = summed(part, recv, at, 16, row0)
         back, prod = norm_back_rows(grad, tok[pl.ds(at, 16)], gain[...])
-        gain_buf[0] += prod[:8] + prod[8:]
+        gain_buf[...] += prod[:8] + prod[8:]
         out[pl.ds(pl.multiple_of(row0 + at, 16), 16)] = (d_res[pl.ds(at, 16)] + back).astype(BF16)
 
     step_rows(rows, 16, body)
     second = gather_start(out, rows, s_gather, "wt")
-    n_wt = lax.axis_size("wt")
-    zs = [
-        send(gain_buf, recv_gz.at[me], s_gz, k - 1, "wt", lax.rem(me + k, n_wt))
-        for k in range(1, n_wt)
-    ]
-    recv_gz[me] = gain_buf[...]
+    high = recv_gz.shape[1] // 2
+    for i, grad in enumerate((gain_buf, gain_grad2)):
+        line = jnp.sum(grad[...], axis=0, keepdims=True)
+        for t in range(high):
+            recv_gz[me, i * high + t : i * high + t + 1] = line[:, t * 128 : (t + 1) * 128]
+    mine_z = recv_gz.at[me]
+    zs = [send(mine_z, mine_z, s_gz, k - 1, "wt", lax.rem(me + k, n_wt)) for k in range(1, n_wt)]
+    cubes2 = [cube_second(whole, sems, one) for one, sems, whole, _ in cubes]
+    if cube:
+        lax.fori_loop(tiles // 2, tiles, one_tile, 0)
     arrived(zs)
     total = recv_gz[0]
     for pos in range(1, n_wt):
         total = total + recv_gz[pos]
     recv_gs[seq] = total
-    mine = recv_gs.at[seq]
+    mine_s = recv_gs.at[seq]
     ss = [
-        send(mine, mine, s_gs, k - 1, "seq", lax.rem(seq + k, n_seq)) for k in range(1, n_seq)
+        send(mine_s, mine_s, s_gs, k - 1, "seq", lax.rem(seq + k, n_seq)) for k in range(1, n_seq)
     ]
+    cubes3 = [cube_third(whole, sems, two) for (_, sems, whole, _), two in zip(cubes, cubes2)]
     arrived(ss)
     total = recv_gs[0]
     for pos in range(1, n_seq):
         total = total + recv_gs[pos]
-    gains_out[...] = jnp.sum(total, axis=1, keepdims=True)
+    gains_out[...] = total
+    arrived(chans)
+    for (one, _, _, kept), two, three in zip(cubes, cubes2, cubes3):
+        cube_end(one, two, three)
+        kept.wait()
     arrived(second)
     for group in (first, second, smalls, chans, zs, ss):
         left(group)
 
 
-def last(part, tok_own, d_res, gain, rows_small, by_chan, gain_grad2, n_wt, n_seq, ident):
+def last(part, tok_own, d_res, gain, gain_grad2, sel, stp, taps, decays, bias3, blocks, more, n_wt, n_seq, ident):
     rows, cols = part.shape
     own = rows // n_wt
+    chan = taps.shape[1]
+    if more:
+        deep, tok_all = more[0].shape
+        units = more[2].shape[1] // 3
     return pl.pallas_call(
-        last_kernel,
+        functools.partial(last_kernel, len(blocks)),
         out_shape=[
             jax.ShapeDtypeStruct((rows, cols), BF16),
-            jax.ShapeDtypeStruct(rows_small.shape[1:], F32),
-            jax.ShapeDtypeStruct(by_chan.shape, F32),
-            jax.ShapeDtypeStruct((2, 1, cols), F32),
-        ],
-        in_specs=[VMEM] * 7,
-        out_specs=[VMEM] * 4,
-        scratch_shapes=[
+            jax.ShapeDtypeStruct(sel.shape[1:], F32),
+            jax.ShapeDtypeStruct(stp.shape[1:], F32),
+            jax.ShapeDtypeStruct((n_seq, 8, chan), F32),
+            jax.ShapeDtypeStruct((2 * cols // 128, 128), F32),
+        ]
+        + [jax.ShapeDtypeStruct((n_seq,) + a.shape, BF16) for a in blocks]
+        + ([jax.ShapeDtypeStruct((deep, units), F32)] * 3 if more else []),
+        in_specs=[VMEM] * 10 + [ANY] * len(blocks) + ([VMEM, VMEM, ANY] if more else []),
+        out_specs=[VMEM] * 5 + [ANY] * len(blocks) + ([VMEM] * 3 if more else []),
+        scratch_shapes=(
+            [pltpu.VMEM((2, tok_all, 3 * UNITS), BF16), pltpu.SemaphoreType.DMA((2,))]
+            if more
+            else []
+        )
+        + [
             pltpu.VMEM((n_wt - 1, own, cols), BF16),
-            pltpu.VMEM((n_seq - 1,) + rows_small.shape[1:], F32),
-            pltpu.VMEM((n_seq - 1,) + by_chan.shape, F32),
-            pltpu.VMEM((2, 8, cols), F32),
-            pltpu.VMEM((n_wt, 2, 8, cols), F32),
-            pltpu.VMEM((n_seq, 2, 8, cols), F32),
+            pltpu.VMEM((n_seq - 1,) + sel.shape[1:], BF16),
+            pltpu.VMEM((n_seq - 1,) + stp.shape[1:], BF16),
+            pltpu.VMEM((n_seq - 1, 8, chan), F32),
+            pltpu.VMEM((n_seq, 8, chan), F32),
+            pltpu.VMEM((8, cols), F32),
+            pltpu.VMEM((n_wt, 2 * cols // 128, 128), F32),
+            pltpu.VMEM((n_seq, 2 * cols // 128, 128), F32),
             pair_sems(n_wt),
             pair_sems(n_wt),
             pair_sems(n_seq),
             pair_sems(n_seq),
-            pair_sems(n_wt),
             pair_sems(n_seq),
-        ],
+            pair_sems(n_seq),
+            pair_sems(n_wt),
+            pair_sems(n_seq),
+        ]
+        + [cube_sems(), pltpu.SemaphoreType.DMA] * len(blocks),
         compiler_params=pltpu.CompilerParams(
             collective_id=ident, has_side_effects=True, vmem_limit_bytes=40 * MIB
         ),
         cost_estimate=pl.CostEstimate(flops=10**6, bytes_accessed=10**8, transcendentals=0),
-    )(part, tok_own, d_res, gain[None], rows_small, by_chan, gain_grad2)
+    )(part, tok_own, d_res, gain[None], gain_grad2, sel, stp, taps, decays, bias3, *blocks, *more)
 
 
 def load(ref):
@@ -619,19 +956,29 @@
     n_seq, n_wt = lax.axis_size("seq"), lax.axis_size("wt")
     z = lax.axis_index("wt")
     own = tok_count // n_wt
-    gather_acts = n_seq * tok_count <= width
-
-    w_mixer = gather(jnp.concatenate([inner_proj, switch_proj, mixer_out], axis=1))
-    w_first, w_mix = w_mixer[:, : 2 * chan], w_mixer[:, 2 * chan :]
-    w_small = lax.all_gather(jnp.concatenate([select_proj, step_proj], axis=0), "seq", axis=0)
-    w_select = w_small[:, : select_proj.shape[0]].reshape(-1, chan)
-    w_step = w_small[:, select_proj.shape[0] :].reshape(-1, chan)
-    w_all = gather(jnp.concatenate([ffn_gate, ffn_up, ffn_down], axis=1))
-    w_ffn, w_down = w_all[:, : 2 * units], w_all[:, 2 * units :]
+    cube = n_seq == 8 and n_seq * tok_count <= width
 
     token_vals = tokens.astype(F32)
     first_inv = lax.rsqrt(jnp.mean(token_vals * token_vals, axis=-1, keepdims=True) + EPS)
     first_in = (token_vals * first_inv * premix_gain).astype(BF16)
+    rows_sel, rows_step = select_proj.shape[0], step_proj.shape[0]
+    if cube:
+        fill = jnp.zeros((-(rows_sel + rows_step) % 32, chan), BF16)
+        small = jnp.concatenate([select_proj, step_proj, fill], axis=0)
+        w_mixer, w_small, cot_f, first_f = first_gather(
+            jnp.concatenate([inner_proj, switch_proj, mixer_out], axis=1),
+            small, cotangent, first_in, n_wt, n_seq, 7,
+        )
+        w_mixer = w_mixer.reshape(width, 3 * chan)
+    else:
+        w_mixer = gather(jnp.concatenate([inner_proj, switch_proj, mixer_out], axis=1))
+        w_small = lax.all_gather(jnp.concatenate([select_proj, step_proj], axis=0), "seq", axis=0)
+    w_first, w_mix = w_mixer[:, : 2 * chan], w_mixer[:, 2 * chan :]
+    w_select = w_small[:, :rows_sel].reshape(-1, chan)
+    w_step = w_small[:, rows_sel : rows_sel + rows_step].reshape(-1, chan)
+    ffn_own = jnp.concatenate([ffn_gate, ffn_up, ffn_down], axis=1)
+    ffn_own, w_small = lax.optimization_barrier((ffn_own, w_small))
+    w_all = gather(ffn_own)
     both = contract(first_in, w_first, "td,dc->tc")
     inner_act = both[:, :chan].astype(BF16)
     switch = both[:, chan:]
@@ -657,7 +1004,7 @@
         )
     mixed_in = jax.nn.silu(conv_out).astype(BF16)
     mixed_f = mixed_in.astype(F32)
-    select = wt_sum(contract(w_select, mixed_in, "jc,tc->jt"), n_wt, 0)
+    (select,) = wt_sum(contract(w_select, mixed_in, "jc,tc->jt"), (), (), n_wt, n_seq, 0)
     low_rank = select[:R].astype(BF16)
     write_vec = select[R : R + NS].T
     read_vec = select[R + NS :].T
@@ -676,18 +1023,10 @@
     tokens_own = lax.dynamic_slice_in_dim(tokens, z * own, own, 0).astype(F32)
     cot_own = lax.dynamic_slice_in_dim(cotangent, z * own, own, 0).astype(F32)
     second_in, residual = second_norm(mix_part, tokens_own, preffn_gain, n_wt, 2)
-    gate_up = contract(second_in, w_ffn, "td,df->tf")
-    gate_pre, up_pre = gate_up[:, :units], gate_up[:, units:]
-    gate_act = jax.nn.silu(gate_pre)
-    hidden = (gate_act * up_pre).astype(BF16)
-
-    d_hidden = contract(cotangent, w_down, "td,df->tf")
-    d_gate = (d_hidden * up_pre * silu_slope(gate_pre)).astype(BF16)
-    d_up = (d_hidden * gate_act).astype(BF16)
-    d_ffn = jnp.concatenate([d_gate, d_up], axis=1)
-    d_second = contract(d_ffn, w_ffn, "tf,df->td").astype(BF16)
-    d_branch, d_residual, grad_preffn = second_back(d_second, residual, cot_own, preffn_gain, n_wt, 3)
-    down_part = contract(hidden, w_down, "tf,df->td").astype(BF16)
+    acts, down_part, d_second = ffn(second_in, cotangent, w_all)
+    d_branch, d_residual, grad_preffn = second_back(
+        d_second, residual, cot_own, preffn_gain, n_wt, 3
+    )
     d_gated = contract(d_branch, w_mix, "td,dc->tc")
     d_scanned = d_gated * switch_act
     d_switch = (d_gated * scanned * silu_slope(switch)).astype(BF16)
@@ -702,8 +1041,11 @@
     d_pre = d_step * jax.nn.sigmoid(step_pre)
     grad_step_bias = jnp.sum(d_pre, axis=0)
     d_pre_low = d_pre.astype(BF16)
-    grad_step = contract(low_rank, d_pre_low, "rt,tc->rc")
-    d_select = wt_sum(
+    pad_rows = lambda v: jnp.pad(
+        v.reshape(n_seq, -1, tok_count), ((0, 0), (0, -(v.shape[0] // n_seq) % 16), (0, 0))
+    ).reshape(-1, tok_count)
+    grad_step = contract(pad_rows(low_rank), d_pre_low, "rt,tc->rc").astype(BF16)
+    d_select, *gathered = wt_sum(
         jnp.concatenate(
             [
                 contract(w_step, d_pre_low, "rc,tc->rt"),
@@ -712,10 +1054,14 @@
             ],
             axis=0,
         ),
+        (gated,) if cube else (),
+        (second_in, d_branch) if cube else (),
         n_wt,
+        n_seq,
         5,
-    ).astype(BF16)
-    grad_select = contract(d_select, mixed_in, "jt,tc->jc")
+    )
+    d_select = d_select.astype(BF16)
+    grad_select = contract(pad_rows(d_select), mixed_in, "jt,tc->jc").astype(BF16)
     d_mixed = (
         along * step_size
         + skip_gain[None, :] * d_scanned
@@ -749,65 +1095,53 @@
     d_first = contract(
         jnp.concatenate([d_inner_low, d_switch], axis=1), w_first, "tc,dc->td"
     ).astype(BF16)
-    small = jnp.concatenate(
-        [grad_select.reshape(n_seq, -1, chan), grad_step.reshape(n_seq, -1, chan)], axis=1
+    more = ()
+    if cube:
+        line_up = lambda v: v.reshape(n_seq * tok_count, v.shape[-1])
+        gated_all, second_f, branch_f = map(line_up, gathered)
+        more = (line_up(cot_f).T, second_f.T, gather(acts))
+    tokens_grad, out_select, out_step, by_chan, gains, *others = last(
+        d_first, tokens_own, d_residual, premix_gain, grad_preffn,
+        grad_select.reshape(n_seq, -1, chan), grad_step.reshape(n_seq, -1, chan),
+        jnp.stack(taps_rows, axis=0), grad_decay_log,
+        jnp.stack([grad_conv_bias, grad_step_bias, grad_skip]),
+        (d_switch, d_inner_low) if cube else (), more, n_wt, n_seq, 6,
     )
-    by_chan = jnp.concatenate(
-        [
-            jnp.stack(taps_rows, axis=0),
-            grad_decay_log,
-            grad_conv_bias[None],
-            grad_step_bias[None],
-            grad_skip[None],
-            jnp.zeros((1, chan), F32),
-        ],
-        axis=0,
-    )
-    tokens_grad, small, by_chan, gains = last(
-        d_first, tokens_own, d_residual, premix_gain, small, by_chan, grad_preffn, n_wt, n_seq, 6
-    )
-
-    if gather_acts:
-        ffn_all = gather(jnp.concatenate([hidden, d_ffn], axis=1))
-        mix_all = gather(jnp.concatenate([gated, d_switch, d_inner_low], axis=1))
-        blocks = lambda v: v.reshape(tok_count, n_seq, 1, width // n_seq)
-        early = jnp.concatenate([blocks(cotangent), blocks(first_in)], axis=2)
-        late = jnp.concatenate([blocks(second_in), blocks(d_branch)], axis=2)
-        early = lax.all_to_all(early, "seq", 1, 0, tiled=True).reshape(n_seq * tok_count, -1)
-        late = lax.all_to_all(late, "seq", 1, 0, tiled=True).reshape(n_seq * tok_count, -1)
-        piece = width // n_seq
-        cot_f, first_f = early[:, :piece], early[:, piece:]
-        second_f, branch_f = late[:, :piece], late[:, piece:]
-        out_down = contract(cot_f, ffn_all[:, :units], "td,tf->df")
-        out_gate = contract(second_f, ffn_all[:, units : 2 * units], "td,tf->df")
-        out_up = contract(second_f, ffn_all[:, 2 * units :], "td,tf->df")
-        out_mix = contract(branch_f, mix_all[:, :chan], "td,tc->dc")
-        out_switch = contract(first_f, mix_all[:, chan : 2 * chan], "td,tc->dc")
-        out_inner = contract(first_f, mix_all[:, 2 * chan :], "td,tc->dc")
+    share = -(-(KC + NS + 3) // n_seq)
+    by_chan = by_chan[:, :share].reshape(n_seq * share, chan)
+    gains = gains.reshape(2, width)
+    if cube:
+        out_down, out_gate, out_up = others[2:]
+        out_mix, out_switch, out_inner = grads(
+            (branch_f.T, line_up(first_f).T),
+            (0, 1, 1),
+            (gated_all, line_up(others[0]), line_up(others[1])),
+        )
     else:
         scatter = lambda v: lax.psum_scatter(v, "seq", scatter_dimension=0, tiled=True)
+        by_unit = acts.reshape(tok_count, -1, 3, UNITS)
+        hidden, d_gate, d_up = [by_unit[:, :, i].reshape(tok_count, units) for i in range(3)]
         out_down = scatter(contract(cotangent, hidden, "td,tf->df"))
         out_gate = scatter(contract(second_in, d_gate, "td,tf->df"))
         out_up = scatter(contract(second_in, d_up, "td,tf->df"))
         out_mix = scatter(contract(d_branch, gated, "td,tc->dc"))
         out_switch = scatter(contract(first_in, d_switch, "td,tc->dc"))
         out_inner = scatter(contract(first_in, d_inner_low, "td,tc->dc"))
-    rows_sel = select_proj.shape[0]
     return (
         block_out,
         tokens_grad,
-        gains[0, 0],
+        gains[0],
         out_inner,
         out_switch,
         by_chan[:KC],
         by_chan[KC + NS],
-        small[:rows_sel],
-        small[rows_sel:],
+        out_select[:rows_sel],
+        out_step[:rows_step],
         by_chan[KC + NS + 1],
         by_chan[KC : KC + NS],
         by_chan[KC + NS + 2],
         out_mix,
-        gains[1, 0],
+        gains[1],
         out_gate,
         out_up,
         out_down,

time: 740 us -> 544 us (0.74)
  waiting for transfers between devices: 149 us -> 18.8 us
  matrix products: 109 us -> 33.4 us
  Pallas kernels: 336 us -> 399 us
  blocking collectives: 57.4 us -> 0 us
  local copies, waits for them, and re-layouts: 27.5 us -> 45.9 us
    all_gather x4 -> x2, waiting for transfers between devices: 147 us -> 18.8 us  [gather(): return lax.all_gather(block, 'seq', axis=0, tiled=True)]
    dot_general x20 -> x10, matrix products: 109 us -> 33.4 us  [contract(): return jnp.einsum(pattern, left_op, right_op, preferred_element_type=F32)]
    pallas_call x3 -> x6, Pallas kernels: 158 us -> 228 us  [the longest x1 75 us: first_gather(): pl.pallas_call(first_kernel, out_shape=[jax.ShapeDtypeStruct((n_seq,) + m...]
    all_to_all x1 -> x0, blocking collectives: 43.9 us -> none  [local(): lax.all_to_all(early, 'seq', 1, 0, tiled=True)]
    unnamed x163 -> x154, local copies, waits for them, and re-layouts: 15.6 us -> 30.4 us
    all_gather x1 -> x0, blocking collectives: 13.4 us -> none  [local(): lax.all_gather(jnp.concatenate([select_proj, step_proj], axis=0), 'seq',...]
  transfers between devices with their start and end apart: 7 -> 4, of which waited for: 4 -> 1; matrix products, arithmetic and copies ran while one was open for 10% -> 12% of each run, Pallas kernels for 28% -> 44%
where the time goes in v2:
time: 544 us; the launch traced here: 543 us
  Pallas kernels  399 us (73%)
  local copies, waits for them, and re-layouts  45.9 us (8%)
  matrix products  33.4 us (6%)
  other arithmetic  26.4 us (5%)
  waiting for transfers between devices  18.8 us (3%)
  between operations  14.9 us (3%)
    pallas_call x1, Pallas kernels, first_gather(): pl.pallas_call(first_kernel, out_shape=[jax.ShapeDtypeStruct((n_seq,) + m...  75 us
    pallas_call x2, Pallas kernels, wt_sum(): pl.pallas_call(functools.partial(wt_sum_kernel, len(blocks), len(srcs)),...  67.3 us
    pallas_call x1, Pallas kernels, bwd_scan(): pl.pallas_call(bwd_kernel, out_shape=[jax.ShapeDtypeStruct((tok, high, 12...  60.3 us
    pallas_call x1, Pallas kernels, last(): pl.pallas_call(functools.partial(last_kernel, len(blocks)), out_shape=[ja...  58.3 us
    pallas_call x1, Pallas kernels, second_back(): pl.pallas_call(second_back_kernel, out_shape=[jax.ShapeDtypeStruct((rows,...  47 us
    pallas_call x1, Pallas kernels, second_norm(): pl.pallas_call(second_norm_kernel, out_shape=[jax.ShapeDtypeStruct((rows,...  46.9 us
    dot_general x10, matrix products, contract(): return jnp.einsum(pattern, left_op, right_op, preferred_element_type=F32)  33.4 us
    unnamed x154, local copies, waits for them, and re-layouts  30.4 us
  transfers between devices with their start and end apart: 4, of which 1 were waited for; matrix products, arithmetic and copies ran while one was open for 12% of the time, Pallas kernels for 44%

profile of v2, /device:TPU:0, one launch (start us, length us, event | category | flops | bytes accessed | tf_op | source)
XLA Modules:
  0.0 542.6 jit_solution(9378605343947581156)
XLA Ops:
  7.3 1.6 fusion.14
  8.9 2.5 fusion.16.act
  11.5 1.2 pad_maximum_fusion.1.mixer
  12.8 0.7 maximum_maximum_fusion.small
  13.9 1.7 pad_maximum_fusion
  15.6 75.0 %shard_map.305 = (bf16[8,256,3072]{2,1,0:T(8,128)(2,1)}, bf16[8,64,1024]{2,1,0:T(8,128)(2,1)}, bf16[8,4,64,256]{3,2,1,0:T(8,128)(2,1)}, bf16[8,4,64,256]{3,2,1,0:T(8,128)(2,1)}) custom-call(bf16[256,3072]{1,0:T(8,128)(2,1)} %pad_maximum_fusion.1.mixer, bf16[64,1024]{1,0:T(8,128)(2,1)} %maximum_maximum_fusion.small, bf16[256,2048]{1,0:T(8,128)(2,1)} %c.1, ...), custom_call_target="tpu_custom_call" | custom-call | flops 1000000 | bytes 100000000 | tf_op jit(solution)/shard_map/pallas_call | solution.py:237
  93.3 7.1 %fusion.56 = (bf16[256,2048]{1,0:T(8,128)(2,1)S(1)}, f32[256,2048]{1,0:T(8,128)}) fusion(bf16[256,2048]{1,0:T(8,128)(2,1)S(1)} %copy-done.42, bf16[2048,3072]{1,0:T(8,128)(2,1)} %bitcast.150), kind=kOutput, calls=%fused_computation.117 | convolution fusion | flops 2148007936 | bytes 12582912 | tf_op jit(solution)/shard_map/td,dc->tc/dot_general | solution.py:916
  100.5 2.4 collective-permute-start
  103.1 1.8 dynamic-slice_convert_fusion.1.tok
  105.6 1.8 multiply_convert_fusion.2
  107.4 1.0 fusion.57.part
  108.4 13.9 %shard_map.306 = f32[160,256]{1,0:T(8,128)} custom-call(f32[160,256]{1,0:T(8,128)} %fusion.57.part), custom_call_target="tpu_custom_call" | custom-call | flops 100000 | bytes 1000000 | tf_op jit(solution)/shard_map/pallas_call | solution.py:382
  122.3 1.2 convolution_add_fusion.1
  124.8 0.8 fusion.53
  125.8 17.2 %shard_map.307 = (f32[256,8,128]{2,1,0:T(8,128)S(1)}, f32[16,8,128]{2,1,0:T(8,128)S(1)}) custom-call(f32[256,8,128]{2,1,0:T(8,128)S(1)} %bitcast.96, f32[256,8,128]{2,1,0:T(8,128)S(1)} %bitcast.98, f32[256,16]{1,0:T(8,128)S(1)} %bitcast.104, f32[256,16]{1,0:T(8,128)S(1)} %bitcast.102, f32[16,8,128]{2,1,0:T(8,128)S(1)} %bitcast.106), custom_call_target="tpu_custom_call" | custom-call | flops 100000000 | bytes 80000000 | tf_op jit(solution)/shard_map/pallas_call | solution.py:747
  144.1 5.9 %fusion.8.part = bf16[256,2048]{1,0:T(8,128)(2,1)} fusion(bf16[256,1024]{1,0:T(8,128)(2,1)S(1)} %multiply_convert_fusion.1.refs_0_, bf16[2048,3072]{1,0:T(8,128)(2,1)} %bitcast.151), kind=kOutput, calls=%fused_computation.12 | convolution fusion | flops 1074266112 | bytes 5767168 | tf_op jit(solution)/shard_map/tc,dc->td/dot_general | solution.py:916
  149.9 46.9 %shard_map.308 = (bf16[256,2048]{1,0:T(8,128)(2,1)}, f32[64,2048]{1,0:T(8,128)}) custom-call(bf16[256,2048]{1,0:T(8,128)(2,1)} %fusion.8.part, f32[64,2048]{1,0:T(8,128)} %dynamic-slice_convert_fusion.1.tok, f32[1,2048]{1,0:T(1,128)} %bitcast.137), custom_call_target="tpu_custom_call" | custom-call | flops 1000000 | bytes 100000000 | tf_op jit(solution)/shard_map/pallas_call | solution.py:425
  196.8 18.8 %all-gather.3.cloned.1.call-done.wg.wu.wd = bf16[2048,6144]{1,0:T(8,128)(2,1)} async-done(((bf16[256,6144]{1,0:T(8,128)(2,1)}), bf16[2048,6144]{1,0:T(8,128)(2,1)}) %all-gather.3.cloned.1.call-update) | async-done | bytes 25165840 | tf_op jit(solution)/shard_map/all_gather | solution.py:906
  215.6 1.2 copy-done.2
  216.8 18.1 %shard_map.309 = (bf16[256,6144]{1,0:T(8,128)(2,1)S(1)}, bf16[256,2048]{1,0:T(8,128)(2,1)S(1)}, bf16[256,2048]{1,0:T(8,128)(2,1)S(1)}) custom-call(bf16[256,2048]{1,0:T(8,128)(2,1)S(1)} %copy-done.2, bf16[256,2048]{1,0:T(8,128)(2,1)S(1)} %copy-done, bf16[2048,6144]{1,0:T(8,128)(2,1)} %all-gather.3.cloned.1.call-done.wg.wu.wd, ...), custom_call_target="tpu_custom_call" | custom-call | flops 12884901888 | bytes 25165824 | tf_op jit(solution)/shard_map/pallas_call | solution.py:304
  234.9 1.6 copy-done.3
  236.5 1.0 copy-done.18
  237.5 1.0 copy-done.30
  238.5 1.6 copy.51
  240.6 0.8 dynamic-slice_convert_fusion.cot
  241.4 47.0 %shard_map.310 = (bf16[256,2048]{1,0:T(8,128)(2,1)}, f32[64,2048]{1,0:T(8,128)}, f32[8,2048]{1,0:T(8,128)}) custom-call(bf16[256,2048]{1,0:T(8,128)(2,1)} %copy-done.18, f32[64,2048]{1,0:T(8,128)} %get-tuple-element.61.res, f32[64,2048]{1,0:T(8,128)} %dynamic-slice_convert_fusion.cot, f32[1,2048]{1,0:T(1,128)} %bitcast.138), custom_call_target="tpu_custom_call" | custom-call | flops 1000000 | bytes 100000000 | tf_op jit(solution)/shard_map/pallas_call | solution.py:478
  288.5 5.9 %fusion.23 = (f32[1024]{0:T(1024)}, f32[256,1024]{1,0:T(8,128)S(1)}, bf16[256,1024]{1,0:T(8,128)(2,1)}) fusion(bf16[256,1024]{1,0:T(8,128)(2,1)S(1)} %copy-done.36, f32[256,2048]{1,0:T(8,128)} %get-tuple-element.128, f32[1024]{0:T(1024)S(1)} %copy-done.68, f32[32,8,8,128]{3,2,1,0:T(8,128)S(1)} %bitcast.101, ...), kind=kOutput, calls=%fused_computation.37 | convolution fusion | flops 1078197248 | bytes 9445376 | tf_op jit(solution)/shard_map/td,dc->tc/dot_general | solution.py:916
  294.4 1.0 copy-done.49
  295.4 1.2 copy.61
  296.5 60.3 %shard_map.311 = (f32[256,8,128]{2,1,0:T(8,128)}, f32[256,8,128]{2,1,0:T(8,128)}, f32[16,8,128]{2,1,0:T(8,128)}, f32[256,16,128]{2,1,0:T(8,128)}, f32[256,16,128]{2,1,0:T(8,128)}, /*index=5*/bf16[256,2048]{1,0:T(8,128)(2,1)}) custom-call(f32[256,8,128]{2,1,0:T(8,128)} %bitcast.97, f32[256,8,128]{2,1,0:T(8,128)} %bitcast.99, f32[256,16]{1,0:T(8,128)} %bitcast.105, ...), custom_call_target="tpu_custom_call" | custom-call | flops 100000000 | bytes 150000000 | tf_op jit(solution)/shard_map/pallas_call | solution.py:872
  356.8 2.2 reduce_sum.91
  359.1 2.4 reduce_sum.92
  361.6 1.4 broadcast_multiply_fusion
  364.8 2.3 copy.54
  367.1 53.4 %shard_map.312 = (f32[160,256]{1,0:T(8,128)}, bf16[8,256,1024]{2,1,0:T(8,128)(2,1)}, bf16[8,256,256]{2,1,0:T(8,128)(2,1)}, bf16[8,256,256]{2,1,0:T(8,128)(2,1)}) custom-call(f32[160,256]{1,0:T(8,128)} %pad_maximum_fusion.2.part, bf16[256,1024]{1,0:T(8,128)(2,1)} %copy-done.43, bf16[256,2048]{1,0:T(8,128)(2,1)} %get-tuple-element.58.x.refs_1_, ...), custom_call_target="tpu_custom_call" | custom-call | flops 100000 | bytes 1000000 | tf_op jit(solution)/shard_map/pallas_call | solution.py:382
  420.5 1.6 convert_element_type.97
  422.1 1.5 reshape.159
  423.6 0.9 pad.6
  424.6 3.8 fusion.24
  428.6 1.5 collective-permute-start.1
  430.5 1.1 convolution_convert_fusion
  431.6 1.5 copy.55
  433.1 1.4 copy.56
  434.5 1.1 maximum_convert_fusion.1
  436.8 6.8 %fusion.11.part = bf16[256,2048]{1,0:T(8,128)(2,1)} fusion(bf16[2048,3072]{1,0:T(8,128)(2,1)} %bitcast.153, bf16[256,1024]{1,0:T(8,128)(2,1)S(1)} %copy-done.20, bf16[256,1024]{1,0:T(8,128)(2,1)S(1)} %fusion.34.refs_1_), kind=kOutput, calls=%fused_computation.13 | convolution fusion | flops 2150105088 | bytes 10485760 | tf_op jit(solution)/shard_map/tc,dc->td/dot_general | solution.py:916
  443.5 1.0 copy-done.4
  444.6 1.2 copy-done.11
  445.8 1.0 copy-done.19
  446.8 1.0 copy-done.21
  447.9 0.8 copy-done.25
  448.7 58.3 %shard_map.313 = (bf16[256,2048]{1,0:T(8,128)(2,1)S(1)}, f32[32,1024]{1,0:T(8,128)S(1)}, f32[16,1024]{1,0:T(8,128)S(1)}, f32[8,8,1024]{2,1,0:T(8,128)S(1)}, f32[...) custom-call(bf16[256,2048]{1,0:T(8,128)(2,1)S(1)} %copy-done.11, ...), custom_call_target="tpu_custom_call" | custom-call | flops 1000000 | bytes 100000000 | tf_op jit(solution)/shard_map/pallas_call | solution.py:622
  507.0 1.3 copy-done.5
  508.3 1.3 copy-done.7
  509.7 1.3 copy-done.9
  511.0 1.0 copy-done.14
  515.2 1.5 slice.192
  517.3 9.2 %shard_map.314 = (f32[256,1024]{1,0:T(8,128)}, f32[256,1024]{1,0:T(8,128)}, f32[256,1024]{1,0:T(8,128)}) custom-call(bf16[256,2048]{1,0:T(8,128)(2,1)} %bitcast.110, bf16[256,2048]{1,0:T(8,128)(2,1)} %bitcast.109, bf16[2048,1024]{1,0:T(8,128)(2,1)} %bitcast.111, bf16[2048,1024]{1,0:T(8,128)(2,1)} %bitcast.112, bf16[2048,1024]{1,0:T(8,128)(2,1)} %bitcast.113), custom_call_target="tpu_custom_call" | custom-call | flops 3221225472 | bytes 12582912 | tf_op jit(solution)/shard_map/pallas_call | solution.py:332
  526.6 1.0 copy.82
  528.1 1.0 copy.83
  529.8 1.3 copy.85
  531.1 1.0 copy-done.8
  532.1 1.3 copy.86
  533.4 1.0 copy-done.6
  534.4 1.3 copy.87
  (181 shorter events, 15.3 us)
Async XLA Ops:
  7.2 4.3 copy-start.58
  7.2 4.3 copy-start.57
  7.2 4.3 copy-start.56
  7.2 208.4 %all-gather.3.cloned.1.call-start = ((), (), s32[]{:S(2)}) async-start(), calls=%async_computation | async-start | bytes 28311552 | tf_op jit(solution)/shard_map/all_gather | solution.py:906
  8.9 3.9 copy-start.63
  8.9 3.9 copy-start.64
  11.4 2.1 copy-start.51
  11.4 2.1 copy-start.52
  11.4 2.5 copy-start.53
  90.6 2.7 copy-start.42
  90.7 352.8 %all-gather.5.cloned.1.call-start = ((), (), s32[]{:S(2)}) async-start(), calls=%async_computation.1 | async-start | bytes 28311552 | tf_op jit(solution)/shard_map/all_gather | solution.py:906
  93.3 9.7 %copy-start.65 = (f32[4,1024]{1,0:T(4,128)S(1)}, f32[4,1024]{1,0:T(4,128)}, u32[]{:S(2)}) copy-start(f32[4,1024]{1,0:T(4,128)} %param.24) | copy-start | bytes 49156
  93.3 9.7 %copy-start.60 = (f32[16,1024]{1,0:T(8,128)S(1)}, f32[16,1024]{1,0:T(8,128)}, u32[]{:S(2)}) copy-start(f32[16,1024]{1,0:T(8,128)} %param.29) | copy-start | bytes 196612
  100.4 4.5 copy-start.59
  100.5 4.6 collective-permute-start
  105.2 2.3 copy-start.44
  105.3 2.1 copy-start.32
  105.6 16.7 %copy-start.67 = (f32[1024]{0:T(1024)S(1)}, f32[1024]{0:T(1024)}, u32[]{:S(2)}) copy-start(f32[1024]{0:T(1024)} %param.28) | copy-start | bytes 12292
  107.4 16.9 %copy-start.34 = (bf16[256,1024]{1,0:T(8,128)(2,1)}, bf16[256,1024]{1,0:T(8,128)(2,1)S(1)}, u32[]{:S(2)}) copy-start(bf16[256,1024]{1,0:T(8,128)(2,1)S(1)} %get-tuple-element.104) | copy-start | bytes 1572868
  108.4 17.4 %copy-start.26 = (f32[2,8,8,128]{3,2,1,0:T(8,128)}, f32[2,8,8,128]{3,2,1,0:T(8,128)S(1)}, u32[]{:S(2)}) copy-start(f32[2,8,8,128]{3,2,1,0:T(8,128)S(1)} %copy.59) | copy-start | bytes 196612
  124.5 18.5 %copy-start.12 = (f32[32,8,8,128]{3,2,1,0:T(8,128)}, f32[32,8,8,128]{3,2,1,0:T(8,128)S(1)}, u32[]{:S(2)}) copy-start(f32[32,8,8,128]{3,2,1,0:T(8,128)S(1)} %copy.57) | copy-start | bytes 3145732
  124.7 18.3 %copy-start.13 = (f32[32,8,8,128]{3,2,1,0:T(8,128)}, f32[32,8,8,128]{3,2,1,0:T(8,128)S(1)}, u32[]{:S(2)}) copy-start(f32[32,8,8,128]{3,2,1,0:T(8,128)S(1)} %copy.58) | copy-start | bytes 3145732
  125.7 17.4 %copy-start.22 = (f32[16,256]{0,1:T(8,128)}, f32[16,256]{0,1:T(8,128)S(1)}, u32[]{:S(2)}) copy-start(f32[16,256]{0,1:T(8,128)S(1)} %copy.48) | copy-start | bytes 49156
  125.8 17.3 %copy-start.23 = (f32[16,256]{0,1:T(8,128)}, f32[16,256]{0,1:T(8,128)S(1)}, u32[]{:S(2)}) copy-start(f32[16,256]{0,1:T(8,128)S(1)} %copy.47) | copy-start | bytes 49156
  125.8 17.3 %copy-start.35 = (bf16[256,1024]{1,0:T(8,128)(2,1)S(1)}, bf16[256,1024]{1,0:T(8,128)(2,1)}, u32[]{:S(2)}) copy-start(bf16[256,1024]{1,0:T(8,128)(2,1)} %copy-done.34) | copy-start | bytes 1572868
  125.8 17.3 %copy-start.55 = (f32[256,2048]{1,0:T(8,128)S(1)}, f32[256,2048]{1,0:T(8,128)}, u32[]{:S(2)}) copy-start(f32[256,2048]{1,0:T(8,128)} %get-tuple-element.128) | copy-start | bytes 6291460
  125.8 17.3 %copy-start.68 = (f32[1024]{0:T(1024)S(1)}, f32[1024]{0:T(1024)}, u32[]{:S(2)}) copy-start(f32[1024]{0:T(1024)} %param.30) | copy-start | bytes 12292
  143.1 6.8 %copy-start.31 = (f32[16,8,128]{2,1,0:T(8,128)}, f32[16,8,128]{2,1,0:T(8,128)S(1)}, u32[]{:S(2)}) copy-start(f32[16,8,128]{2,1,0:T(8,128)S(1)} %get-tuple-element.63.h0) | copy-start | bytes 196612
  144.1 5.9 %copy-start.43 = (bf16[256,1024]{1,0:T(8,128)(2,1)}, bf16[256,1024]{1,0:T(8,128)(2,1)S(1)}, u32[]{:S(2)}) copy-start(bf16[256,1024]{1,0:T(8,128)(2,1)S(1)} %multiply_convert_fusion.1.refs_0_) | copy-start | bytes 1572868
  149.9 65.7 %copy-start = (bf16[256,2048]{1,0:T(8,128)(2,1)S(1)}, bf16[256,2048]{1,0:T(8,128)(2,1)}, u32[]{:S(2)}) copy-start(bf16[256,2048]{1,0:T(8,128)(2,1)} %c.1) | copy-start | bytes 3145732
  215.6 1.2 copy-start.2
  234.9 1.6 copy-start.3
  238.5 50.0 %copy-start.17 = (f32[256,8,128]{2,1,0:T(8,128)S(1)}, f32[256,8,128]{2,1,0:T(8,128)}, u32[]{:S(2)}) copy-start(f32[256,8,128]{2,1,0:T(8,128)} %copy-done.16) | copy-start | bytes 3145732
  241.4 47.0 %copy-start.36 = (bf16[256,1024]{1,0:T(8,128)(2,1)S(1)}, bf16[256,1024]{1,0:T(8,128)(2,1)}, u32[]{:S(2)}) copy-start(bf16[256,1024]{1,0:T(8,128)(2,1)} %copy-done.34) | copy-start | bytes 1572868
  359.1 3.9 copy-start.39
  361.6 1.6 copy-start.47
  367.1 57.4 %copy-start.33 = (f32[259,1024]{1,0:T(8,128)S(1)}, f32[259,1024]{1,0:T(8,128)}, u32[]{:S(2)}) copy-start(f32[259,1024]{1,0:T(8,128)} %copy-done.32) | copy-start | bytes 3182596
  367.1 57.4 %copy-start.45 = (bf16[160,1024]{1,0:T(8,128)(2,1)S(1)}, bf16[160,1024]{1,0:T(8,128)(2,1)}, u32[]{:S(2)}) copy-start(bf16[160,1024]{1,0:T(8,128)(2,1)} %copy-done.44) | copy-start | bytes 983044
  424.5 3.9 copy-start.71
  424.6 5.6 %copy-start.69 = (f32[1024]{0:T(1024)S(1)}, f32[1024]{0:T(1024)}, u32[]{:S(2)}) copy-start(f32[1024]{0:T(1024)} %get-tuple-element.100) | copy-start | bytes 12292
  424.6 5.6 %copy-start.61 = (f32[16,1024]{1,0:T(8,128)S(1)}, f32[16,1024]{1,0:T(8,128)}, u32[]{:S(2)}) copy-start(f32[16,1024]{1,0:T(8,128)} %param.29) | copy-start | bytes 196612
  424.6 5.6 %copy-start.62 = (f32[16,8,128]{2,1,0:T(8,128)S(1)}, f32[16,8,128]{2,1,0:T(8,128)}, u32[]{:S(2)}) copy-start(f32[16,8,128]{2,1,0:T(8,128)} %get-tuple-element.73) | copy-start | bytes 196612
  424.6 5.6 %copy-start.41 = (bf16[256,1024]{1,0:T(8,128)(2,1)S(1)}, bf16[256,1024]{1,0:T(8,128)(2,1)}, u32[]{:S(2)}) copy-start(bf16[256,1024]{1,0:T(8,128)(2,1)} %copy-done.40) | copy-start | bytes 1572868
  424.6 5.6 %copy-start.46 = (f32[160,256]{1,0:T(8,128)S(1)}, f32[160,256]{1,0:T(8,128)}, u32[]{:S(2)}) copy-start(f32[160,256]{1,0:T(8,128)} %shard_map.306) | copy-start | bytes 491524
  424.6 5.9 %copy-start.37 = (bf16[256,1024]{1,0:T(8,128)(2,1)S(1)}, bf16[256,1024]{1,0:T(8,128)(2,1)}, u32[]{:S(2)}) copy-start(bf16[256,1024]{1,0:T(8,128)(2,1)} %copy-done.34) | copy-start | bytes 1572868
  428.5 3.1 copy-start.54
  428.6 6.0 %collective-permute-start.1 = (bf16[3,1024]{1,0:T(4,128)(2,1)S(1)}, bf16[3,1024]{1,0:T(4,128)(2,1)S(1)}, u32[]{:S(2)}, u32[]{:S(2)}) collective-permute-start(bf16[3,1024]{1,0:T(4,128)(2,1)S(1)} %slice_select_fusion), channel_id=1, source_target_pairs={{4,0},{8,4},{12,8},{16,12},{20,16},{24,20},{28,24},{5,1},{9,5},{13... | collective-permute-start | bytes 18440 | tf_op jit(solution)/shard_map/ppermute | solution.py:912
  430.2 2.9 copy-start.50
  435.7 1.0 copy-start.20
  436.7 6.8 %copy-start.1 = (f32[64,2048]{1,0:T(8,128)S(1)}, f32[64,2048]{1,0:T(8,128)}, u32[]{:S(2)}) copy-start(f32[64,2048]{1,0:T(8,128)} %dynamic-slice_convert_fusion.1.tok) | copy-start | bytes 1572868
  436.8 6.8 %copy-start.29 = (f32[2048]{0:T(1024)S(1)}, f32[2048]{0:T(1024)}, u32[]{:S(2)}) copy-start(f32[2048]{0:T(1024)} %param.21) | copy-start | bytes 24580
  443.5 1.0 copy-start.4
  444.6 1.2 copy-start.11
  445.8 1.0 copy-start.19
  446.8 1.0 copy-start.21
  507.0 1.3 copy-start.5
  508.3 1.3 copy-start.7
  509.7 1.3 copy-start.9
  517.3 9.2 %copy-start.48 = (bf16[256,2048]{1,0:T(8,128)(2,1)S(1)}, bf16[256,2048]{1,0:T(8,128)(2,1)}, u32[]{:S(2)}) copy-start(bf16[256,2048]{1,0:T(8,128)(2,1)} %get-tuple-element.149) | copy-start | bytes 3145732
  526.5 1.6 copy-start.15
  526.5 2.6 copy-start.28
  526.6 3.2 copy-start.10
  529.7 2.3 copy-start.8
  532.1 2.3 copy-start.6
  (12 other events, 10.3 us)
Sparse Core Ops, SparseCore 0:
  90.8 124.7 all-gather.2
  238.6 131.2 all-gather.4

commit v3 on v2

--- a/solution.py
+++ b/solution.py
@@ -19,7 +19,7 @@
 VMEM = pl.BlockSpec(memory_space=pltpu.VMEM)
 SMEM = pl.BlockSpec(memory_space=pltpu.SMEM)
 ANY = pl.BlockSpec(memory_space=pl.ANY)
-MIB = 2**20
+VMEM_BYTES = 60 * 2**20
 
 
 def greet(axes):
@@ -97,6 +97,76 @@
         return carry
 
     lax.fori_loop(0, rows // step, run, 0)
+
+
+def mates():
+    z = lax.axis_index("wt")
+    mate = z + 1 - 2 * lax.rem(z, 2)
+    return z, mate, lax.rem(z + 2, 4), lax.rem(mate + 2, 4)
+
+
+def line_scatter_start(part, recv, sems):
+    if lax.axis_size("wt") != 4:
+        return scatter_start(part, recv, sems, "wt")
+    rows = recv.shape[1]
+    _, mate, _, far_mate = mates()
+    return [
+        send(part.at[pl.ds(far_mate * rows, rows)], recv.at[0], sems, 0, "wt", mate),
+        send(part.at[pl.ds(mate * rows, rows)], recv.at[1], sems, 1, "wt", mate),
+    ]
+
+
+def line_scatter_mid(part, recv, pend, sems, copies):
+    if lax.axis_size("wt") != 4:
+        return copies
+    rows = recv.shape[1]
+    _, _, far, _ = mates()
+    copies[0].wait_recv()
+
+    def body(at):
+        mine = part[pl.ds(pl.multiple_of(far * rows + at, 16), 16)].astype(F32)
+        pend[pl.ds(at, 16)] = (mine + recv[0, pl.ds(at, 16)].astype(F32)).astype(BF16)
+
+    step_rows(rows, 16, body)
+    return copies + [send(pend, recv.at[2], sems, 2, "wt", far)]
+
+
+def line_scatter_end(copies):
+    if lax.axis_size("wt") != 4:
+        arrived(copies)
+    else:
+        arrived(copies[1:])
+
+
+def line_summed(part, recv, at, step, row0):
+    if lax.axis_size("wt") != 4:
+        return summed(part, recv, at, step, row0)
+    total = part[pl.ds(row0 + at, step)].astype(F32)
+    return total + recv[1, pl.ds(at, step)].astype(F32) + recv[2, pl.ds(at, step)].astype(F32)
+
+
+def line_gather_start(whole, rows, sems):
+    if lax.axis_size("wt") != 4:
+        return gather_start(whole, rows, sems, "wt")
+    z, mate, far, _ = mates()
+    mine = whole.at[pl.ds(z * rows, rows)]
+    return [send(mine, mine, sems, 0, "wt", far), send(mine, mine, sems, 1, "wt", mate)]
+
+
+def line_gather_mid(whole, rows, sems, copies):
+    if lax.axis_size("wt") != 4:
+        return copies
+    _, mate, far, _ = mates()
+    copies[0].wait_recv()
+    piece = whole.at[pl.ds(far * rows, rows)]
+    return copies + [send(piece, piece, sems, 2, "wt", mate)]
+
+
+def line_gather_end(copies):
+    if lax.axis_size("wt") != 4:
+        arrived(copies)
+    else:
+        arrived(copies[1:])
 
 
 def flips():
@@ -186,38 +256,51 @@
         left(group)
 
 
+def share(src, dst, sems, own_sem):
+    seq, n_seq, z = lax.axis_index("seq"), lax.axis_size("seq"), lax.axis_index("wt")
+    own, piece = dst.shape[2:]
+    rows = src.at[pl.ds(pl.multiple_of(z * own, own), own)]
+
+    def columns(peer):
+        return rows.at[:, pl.ds(pl.multiple_of(peer * piece, piece), piece)]
+
+    sent = []
+    for k in range(1, n_seq):
+        peer = lax.rem(seq + k, n_seq)
+        sent.append(send(columns(peer), dst.at[seq, z], sems, k - 1, "seq", peer))
+    kept = pltpu.make_async_copy(columns(seq), dst.at[seq, z], own_sem)
+    kept.start()
+    return sent, kept
+
+
+def pass_along(dst, sems):
+    z, n_wt = lax.axis_index("wt"), lax.axis_size("wt")
+    lines = dst.at[:, z]
+    return [send(lines, lines, sems, k - 1, "wt", lax.rem(z + k, n_wt)) for k in range(1, n_wt)]
+
+
 def first_kernel(
-    mixer, small, cot, act, w_mixer, w_small, cot_f, act_f,
+    mixer, small, cot, tok, gain, w_mixer, w_small, cot_f, act_f, act,
     s_big, s_small, s_own, s_cot, s_act, s_cz, s_az,
 ):
-    seq, n_seq = lax.axis_index("seq"), lax.axis_size("seq")
-    z, n_wt = lax.axis_index("wt"), lax.axis_size("wt")
-    own, piece = cot_f.shape[2:]
     kept = [keep(mixer, w_mixer, s_own.at[0]), keep(small, w_small, s_own.at[1])]
+
+    def norm(at):
+        v = tok[pl.ds(at, 16)].astype(F32)
+        inverse = lax.rsqrt(jnp.mean(v * v, axis=-1, keepdims=True) + EPS)
+        act[pl.ds(at, 16)] = (v * inverse * gain[...]).astype(BF16)
+
+    step_rows(tok.shape[0], 16, norm)
     greet(("seq", "wt"))
     little = cube_first(small, w_small, s_small)
-    sent, mine = [], []
-    for i, (src, dst, sems) in enumerate(((cot, cot_f, s_cot), (act, act_f, s_act))):
-        rows = src.at[pl.ds(pl.multiple_of(z * own, own), own)]
-
-        def columns(peer, rows=rows):
-            return rows.at[:, pl.ds(pl.multiple_of(peer * piece, piece), piece)]
-
-        for k in range(1, n_seq):
-            peer = lax.rem(seq + k, n_seq)
-            sent.append(send(columns(peer), dst.at[seq, z], sems, k - 1, "seq", peer))
-        mine.append(pltpu.make_async_copy(columns(seq), dst.at[seq, z], s_own.at[2 + i]))
-        mine[-1].start()
+    sent1, kept1 = share(cot, cot_f, s_cot, s_own.at[2])
+    sent2, kept2 = share(act, act_f, s_act, s_own.at[3])
     big = cube_first(mixer, w_mixer, s_big)
+    sent = sent1 + sent2
     arrived(sent)
-    for copy in mine:
-        copy.wait()
-    along = []
-    for dst, sems in ((cot_f, s_cz), (act_f, s_az)):
-        lines = dst.at[:, z]
-        along += [
-            send(lines, lines, sems, k - 1, "wt", lax.rem(z + k, n_wt)) for k in range(1, n_wt)
-        ]
+    kept1.wait()
+    kept2.wait()
+    along = pass_along(cot_f, s_cz) + pass_along(act_f, s_az)
     little2 = cube_second(w_small, s_small, little)
     little3 = cube_third(w_small, s_small, little2)
     big2 = cube_second(w_mixer, s_big, big)
@@ -231,9 +314,9 @@
         copy.wait()
 
 
-def first_gather(mixer, small, cot, act, n_wt, n_seq, ident):
-    tok, width = cot.shape
-    far = jax.ShapeDtypeStruct((n_seq, n_wt, tok // n_wt, width // n_seq), BF16)
+def first_gather(mixer, small, cot, tok, gain, n_wt, n_seq, ident):
+    count, width = cot.shape
+    far = jax.ShapeDtypeStruct((n_seq, n_wt, count // n_wt, width // n_seq), BF16)
     return pl.pallas_call(
         first_kernel,
         out_shape=[
@@ -241,9 +324,10 @@
             jax.ShapeDtypeStruct((n_seq,) + small.shape, BF16),
             far,
             far,
+            jax.ShapeDtypeStruct((count, width), BF16),
         ],
-        in_specs=[ANY, ANY, VMEM, VMEM],
-        out_specs=[ANY] * 4,
+        in_specs=[ANY, ANY] + [VMEM] * 3,
+        out_specs=[ANY] * 4 + [VMEM],
         scratch_shapes=[
             cube_sems(),
             cube_sems(),
@@ -253,9 +337,11 @@
             pair_sems(n_wt),
             pair_sems(n_wt),
         ],
-        compiler_params=pltpu.CompilerParams(collective_id=ident, has_side_effects=True),
+        compiler_params=pltpu.CompilerParams(
+            collective_id=ident, has_side_effects=True, vmem_limit_bytes=VMEM_BYTES
+        ),
         cost_estimate=pl.CostEstimate(flops=10**6, bytes_accessed=10**8, transcendentals=0),
-    )(mixer, small, cot, act)
+    )(mixer, small, cot, tok, gain[None])
 
 
 UNITS = 256
@@ -267,7 +353,7 @@
     )
 
 
-def ffn_kernel(x, c, wg, wu, wd, acts, down, d_second, acc_down, acc_second):
+def ffn_kernel(x, c, wg, wu, wd, gated, acts, down, d_second, acc_down, acc_second):
     step = pl.program_id(0)
 
     @pl.when(step == 0)
@@ -285,7 +371,8 @@
     d_up = (d_hidden * act).astype(BF16)
     acts[:, :UNITS] = hidden
     acts[:, UNITS : 2 * UNITS] = d_gate
-    acts[:, 2 * UNITS :] = d_up
+    acts[:, 2 * UNITS : 3 * UNITS] = d_up
+    acts[:, 3 * UNITS :] = gated[...]
     acc_down[...] += nt(hidden, wd[...])
     acc_second[...] += nt(d_gate, wg[...]) + nt(d_up, wu[...])
 
@@ -295,28 +382,30 @@
         d_second[...] = acc_second[...].astype(BF16)
 
 
-def ffn(x, c, w_all):
+def ffn(x, c, w_all, gated):
     tok, width = x.shape
-    units = w_all.shape[1] // 3
+    units, chan = w_all.shape[1] // 3, gated.shape[1]
     steps = units // UNITS
+    span = 3 * UNITS + chan // steps
     whole = pl.BlockSpec((tok, width), lambda i: (0, 0))
     tile = lambda part: pl.BlockSpec((width, UNITS), lambda i: (0, part * steps + i))
     return pl.pallas_call(
         ffn_kernel,
         grid=(steps,),
-        in_specs=[whole, whole, tile(0), tile(1), tile(2)],
-        out_specs=[pl.BlockSpec((tok, 3 * UNITS), lambda i: (0, i)), whole, whole],
+        in_specs=[whole, whole, tile(0), tile(1), tile(2)]
+        + [pl.BlockSpec((tok, chan // steps), lambda i: (0, i))],
+        out_specs=[pl.BlockSpec((tok, span), lambda i: (0, i)), whole, whole],
         out_shape=[
-            jax.ShapeDtypeStruct((tok, 3 * units), BF16),
+            jax.ShapeDtypeStruct((tok, 3 * units + chan), BF16),
             jax.ShapeDtypeStruct((tok, width), BF16),
             jax.ShapeDtypeStruct((tok, width), BF16),
         ],
         scratch_shapes=[pltpu.VMEM((tok, width), F32)] * 2,
-        compiler_params=pltpu.CompilerParams(vmem_limit_bytes=40 * MIB),
+        compiler_params=pltpu.CompilerParams(vmem_limit_bytes=VMEM_BYTES),
         cost_estimate=pl.CostEstimate(
             flops=12 * tok * width * units, bytes_accessed=6 * width * units, transcendentals=0
         ),
-    )(x, c, w_all, w_all, w_all)
+    )(x, c, w_all, w_all, w_all, gated)
 
 
 def grads_kernel(lefts, *refs):
@@ -336,22 +425,26 @@
         + [pl.BlockSpec((tok, UNITS), lambda i: (0, i))] * n,
         out_specs=[pl.BlockSpec((rows, UNITS), lambda i: (0, i))] * n,
         out_shape=[jax.ShapeDtypeStruct((rows, cols), F32)] * n,
-        compiler_params=pltpu.CompilerParams(vmem_limit_bytes=60 * MIB),
+        compiler_params=pltpu.CompilerParams(vmem_limit_bytes=VMEM_BYTES),
         cost_estimate=pl.CostEstimate(
             flops=2 * n * tok * rows * cols, bytes_accessed=2 * n * tok * cols, transcendentals=0
         ),
     )(*left_ops, *acts)
 
 
-def wt_sum_kernel(n_cube, n_spread, part, *refs):
+def wt_sum_kernel(n_cube, n_spread, n_line, part, *refs):
     n = n_cube + n_spread
-    srcs, out, dsts, refs = refs[:n], refs[n], refs[n + 1 : 2 * n + 1], refs[2 * n + 1 :]
+    srcs, refs = refs[:n], refs[n:]
+    lines, out, refs = refs[:n_line], refs[n_line], refs[n_line + 1 :]
+    dsts, wholes, refs = refs[:n], refs[n : n + n_line], refs[n + n_line :]
     recv, s_scatter, s_gather = refs[:3]
+    sems = refs[3:]
     me = lax.axis_index("wt")
     rows = recv.shape[1]
+    for line, whole in zip(lines, wholes):
+        whole[pl.ds(pl.multiple_of(me * line.shape[0], 16), line.shape[0])] = line[...]
     greet(("wt", "seq") if n else ("wt",))
     first = scatter_start(part, recv, s_scatter, "wt")
-    sems = refs[3:]
     cubes, sent, kept = [], [], []
     for i in range(n):
         if i < n_cube:
@@ -364,57 +457,69 @@
     arrived(first)
     out[pl.ds(me * rows, rows)] = summed(part, recv, 0, rows, me * rows)
     second = gather_start(out, rows, s_gather, "wt")
+    along = [line_gather_start(w, w.shape[0] // lax.axis_size("wt"), sems[-1]) for w in wholes]
     cubes2 = [cube_second(dsts[i], sems[2 * i], cubes[i]) for i in range(n_cube)]
     cubes3 = [cube_third(dsts[i], sems[2 * i], cubes2[i]) for i in range(n_cube)]
+    along = [
+        line_gather_mid(w, w.shape[0] // lax.axis_size("wt"), sems[-1], a)
+        for w, a in zip(wholes, along)
+    ]
+    for copies in along:
+        line_gather_end(copies)
     for one, two, three in zip(cubes, cubes2, cubes3):
         cube_end(one, two, three)
     for copy in kept:
         copy.wait()
     arrived(second)
     arrived(sent)
-    left(first)
-    left(second)
-    left(sent)
-
-
-def wt_sum(part, blocks, srcs, n_wt, n_seq, ident):
+    for group in (first, second, sent, *along):
+        left(group)
+
+
+def wt_sum(part, blocks, srcs, lines, n_wt, n_seq, ident):
     rows, cols = part.shape
     return pl.pallas_call(
-        functools.partial(wt_sum_kernel, len(blocks), len(srcs)),
+        functools.partial(wt_sum_kernel, len(blocks), len(srcs), len(lines)),
         out_shape=[jax.ShapeDtypeStruct((rows, cols), F32)]
         + [jax.ShapeDtypeStruct((n_seq,) + a.shape, BF16) for a in blocks]
-        + [jax.ShapeDtypeStruct((n_seq, a.shape[0], a.shape[1] // n_seq), BF16) for a in srcs],
-        in_specs=[VMEM] + [ANY] * len(blocks) + [VMEM] * len(srcs),
-        out_specs=[VMEM] + [ANY] * len(blocks + srcs),
+        + [jax.ShapeDtypeStruct((n_seq, a.shape[0], a.shape[1] // n_seq), BF16) for a in srcs]
+        + [jax.ShapeDtypeStruct((n_wt * a.shape[0], a.shape[1]), BF16) for a in lines],
+        in_specs=[VMEM] + [ANY] * len(blocks) + [VMEM] * len(srcs + lines),
+        out_specs=[VMEM] + [ANY] * len(blocks + srcs) + [VMEM] * len(lines),
         scratch_shapes=[
             pltpu.VMEM((n_wt - 1, rows // n_wt, cols), F32),
             pair_sems(n_wt),
             pair_sems(n_wt),
         ]
         + [cube_sems(), pltpu.SemaphoreType.DMA] * len(blocks)
-        + [pair_sems(n_seq), pltpu.SemaphoreType.DMA] * len(srcs),
-        compiler_params=pltpu.CompilerParams(collective_id=ident, has_side_effects=True),
+        + [pair_sems(n_seq), pltpu.SemaphoreType.DMA] * len(srcs)
+        + [pair_sems(n_wt)] * len(lines),
+        compiler_params=pltpu.CompilerParams(
+            collective_id=ident, has_side_effects=True, vmem_limit_bytes=VMEM_BYTES
+        ),
         cost_estimate=pl.CostEstimate(flops=10**5, bytes_accessed=10**6, transcendentals=0),
-    )(part, *blocks, *srcs)
-
-
-def second_norm_kernel(part, tok, gain, out, res, recv, s_scatter, s_gather):
+    )(part, *blocks, *srcs, *lines)
+
+
+def second_norm_kernel(part, tok, gain, out, res, recv, pend, s_scatter, s_gather):
     me = lax.axis_index("wt")
     rows = recv.shape[1]
     greet(("wt",))
-    first = scatter_start(part, recv, s_scatter, "wt")
-    arrived(first)
+    first = line_scatter_start(part, recv, s_scatter)
+    first = line_scatter_mid(part, recv, pend, s_scatter, first)
+    line_scatter_end(first)
     row0 = me * rows
 
     def body(at):
-        r = tok[pl.ds(at, 16)] + summed(part, recv, at, 16, row0)
+        r = tok[pl.ds(at, 16)] + line_summed(part, recv, at, 16, row0)
         res[pl.ds(at, 16)] = r
         inverse = lax.rsqrt(jnp.mean(r * r, axis=-1, keepdims=True) + EPS)
         out[pl.ds(pl.multiple_of(row0 + at, 16), 16)] = (r * inverse * gain[...]).astype(BF16)
 
     step_rows(rows, 16, body)
-    second = gather_start(out, rows, s_gather, "wt")
-    arrived(second)
+    second = line_gather_start(out, rows, s_gather)
+    second = line_gather_mid(out, rows, s_gather, second)
+    line_gather_end(second)
     left(first)
     left(second)
 
@@ -432,10 +537,13 @@
         out_specs=[VMEM] * 2,
         scratch_shapes=[
             pltpu.VMEM((n_wt - 1, own, cols), BF16),
+            pltpu.VMEM((own, cols), BF16),
             pair_sems(n_wt),
             pair_sems(n_wt),
         ],
-        compiler_params=pltpu.CompilerParams(collective_id=ident, has_side_effects=True),
+        compiler_params=pltpu.CompilerParams(
+            collective_id=ident, has_side_effects=True, vmem_limit_bytes=VMEM_BYTES
+        ),
         cost_estimate=pl.CostEstimate(flops=10**6, bytes_accessed=10**8, transcendentals=0),
     )(part, tok_own, gain[None])
 
@@ -448,17 +556,25 @@
     return inverse * (scaled - normed * mean), grad * normed
 
 
-def second_back_kernel(part, res, cot, gain, out, d_res, gain_grad, recv, s_scatter, s_gather):
+def second_back_kernel(n_spread, part, res, cot, gain, *refs):
+    srcs, refs = refs[:n_spread], refs[n_spread:]
+    out, d_res, gain_grad = refs[:3]
+    dsts, refs = refs[3 : 3 + n_spread], refs[3 + n_spread :]
+    recv, pend, s_scatter, s_gather = refs[:4]
     me = lax.axis_index("wt")
     rows = recv.shape[1]
-    greet(("wt",))
-    first = scatter_start(part, recv, s_scatter, "wt")
+    greet(("wt", "seq") if n_spread else ("wt",))
+    first = line_scatter_start(part, recv, s_scatter)
+    spreads = [
+        spread(srcs[i], dsts[i], refs[4 + 2 * i], refs[5 + 2 * i]) for i in range(n_spread)
+    ]
     gain_grad[...] = jnp.zeros_like(gain_grad)
-    arrived(first)
+    first = line_scatter_mid(part, recv, pend, s_scatter, first)
+    line_scatter_end(first)
     row0 = me * rows
 
     def body(at):
-        grad = summed(part, recv, at, 16, row0)
+        grad = line_summed(part, recv, at, 16, row0)
         back, prod = norm_back_rows(grad, res[pl.ds(at, 16)], gain[...])
         gain_grad[...] += prod[:8] + prod[8:]
         d = cot[pl.ds(at, 16)] + back
@@ -466,42 +582,52 @@
         out[pl.ds(pl.multiple_of(row0 + at, 16), 16)] = d.astype(BF16)
 
     step_rows(rows, 16, body)
-    second = gather_start(out, rows, s_gather, "wt")
-    arrived(second)
+    second = line_gather_start(out, rows, s_gather)
+    second = line_gather_mid(out, rows, s_gather, second)
+    line_gather_end(second)
+    for sent, kept in spreads:
+        kept.wait()
+        arrived(sent)
+        left(sent)
     left(first)
     left(second)
 
 
-def second_back(part, res, cot_own, gain, n_wt, ident):
+def second_back(part, res, cot_own, gain, srcs, n_wt, n_seq, ident):
     rows, cols = part.shape
     own = rows // n_wt
     return pl.pallas_call(
-        second_back_kernel,
+        functools.partial(second_back_kernel, len(srcs)),
         out_shape=[
             jax.ShapeDtypeStruct((rows, cols), BF16),
             jax.ShapeDtypeStruct((own, cols), F32),
             jax.ShapeDtypeStruct((8, cols), F32),
-        ],
-        in_specs=[VMEM] * 4,
-        out_specs=[VMEM] * 3,
+        ]
+        + [jax.ShapeDtypeStruct((n_seq, rows, cols // n_seq), BF16)] * len(srcs),
+        in_specs=[VMEM] * (4 + len(srcs)),
+        out_specs=[VMEM] * 3 + [ANY] * len(srcs),
         scratch_shapes=[
             pltpu.VMEM((n_wt - 1, own, cols), BF16),
+            pltpu.VMEM((own, cols), BF16),
             pair_sems(n_wt),
             pair_sems(n_wt),
-        ],
-        compiler_params=pltpu.CompilerParams(collective_id=ident, has_side_effects=True),
+        ]
+        + [pair_sems(n_seq), pltpu.SemaphoreType.DMA] * len(srcs),
+        compiler_params=pltpu.CompilerParams(
+            collective_id=ident, has_side_effects=True, vmem_limit_bytes=VMEM_BYTES
+        ),
         cost_estimate=pl.CostEstimate(flops=10**6, bytes_accessed=10**8, transcendentals=0),
-    )(part, res, cot_own, gain[None])
+    )(part, res, cot_own, gain[None], *srcs)
 
 
 def last_kernel(cube, part, tok, d_res, gain, gain_grad2, sel, stp, taps, decays, bias3, *refs):
     blocks, refs = refs[:cube], refs[cube:]
     if cube:
-        cot_t, second_t, acts, refs = refs[0], refs[1], refs[2], refs[3:]
+        cot_t, second_t, branch_t, acts, refs = refs[0], refs[1], refs[2], refs[3], refs[4:]
     out, sel_out, stp_out, chan_out, gains_out = refs[:5]
     wholes, refs = refs[5 : 5 + cube], refs[5 + cube :]
     if cube:
-        grad_outs, refs = refs[:3], refs[3:]
+        grad_outs, refs = refs[:4], refs[4:]
         tile, s_tile, refs = refs[0], refs[1], refs[2:]
         width = tile.shape[2]
         tiles = acts.shape[1] // width
@@ -518,23 +644,24 @@
                 fetch(j + 1, 1 - slot).start()
 
             fetch(j, slot).wait()
-            columns = pl.ds(pl.multiple_of(j * UNITS, UNITS), UNITS)
-            for i, left_op in enumerate((cot_t, second_t, second_t)):
-                grad_outs[i][:, columns] = jnp.dot(
-                    left_op[...],
-                    tile[slot, :, i * UNITS : (i + 1) * UNITS],
-                    preferred_element_type=F32,
+            at = 0
+            for left_op, out_ref in zip((cot_t, second_t, second_t, branch_t), grad_outs):
+                wide = out_ref.shape[1] // tiles
+                out_ref[:, pl.ds(pl.multiple_of(j * wide, wide), wide)] = jnp.dot(
+                    left_op[...], tile[slot, :, at : at + wide], preferred_element_type=F32
                 )
+                at += wide
             return carry
 
         fetch(0, 0).start()
-    recv, recv_sel, recv_stp, recv_chan, pack, gain_buf, recv_gz, recv_gs = refs[:8]
-    s_scatter, s_gather, s_sel, s_stp, s_chan, s_cg, s_gz, s_gs = refs[8:16]
+    recv, pend, recv_sel, recv_stp, recv_chan, pack, gain_buf, recv_gz, recv_gs = refs[:9]
+    s_scatter, s_gather, s_sel, s_stp, s_chan, s_cg, s_gz, s_gs = refs[9:17]
+    refs = refs[17:]
     me, n_wt = lax.axis_index("wt"), lax.axis_size("wt")
     seq, n_seq = lax.axis_index("seq"), lax.axis_size("seq")
     rows = recv.shape[1]
     greet(("wt", "seq"))
-    first = scatter_start(part, recv, s_scatter, "wt")
+    first = line_scatter_start(part, recv, s_scatter)
     share = -(-(KC + NS + 3) // n_seq)
     lines = [(taps, i) for i in range(KC)] + [(decays, i) for i in range(NS)]
     lines += [(bias3, i) for i in range(3)]
@@ -547,11 +674,14 @@
             smalls.append(send(src.at[peer], dst.at[k - 1], sems, k - 1, "seq", peer))
     cubes = []
     for i in range(cube):
-        s_cube, s_own = refs[16 + 2 * i : 18 + 2 * i]
+        s_cube, s_own = refs[2 * i : 2 * i + 2]
         cubes.append([cube_first(blocks[i], wholes[i], s_cube), s_cube, wholes[i]])
         cubes[-1].append(keep(blocks[i], wholes[i], s_own))
     if cube:
-        lax.fori_loop(0, tiles // 2, one_tile, 0)
+        lax.fori_loop(0, 3, one_tile, 0)
+    first = line_scatter_mid(part, recv, pend, s_scatter, first)
+    if cube:
+        lax.fori_loop(3, tiles - 2, one_tile, 0)
     arrived(smalls)
     for src, recv_one, one_out in ((sel, recv_sel, sel_out), (stp, recv_stp, stp_out)):
         total = src[seq].astype(F32)
@@ -566,18 +696,18 @@
     chans = [
         send(mine, mine, s_cg, k - 1, "seq", lax.rem(seq + k, n_seq)) for k in range(1, n_seq)
     ]
-    arrived(first)
+    line_scatter_end(first)
     row0 = me * rows
     gain_buf[...] = jnp.zeros_like(gain_buf)
 
     def body(at):
-        grad = summed(part, recv, at, 16, row0)
+        grad = line_summed(part, recv, at, 16, row0)
         back, prod = norm_back_rows(grad, tok[pl.ds(at, 16)], gain[...])
         gain_buf[...] += prod[:8] + prod[8:]
         out[pl.ds(pl.multiple_of(row0 + at, 16), 16)] = (d_res[pl.ds(at, 16)] + back).astype(BF16)
 
     step_rows(rows, 16, body)
-    second = gather_start(out, rows, s_gather, "wt")
+    second = line_gather_start(out, rows, s_gather)
     high = recv_gz.shape[1] // 2
     for i, grad in enumerate((gain_buf, gain_grad2)):
         line = jnp.sum(grad[...], axis=0, keepdims=True)
@@ -587,7 +717,8 @@
     zs = [send(mine_z, mine_z, s_gz, k - 1, "wt", lax.rem(me + k, n_wt)) for k in range(1, n_wt)]
     cubes2 = [cube_second(whole, sems, one) for one, sems, whole, _ in cubes]
     if cube:
-        lax.fori_loop(tiles // 2, tiles, one_tile, 0)
+        lax.fori_loop(tiles - 2, tiles, one_tile, 0)
+    second = line_gather_mid(out, rows, s_gather, second)
     arrived(zs)
     total = recv_gz[0]
     for pos in range(1, n_wt):
@@ -607,7 +738,7 @@
     for (one, _, _, kept), two, three in zip(cubes, cubes2, cubes3):
         cube_end(one, two, three)
         kept.wait()
-    arrived(second)
+    line_gather_end(second)
     for group in (first, second, smalls, chans, zs, ss):
         left(group)
 
@@ -618,7 +749,8 @@
     chan = taps.shape[1]
     if more:
         deep, tok_all = more[0].shape
-        units = more[2].shape[1] // 3
+        units = (more[3].shape[1] - chan) // 3
+        span = more[3].shape[1] // (units // UNITS)
     return pl.pallas_call(
         functools.partial(last_kernel, len(blocks)),
         out_shape=[
@@ -629,16 +761,17 @@
             jax.ShapeDtypeStruct((2 * cols // 128, 128), F32),
         ]
         + [jax.ShapeDtypeStruct((n_seq,) + a.shape, BF16) for a in blocks]
-        + ([jax.ShapeDtypeStruct((deep, units), F32)] * 3 if more else []),
-        in_specs=[VMEM] * 10 + [ANY] * len(blocks) + ([VMEM, VMEM, ANY] if more else []),
-        out_specs=[VMEM] * 5 + [ANY] * len(blocks) + ([VMEM] * 3 if more else []),
+        + ([jax.ShapeDtypeStruct((deep, w), F32) for w in (units, units, units, chan)] if more else []),
+        in_specs=[VMEM] * 10 + [ANY] * len(blocks) + ([VMEM, VMEM, VMEM, ANY] if more else []),
+        out_specs=[VMEM] * 5 + [ANY] * len(blocks) + ([VMEM] * 4 if more else []),
         scratch_shapes=(
-            [pltpu.VMEM((2, tok_all, 3 * UNITS), BF16), pltpu.SemaphoreType.DMA((2,))]
+            [pltpu.VMEM((2, tok_all, span), BF16), pltpu.SemaphoreType.DMA((2,))]
             if more
             else []
         )
         + [
             pltpu.VMEM((n_wt - 1, own, cols), BF16),
+            pltpu.VMEM((own, cols), BF16),
             pltpu.VMEM((n_seq - 1,) + sel.shape[1:], BF16),
             pltpu.VMEM((n_seq - 1,) + stp.shape[1:], BF16),
             pltpu.VMEM((n_seq - 1, 8, chan), F32),
@@ -657,7 +790,7 @@
         ]
         + [cube_sems(), pltpu.SemaphoreType.DMA] * len(blocks),
         compiler_params=pltpu.CompilerParams(
-            collective_id=ident, has_side_effects=True, vmem_limit_bytes=40 * MIB
+            collective_id=ident, has_side_effects=True, vmem_limit_bytes=VMEM_BYTES
         ),
         cost_estimate=pl.CostEstimate(flops=10**6, bytes_accessed=10**8, transcendentals=0),
     )(part, tok_own, d_res, gain[None], gain_grad2, sel, stp, taps, decays, bias3, *blocks, *more)
@@ -708,7 +841,7 @@
             remote(mine, recv.at[k - 1], box, k - 1, "seq", peer).wait_send()
 
 
-def fwd_kernel(sa, dx, w, r, a2, y, h0, mine, recv, box):
+def fwd_kernel(sa, dx, wr, a2, y, h0, mine, recv, box):
     tok = sa.shape[0]
     greet(("seq",))
 
@@ -716,7 +849,7 @@
         s, d = sa[t], dx[t]
         h, total = carry
         return (
-            tuple(jnp.exp2(s * a2[n]) * h[n] + w[t, n] * d for n in range(NS)),
+            tuple(jnp.exp2(s * a2[n]) * h[n] + wr[n, t] * d for n in range(NS)),
             total + s,
         )
 
@@ -731,9 +864,9 @@
         s, d = sa[t], dx[t]
         new, sums = [], [None] * 4
         for n in range(NS):
-            hn = jnp.exp2(s * a2[n]) * h[n] + w[t, n] * d
+            hn = jnp.exp2(s * a2[n]) * h[n] + wr[n, t] * d
             new.append(hn)
-            c = r[t, n] * hn
+            c = wr[NS + n, t] * hn
             sums[n % 4] = c if sums[n % 4] is None else sums[n % 4] + c
         y[t] = (sums[0] + sums[1]) + (sums[2] + sums[3])
         return tuple(new)
@@ -742,7 +875,7 @@
     handed(mine, recv, box, False)
 
 
-def fwd_scan(sa, dx, w, r, a2, n_seq, ident):
+def fwd_scan(sa, dx, wr, a2, n_seq, ident):
     tok, high = sa.shape[:2]
     return pl.pallas_call(
         fwd_kernel,
@@ -750,7 +883,7 @@
             jax.ShapeDtypeStruct((tok, high, 128), F32),
             jax.ShapeDtypeStruct((NS, high, 128), F32),
         ],
-        in_specs=[VMEM, VMEM, SMEM, SMEM, VMEM],
+        in_specs=[VMEM, VMEM, SMEM, VMEM],
         out_specs=[VMEM] * 2,
         scratch_shapes=[
             pltpu.VMEM((NS + 1, high, 128), F32),
@@ -758,19 +891,21 @@
             pair_sems(n_seq),
         ],
         compiler_params=pltpu.CompilerParams(
-            collective_id=ident, has_side_effects=True, vmem_limit_bytes=32 * MIB
+            collective_id=ident, has_side_effects=True, vmem_limit_bytes=VMEM_BYTES
         ),
         cost_estimate=pl.CostEstimate(
             flops=10**8, bytes_accessed=8 * 10**7, transcendentals=2 * tok * NS * 1024
         ),
-    )(sa, dx, w, r, a2)
+    )(sa, dx, wr, a2)
 
 
 def bwd_kernel(
-    sa, dx, w, r, do, a2, h0, part, res,
-    along, ds2, grad_a, pw, pr, out,
-    hs, qw, qr, g0, mine, recv, recv_z, box, s_scatter, s_gather,
+    cube, sa, dx, wr, do, a2, h0, part, res, *refs
 ):
+    src, refs = refs[:cube], refs[cube:]
+    along, ds2, grad_a, sums, out = refs[:5]
+    dst, refs = refs[5 : 5 + cube], refs[5 + cube :]
+    hs, qw, qr, pw, pr, g0, mine, recv, recv_z, box, s_scatter = refs[:11]
     tok = sa.shape[0]
     chunk = qw.shape[0] // (NS * 8)
     greet(("wt", "seq"))
@@ -781,7 +916,7 @@
         s, d = sa[t], do[t]
         g, total = carry
         return (
-            tuple(jnp.exp2(s * a2[n]) * (g[n] + r[t, n] * d) for n in range(NS)),
+            tuple(jnp.exp2(s * a2[n]) * (g[n] + wr[NS + n, t] * d) for n in range(NS)),
             total + s,
         )
 
@@ -790,30 +925,25 @@
     store(mine, ends)
     mine[NS] = total
     hand_on(mine, recv, box, True)
+    if cube:
+        s_seq, s_wt, s_own = refs[11:]
+        sent, kept = share(src[0], dst[0], s_seq, s_own)
 
     def again(t, h):
         s, d = sa[t], dx[t]
         new = []
         for n in range(NS):
             hs[t, n] = h[n]
-            new.append(jnp.exp2(s * a2[n]) * h[n] + w[t, n] * d)
+            new.append(jnp.exp2(s * a2[n]) * h[n] + wr[n, t] * d)
         return tuple(new)
 
     lax.fori_loop(0, tok, again, load(h0), unroll=2)
 
-    arrived(first)
-    me = lax.axis_index("wt")
-    rows = recv_z.shape[1]
-    row0 = me * rows
-
-    def block_rows(at):
-        total = res[pl.ds(at, 16)] + summed(part, recv_z, at, 16, row0)
-        out[pl.ds(pl.multiple_of(row0 + at, 16), 16)] = total.astype(BF16)
-
-    step_rows(rows, 16, block_rows)
-    second = gather_start(out, rows, s_gather, "wt")
-
     fold(mine, box, recv, a2, g0, True)
+    if cube:
+        arrived(sent)
+        kept.wait()
+        passed = pass_along(dst[0], s_wt)
     grad_a[...] = jnp.zeros_like(grad_a)
 
     def one_chunk(j, g):
@@ -828,13 +958,13 @@
             for n in range(NS):
                 hp = hs[t, n]
                 f = jnp.exp2(s * a2[n])
-                hn = f * hp + w[t, n] * d
-                gn = r[t, n] * o + g[n]
+                hn = f * hp + wr[n, t] * d
+                gn = wr[NS + n, t] * o + g[n]
                 adj = f * gn
                 new.append(adj)
                 th = adj * hp
                 grad_a[n] += th * s
-                x = w[t, n] * gn
+                x = wr[n, t] * gn
                 al = x if al is None else al + x
                 x = a2[n] * th
                 d2 = x if d2 is None else d2 + x
@@ -852,54 +982,72 @@
                 acc = q[pl.ds(i * NS * 8, NS, stride=8), :]
                 for s in range(1, 8):
                     acc = acc + q[pl.ds(i * NS * 8 + s, NS, stride=8), :]
-                p[base + i] = acc
+                p[pl.ds(pl.multiple_of(i * NS, NS), NS), :] = acc
             return carry
 
         lax.fori_loop(0, chunk, lanes, 0, unroll=4)
+        ones = jnp.ones((8, 128), BF16)
+        for which, p in enumerate((pw, pr)):
+            high = p[...].astype(BF16)
+            low = (p[...] - high.astype(F32)).astype(BF16)
+            row = which * (tok // chunk) + base // chunk
+            sums[pl.ds(row, 1), :] = (nt(ones, high) + nt(ones, low))[:1]
         return g
 
     lax.fori_loop(0, tok // chunk, one_chunk, load(g0))
     handed(mine, recv, box, True)
-    arrived(second)
+    arrived(first)
+    rows = recv_z.shape[1]
+    row0 = lax.axis_index("wt") * rows
+
+    def block_rows(at):
+        out[pl.ds(at, 16)] = (res[pl.ds(at, 16)] + summed(part, recv_z, at, 16, row0)).astype(BF16)
+
+    step_rows(rows, 16, block_rows)
     left(first)
-    left(second)
-
-
-def bwd_scan(sa, dx, w, r, do, a2, h0, part, res, n_wt, n_seq, ident):
+    if cube:
+        arrived(passed)
+        left(sent)
+        left(passed)
+
+
+def bwd_scan(sa, dx, wr, do, a2, h0, part, res, src, n_wt, n_seq, ident):
     tok, high = sa.shape[:2]
     rows, cols = part.shape
     chunk = 32
     return pl.pallas_call(
-        bwd_kernel,
+        functools.partial(bwd_kernel, len(src)),
         out_shape=[
             jax.ShapeDtypeStruct((tok, high, 128), F32),
             jax.ShapeDtypeStruct((tok, high, 128), F32),
             jax.ShapeDtypeStruct((NS, high, 128), F32),
-            jax.ShapeDtypeStruct((tok, NS, 128), F32),
-            jax.ShapeDtypeStruct((tok, NS, 128), F32),
-            jax.ShapeDtypeStruct((rows, cols), BF16),
-        ],
-        in_specs=[VMEM, VMEM, SMEM, SMEM] + [VMEM] * 5,
-        out_specs=[VMEM] * 6,
+            jax.ShapeDtypeStruct((2 * tok // chunk, chunk * NS), F32),
+            jax.ShapeDtypeStruct((rows // n_wt, cols), BF16),
+        ]
+        + [jax.ShapeDtypeStruct((n_seq, n_wt, rows // n_wt, cols // n_seq), BF16)] * len(src),
+        in_specs=[VMEM, VMEM, SMEM] + [VMEM] * (5 + len(src)),
+        out_specs=[VMEM] * 5 + [ANY] * len(src),
         scratch_shapes=[
             pltpu.VMEM((tok, NS, high, 128), F32),
             pltpu.VMEM((chunk * NS * 8, 128), F32),
             pltpu.VMEM((chunk * NS * 8, 128), F32),
+            pltpu.VMEM((chunk * NS, 128), F32),
+            pltpu.VMEM((chunk * NS, 128), F32),
             pltpu.VMEM((NS, high, 128), F32),
             pltpu.VMEM((NS + 1, high, 128), F32),
             pltpu.VMEM((n_seq - 1, NS + 1, high, 128), F32),
             pltpu.VMEM((n_wt - 1, rows // n_wt, cols), BF16),
             pair_sems(n_seq),
             pair_sems(n_wt),
-            pair_sems(n_wt),
-        ],
+        ]
+        + [pair_sems(n_seq), pair_sems(n_wt), pltpu.SemaphoreType.DMA] * len(src),
         compiler_params=pltpu.CompilerParams(
-            collective_id=ident, has_side_effects=True, vmem_limit_bytes=56 * MIB
+            collective_id=ident, has_side_effects=True, vmem_limit_bytes=VMEM_BYTES
         ),
         cost_estimate=pl.CostEstimate(
             flops=10**8, bytes_accessed=15 * 10**7, transcendentals=3 * tok * NS * 1024
         ),
-    )(sa, dx, w, r, do, a2, h0, part, res)
+    )(sa, dx, wr, do, a2, h0, part, res, *src)
 
 
 def gather(block):
@@ -958,63 +1106,77 @@
     own = tok_count // n_wt
     cube = n_seq == 8 and n_seq * tok_count <= width
 
-    token_vals = tokens.astype(F32)
-    first_inv = lax.rsqrt(jnp.mean(token_vals * token_vals, axis=-1, keepdims=True) + EPS)
-    first_in = (token_vals * first_inv * premix_gain).astype(BF16)
     rows_sel, rows_step = select_proj.shape[0], step_proj.shape[0]
     if cube:
         fill = jnp.zeros((-(rows_sel + rows_step) % 32, chan), BF16)
         small = jnp.concatenate([select_proj, step_proj, fill], axis=0)
-        w_mixer, w_small, cot_f, first_f = first_gather(
+        w_mixer, w_small, cot_f, first_f, first_in = first_gather(
             jnp.concatenate([inner_proj, switch_proj, mixer_out], axis=1),
-            small, cotangent, first_in, n_wt, n_seq, 7,
+            small, cotangent, tokens, premix_gain, n_wt, n_seq, 7,
         )
         w_mixer = w_mixer.reshape(width, 3 * chan)
     else:
+        token_vals = tokens.astype(F32)
+        first_inv = lax.rsqrt(jnp.mean(token_vals * token_vals, axis=-1, keepdims=True) + EPS)
+        first_in = (token_vals * first_inv * premix_gain).astype(BF16)
         w_mixer = gather(jnp.concatenate([inner_proj, switch_proj, mixer_out], axis=1))
         w_small = lax.all_gather(jnp.concatenate([select_proj, step_proj], axis=0), "seq", axis=0)
+    ffn_own = jnp.concatenate([ffn_gate, ffn_up, ffn_down], axis=1)
+    ffn_own, w_small = lax.optimization_barrier((ffn_own, w_small))
+    w_all = gather(ffn_own)
     w_first, w_mix = w_mixer[:, : 2 * chan], w_mixer[:, 2 * chan :]
     w_select = w_small[:, :rows_sel].reshape(-1, chan)
     w_step = w_small[:, rows_sel : rows_sel + rows_step].reshape(-1, chan)
-    ffn_own = jnp.concatenate([ffn_gate, ffn_up, ffn_down], axis=1)
-    ffn_own, w_small = lax.optimization_barrier((ffn_own, w_small))
-    w_all = gather(ffn_own)
     both = contract(first_in, w_first, "td,dc->tc")
     inner_act = both[:, :chan].astype(BF16)
     switch = both[:, chan:]
 
-    counts = jnp.cumsum(doc_start)
-    last_count = counts[-1]
-    head_keep = (counts == 0).astype(F32)
-    tail_keep = (counts == last_count).astype(F32)
-    tail_rows = jnp.where(
-        tail_keep[-edge:, None] > 0, inner_act[-edge:], jnp.zeros_like(inner_act[-edge:])
+    goes_on = (1 - doc_start).astype(F32)
+    before = jnp.concatenate([jnp.ones((edge,), F32), goes_on])
+    after = jnp.concatenate([goes_on, jnp.ones((edge,), F32)])
+
+    def same_back(lag):
+        same = jnp.ones_like(goes_on)
+        for j in range(lag):
+            same = same * before[edge - j : edge - j + tok_count]
+        return same[:, None]
+
+    def same_ahead(lag):
+        same = jnp.ones_like(goes_on)
+        for j in range(1, lag + 1):
+            same = same * after[j : j + tok_count]
+        return same[:, None]
+
+    one = jnp.ones((edge - 1,), F32)
+    last_two, head = goes_on[-2:], goes_on[:edge]
+    tail_keep = jnp.concatenate([last_two, one[:1]]) * jnp.concatenate([last_two[1:], one])
+    head_keep = (
+        head
+        * jnp.concatenate([one[:1], head[:2]])
+        * jnp.concatenate([one, head[:1]])
     )
-    prev_rows = from_behind(tail_rows, "seq", 1)
+    prev_rows = from_behind(inner_act[-edge:] * tail_keep[:, None].astype(BF16), "seq", 1)
     extended = jnp.concatenate([prev_rows, inner_act], axis=0).astype(F32)
-    ext_counts = jnp.concatenate([jnp.zeros((edge,), jnp.int32), counts])
     conv_out = jnp.zeros((tok_count, chan), F32) + conv_bias[None, :]
     for offset in range(KC):
-        same_doc = (counts == ext_counts[edge - offset : edge - offset + tok_count]).astype(F32)
         conv_out = (
             conv_out
             + conv_taps[offset][None, :]
             * extended[edge - offset : edge - offset + tok_count]
-            * same_doc[:, None]
+            * same_back(offset)
         )
     mixed_in = jax.nn.silu(conv_out).astype(BF16)
     mixed_f = mixed_in.astype(F32)
-    (select,) = wt_sum(contract(w_select, mixed_in, "jc,tc->jt"), (), (), n_wt, n_seq, 0)
+    (select,) = wt_sum(contract(w_select, mixed_in, "jc,tc->jt"), (), (), (), n_wt, n_seq, 0)
     low_rank = select[:R].astype(BF16)
-    write_vec = select[R : R + NS].T
-    read_vec = select[R + NS :].T
+    write_read = select[R:]
     step_pre = contract(low_rank, w_step, "rt,rc->tc") + step_bias[None, :]
     step_size = jax.nn.softplus(step_pre)
     decay = -jnp.exp(decay_log)
     decay2 = tiles(decay * LOG2E)
     step_a = tiles(jnp.where(doc_start[:, None] > 0, FAR, step_size))
     drive = tiles(step_size * mixed_f)
-    scan_out, carried_in = fwd_scan(step_a, drive, write_vec, read_vec, decay2, n_seq, 1)
+    scan_out, carried_in = fwd_scan(step_a, drive, write_read, decay2, n_seq, 1)
 
     scanned = flat(scan_out) + skip_gain[None, :] * mixed_f
     switch_act = jax.nn.silu(switch)
@@ -1023,17 +1185,22 @@
     tokens_own = lax.dynamic_slice_in_dim(tokens, z * own, own, 0).astype(F32)
     cot_own = lax.dynamic_slice_in_dim(cotangent, z * own, own, 0).astype(F32)
     second_in, residual = second_norm(mix_part, tokens_own, preffn_gain, n_wt, 2)
-    acts, down_part, d_second = ffn(second_in, cotangent, w_all)
-    d_branch, d_residual, grad_preffn = second_back(
-        d_second, residual, cot_own, preffn_gain, n_wt, 3
+    if cube:
+        line_up = lambda v: v.reshape(n_seq * tok_count, v.shape[-1])
+        second_in, cot_own, head_keep, cot_t, first_t = lax.optimization_barrier(
+            (second_in, cot_own, head_keep, line_up(cot_f).T, line_up(first_f).T)
+        )
+    acts, down_part, d_second = ffn(second_in, cotangent, w_all, gated)
+    d_branch, d_residual, grad_preffn, *second_all = second_back(
+        d_second, residual, cot_own, preffn_gain, (second_in,) if cube else (), n_wt, n_seq, 3
     )
     d_gated = contract(d_branch, w_mix, "td,dc->tc")
     d_scanned = d_gated * switch_act
     d_switch = (d_gated * scanned * silu_slope(switch)).astype(BF16)
     grad_skip = jnp.sum(d_scanned * mixed_f, axis=0)
-    along, through_sum, grad_decay, write_lanes, read_lanes, block_out = bwd_scan(
-        step_a, drive, write_vec, read_vec, tiles(d_scanned), decay2, carried_in,
-        down_part, residual, n_wt, n_seq, 4,
+    along, through_sum, grad_decay, d_write_read, block_own, *branch_all = bwd_scan(
+        step_a, drive, write_read, tiles(d_scanned), decay2, carried_in,
+        down_part, residual, (d_branch,) if cube else (), n_wt, n_seq, 4,
     )
     along = flat(along)
     d_step = along * mixed_f + flat(through_sum) * (1.0 / LOG2E)
@@ -1045,17 +1212,17 @@
         v.reshape(n_seq, -1, tok_count), ((0, 0), (0, -(v.shape[0] // n_seq) % 16), (0, 0))
     ).reshape(-1, tok_count)
     grad_step = contract(pad_rows(low_rank), d_pre_low, "rt,tc->rc").astype(BF16)
-    d_select, *gathered = wt_sum(
+    d_select, *gathered, block_out = wt_sum(
         jnp.concatenate(
             [
                 contract(w_step, d_pre_low, "rc,tc->rt"),
-                jnp.sum(write_lanes, axis=-1).T,
-                jnp.sum(read_lanes, axis=-1).T,
+                d_write_read.reshape(2, tok_count, NS).swapaxes(1, 2).reshape(2 * NS, tok_count),
             ],
             axis=0,
         ),
-        (gated,) if cube else (),
-        (second_in, d_branch) if cube else (),
+        (d_switch,) if cube else (),
+        (),
+        (block_own,),
         n_wt,
         n_seq,
         5,
@@ -1070,26 +1237,24 @@
     d_conv = (d_mixed * silu_slope(conv_out)).astype(BF16)
     d_conv_f = d_conv.astype(F32)
     grad_conv_bias = jnp.sum(d_conv_f, axis=0)
-    head_rows = jnp.where(head_keep[:edge, None] > 0, d_conv[:edge], jnp.zeros_like(d_conv[:edge]))
-    next_rows = from_behind(head_rows, "seq", -1)
+    next_rows = from_behind(d_conv[:edge] * head_keep[:, None].astype(BF16), "seq", -1)
     ext_grad = jnp.concatenate([d_conv, next_rows], axis=0).astype(F32)
-    ext_after = jnp.concatenate([counts, jnp.zeros((edge,), jnp.int32) + last_count])
     d_inner = jnp.zeros_like(d_conv_f)
     taps_rows = []
     for offset in range(KC):
-        same_doc = (counts == ext_counts[edge - offset : edge - offset + tok_count]).astype(F32)
         taps_rows.append(
             jnp.sum(
-                d_conv_f * extended[edge - offset : edge - offset + tok_count] * same_doc[:, None],
+                d_conv_f
+                * extended[edge - offset : edge - offset + tok_count]
+                * same_back(offset),
                 axis=0,
             )
         )
-        later_same = (ext_after[offset : offset + tok_count] == counts).astype(F32)
         d_inner = (
             d_inner
             + conv_taps[offset][None, :]
             * ext_grad[offset : offset + tok_count]
-            * later_same[:, None]
+            * same_ahead(offset)
         )
     d_inner_low = d_inner.astype(BF16)
     d_first = contract(
@@ -1097,30 +1262,29 @@
     ).astype(BF16)
     more = ()
     if cube:
-        line_up = lambda v: v.reshape(n_seq * tok_count, v.shape[-1])
-        gated_all, second_f, branch_f = map(line_up, gathered)
-        more = (line_up(cot_f).T, second_f.T, gather(acts))
+        (switch_all,) = map(line_up, gathered)
+        more = (cot_t, line_up(second_all[0]).T, line_up(branch_all[0]).T, gather(acts))
     tokens_grad, out_select, out_step, by_chan, gains, *others = last(
         d_first, tokens_own, d_residual, premix_gain, grad_preffn,
         grad_select.reshape(n_seq, -1, chan), grad_step.reshape(n_seq, -1, chan),
         jnp.stack(taps_rows, axis=0), grad_decay_log,
         jnp.stack([grad_conv_bias, grad_step_bias, grad_skip]),
-        (d_switch, d_inner_low) if cube else (), more, n_wt, n_seq, 6,
+        (d_inner_low,) if cube else (), more, n_wt, n_seq, 6,
     )
     share = -(-(KC + NS + 3) // n_seq)
     by_chan = by_chan[:, :share].reshape(n_seq * share, chan)
     gains = gains.reshape(2, width)
     if cube:
-        out_down, out_gate, out_up = others[2:]
-        out_mix, out_switch, out_inner = grads(
-            (branch_f.T, line_up(first_f).T),
-            (0, 1, 1),
-            (gated_all, line_up(others[0]), line_up(others[1])),
+        out_down, out_gate, out_up, out_mix = others[1:]
+        out_switch, out_inner = grads(
+            (first_t,), (0, 0), (switch_all, line_up(others[0]))
         )
     else:
         scatter = lambda v: lax.psum_scatter(v, "seq", scatter_dimension=0, tiled=True)
-        by_unit = acts.reshape(tok_count, -1, 3, UNITS)
-        hidden, d_gate, d_up = [by_unit[:, :, i].reshape(tok_count, units) for i in range(3)]
+        by_unit = acts.reshape(tok_count, units // UNITS, -1)
+        hidden, d_gate, d_up = [
+            by_unit[:, :, i * UNITS : (i + 1) * UNITS].reshape(tok_count, units) for i in range(3)
+        ]
         out_down = scatter(contract(cotangent, hidden, "td,tf->df"))
         out_gate = scatter(contract(second_in, d_gate, "td,tf->df"))
         out_up = scatter(contract(second_in, d_up, "td,tf->df"))

time: 544 us -> 504 us (0.926)
  Pallas kernels: 399 us -> 381 us
  local copies, waits for them, and re-layouts: 45.9 us -> 31.7 us
    unnamed x154 -> x91, local copies, waits for them, and re-layouts: 30.4 us -> 14.1 us
    pallas_call x4, Pallas kernels: 175 us -> 165 us  [the longest x2 67.9 us: wt_sum(): pl.pallas_call(functools.partial(wt_sum_kernel, len(blocks), len(srcs), l...]
    pallas_call x1, Pallas kernels: 58.3 us -> 50.5 us  [last(): pl.pallas_call(functools.partial(last_kernel, len(blocks)), out_shape=[ja...]
    pallas_call x1, Pallas kernels: 46.9 us -> 40.5 us  [second_norm(): pl.pallas_call(second_norm_kernel, out_shape=[jax.ShapeDtypeStruct((rows,...]
    reduce_sum x3 -> x0, other arithmetic: 6.22 us -> none  [the longest x1 2.39 us: local(): jnp.sum(read_lanes, axis=-1)]
  transfers between devices with their start and end apart: 4 -> 4, of which waited for: 1 -> 1; matrix products, arithmetic and copies ran while one was open for 12% -> 13% of each run, Pallas kernels for 44% -> 45%
where the time goes in v3:
time: 504 us; the launch traced here: 503 us
  Pallas kernels  381 us (76%)
  matrix products  33.1 us (7%)
  local copies, waits for them, and re-layouts  31.7 us (6%)
  other arithmetic  23 us (5%)
  waiting for transfers between devices  15 us (3%)
  between operations  14.6 us (3%)
    pallas_call x1, Pallas kernels, first_gather(): pl.pallas_call(first_kernel, out_shape=[jax.ShapeDtypeStruct((n_seq,) + m...  77.9 us
    pallas_call x2, Pallas kernels, wt_sum(): pl.pallas_call(functools.partial(wt_sum_kernel, len(blocks), len(srcs), l...  67.9 us
    pallas_call x1, Pallas kernels, last(): pl.pallas_call(functools.partial(last_kernel, len(blocks)), out_shape=[ja...  50.5 us
    pallas_call x1, Pallas kernels, second_back(): pl.pallas_call(functools.partial(second_back_kernel, len(srcs)), out_shap...  49 us
    pallas_call x1, Pallas kernels, bwd_scan(): pl.pallas_call(functools.partial(bwd_kernel, len(src)), out_shape=[jax.Sh...  48.1 us
    pallas_call x1, Pallas kernels, second_norm(): pl.pallas_call(second_norm_kernel, out_shape=[jax.ShapeDtypeStruct((rows,...  40.5 us
    dot_general x10, matrix products, contract(): return jnp.einsum(pattern, left_op, right_op, preferred_element_type=F32)  33.1 us
    pallas_call x1, Pallas kernels, ffn(): pl.pallas_call(ffn_kernel, grid=(steps,), in_specs=[whole, whole, tile(0)...  20.7 us
  transfers between devices with their start and end apart: 4, of which 1 were waited for; matrix products, arithmetic and copies ran while one was open for 13% of the time, Pallas kernels for 45%

profile of v3, /device:TPU:0, one launch (start us, length us, event | category | flops | bytes accessed | tf_op | source)
XLA Modules:
  0.0 502.6 jit_solution(13680195791411773237)
XLA Ops:
  7.4 2.8 pad_maximum_fusion.1.mixer
  10.1 0.7 maximum_maximum_fusion.small
  10.9 1.7 pad_maximum_fusion
  12.6 77.9 %shard_map.305 = (bf16[8,256,3072]{2,1,0:T(8,128)(2,1)}, bf16[8,64,1024]{2,1,0:T(8,128)(2,1)}, bf16[8,4,64,256]{3,2,1,0:T(8,128)(2,1)}, bf16[8,4,64,256]{3,2,1,0:T(8,128)(2,1)}, bf16[256,2048]{1,0:T(8,128)(2,1)}) custom-call(bf16[256,3072]{1,0:T(8,128)(2,1)} %pad_maximum_fusion.1.mixer, bf16[64,1024]{1,0:T(8,128)(2,1)} %maximum_maximum_fusion.small, ...), custom_call_target="tpu_custom_call" | custom-call | flops 1000000 | bytes 100000000 | tf_op jit(solution)/shard_map/pallas_call | solution.py:320
  91.3 0.7 fusion.48
  92.0 7.1 %fusion.60 = (bf16[256,2048]{1,0:T(8,128)(2,1)S(1)}, f32[256,2048]{1,0:T(8,128)}) fusion(bf16[256,2048]{1,0:T(8,128)(2,1)S(1)} %copy-done.39, bf16[2048,3072]{1,0:T(8,128)(2,1)} %bitcast.137), kind=kOutput, calls=%fused_computation.106 | convolution fusion | flops 2148007936 | bytes 12582912 | tf_op jit(solution)/shard_map/td,dc->tc/dot_general | solution.py:1064
  99.2 2.4 collective-permute-start
  101.6 0.6 fusion.47
  102.3 2.2 dynamic-slice_convert_fusion
  104.6 1.2 fusion.49
  105.8 1.0 slice.147
  106.9 1.1 slice.146
  108.0 0.7 copy.48
  108.7 1.4 copy.41
  110.4 1.8 multiply_convert_fusion.2
  112.2 1.0 fusion.61.part
  113.1 1.4 copy.40
  114.6 13.8 %shard_map.306 = f32[160,256]{1,0:T(8,128)} custom-call(f32[160,256]{1,0:T(8,128)} %fusion.61.part), custom_call_target="tpu_custom_call" | custom-call | flops 100000 | bytes 1000000 | tf_op jit(solution)/shard_map/pallas_call | solution.py:481
  128.3 1.4 slice.164.wr
  129.7 1.2 convolution_add_fusion.1
  130.9 0.7 fusion.16
  131.6 1.2 copy.46
  132.8 1.2 copy.47
  134.0 19.6 %shard_map.307 = (f32[256,8,128]{2,1,0:T(8,128)}, f32[16,8,128]{2,1,0:T(8,128)}) custom-call(f32[256,8,128]{2,1,0:T(8,128)} %bitcast.103, f32[256,8,128]{2,1,0:T(8,128)} %bitcast.105, f32[32,256]{1,0:T(8,128)} %slice.164.wr, f32[16,8,128]{2,1,0:T(8,128)} %bitcast.113), custom_call_target="tpu_custom_call" | custom-call | flops 100000000 | bytes 80000000 | tf_op jit(solution)/shard_map/pallas_call | solution.py:880
  153.5 2.1 multiply_convert_fusion.1.gated
  155.6 4.6 fusion.8.part
  160.3 40.5 %shard_map.308 = (bf16[256,2048]{1,0:T(8,128)(2,1)}, f32[64,2048]{1,0:T(8,128)}) custom-call(bf16[256,2048]{1,0:T(8,128)(2,1)} %fusion.8.part, f32[64,2048]{1,0:T(8,128)} %get-tuple-element.143.tok, f32[1,2048]{1,0:T(1,128)} %bitcast.123), custom_call_target="tpu_custom_call" | custom-call | flops 1000000 | bytes 100000000 | tf_op jit(solution)/shard_map/pallas_call | solution.py:530
  200.7 15.0 %all-gather.3.cloned.1.call-done.wg.wu.wd = bf16[2048,6144]{1,0:T(8,128)(2,1)} async-done(((bf16[256,6144]{1,0:T(8,128)(2,1)}), bf16[2048,6144]{1,0:T(8,128)(2,1)}) %all-gather.3.cloned.1.call-update) | async-done | bytes 25165840 | tf_op jit(solution)/shard_map/all_gather | solution.py:1054
  215.7 20.7 %shard_map.309 = (bf16[256,7168]{1,0:T(8,128)(2,1)}, bf16[256,2048]{1,0:T(8,128)(2,1)}, bf16[256,2048]{1,0:T(8,128)(2,1)}) custom-call(bf16[256,2048]{1,0:T(8,128)(2,1)} %get-tuple-element.69.x.refs_0_, bf16[256,2048]{1,0:T(8,128)(2,1)} %c.1, bf16[2048,6144]{1,0:T(8,128)(2,1)} %all-gather.3.cloned.1.call-done.wg.wu.wd, ...), custom_call_target="tpu_custom_call" | custom-call | flops 12884901888 | bytes 25165824 | tf_op jit(solution)/shard_map/pallas_call | solution.py:392
  236.4 49.0 %shard_map.310 = (bf16[256,2048]{1,0:T(8,128)(2,1)}, f32[64,2048]{1,0:T(8,128)}, f32[8,2048]{1,0:T(8,128)}, bf16[8,256,256]{2,1,0:T(8,128)(2,1)}) custom-call(bf16[256,2048]{1,0:T(8,128)(2,1)} %get-tuple-element.71.part, f32[64,2048]{1,0:T(8,128)} %get-tuple-element.72.res, f32[64,2048]{1,0:T(8,128)} %get-tuple-element.73.cot, f32[1,2048]{1,0:T(1,128)} %bitcast.124, ...), custom_call_target="tpu_custom_call" | custom-call | flops 1000000 | bytes 100000000 | tf_op jit(solution)/shard_map/pallas_call | solution.py:599
  285.4 6.2 %fusion.20 = (f32[1024]{0:T(1024)}, f32[256,1024]{1,0:T(8,128)S(1)}, bf16[256,1024]{1,0:T(8,128)(2,1)}) fusion(bf16[256,1024]{1,0:T(8,128)(2,1)S(1)} %get-tuple-element.116, f32[256,2048]{1,0:T(8,128)} %get-tuple-element.140, f32[1024]{0:T(1024)S(1)} %copy-done.30, f32[32,8,8,128]{3,2,1,0:T(8,128)} %bitcast.108, ...), kind=kOutput, calls=%fused_computation.32 | convolution fusion | flops 1078197248 | bytes 9445376 | tf_op jit(solution)/shard_map/td,dc->tc/dot_general | solution.py:1064
  291.7 1.0 copy-done.11
  292.6 1.2 copy.50
  293.8 48.1 %shard_map.311 = (f32[256,8,128]{2,1,0:T(8,128)}, f32[256,8,128]{2,1,0:T(8,128)}, f32[16,8,128]{2,1,0:T(8,128)}, f32[16,512]{1,0:T(8,128)}, bf16[64,2048]{1,0:T(8,128)(2,1)}, /*index=5*/bf16[8,4,64,256]{3,2,1,0:T(8,128)(2,1)}) custom-call(f32[256,8,128]{2,1,0:T(8,128)} %bitcast.104, f32[256,8,128]{2,1,0:T(8,128)} %bitcast.106, f32[32,256]{1,0:T(8,128)} %slice.164.wr, ...), custom_call_target="tpu_custom_call" | custom-call | flops 100000000 | bytes 150000000 | tf_op jit(solution)/shard_map/pallas_call | solution.py:1018
  342.0 0.9 reshape.139
  342.9 1.3 broadcast_multiply_fusion
  344.3 2.5 fusion.51
  347.1 0.7 pad_maximum_fusion.2.part
  347.8 54.1 %shard_map.312 = (f32[160,256]{1,0:T(8,128)}, bf16[8,256,1024]{2,1,0:T(8,128)(2,1)}, bf16[256,2048]{1,0:T(8,128)(2,1)}) custom-call(f32[160,256]{1,0:T(8,128)} %pad_maximum_fusion.2.part, bf16[256,1024]{1,0:T(8,128)(2,1)} %get-tuple-element.120.refs_0_, bf16[64,2048]{1,0:T(8,128)(2,1)} %get-tuple-element.80.refs_1_), custom_call_target="tpu_custom_call" | custom-call | flops 100000 | bytes 1000000 | tf_op jit(solution)/shard_map/pallas_call | solution.py:481
  401.9 0.9 convert_element_type.77
  403.0 3.7 fusion.21
  406.8 1.6 collective-permute-start.1
  409.0 0.7 bitcast_multiply_fusion.1.decays
  409.7 0.9 convolution_convert_fusion.1
  410.6 1.1 convolution_convert_fusion
  411.8 0.6 pad_maximum_fusion.3.taps
  412.4 2.3 copy.44
  414.7 1.4 copy.45
  416.2 0.6 fusion.31.refs_0_
  417.1 6.9 %fusion.11.part = bf16[256,2048]{1,0:T(8,128)(2,1)} fusion(bf16[2048,3072]{1,0:T(8,128)(2,1)} %bitcast.140, bf16[256,1024]{1,0:T(8,128)(2,1)S(1)} %copy-done.19, bf16[256,1024]{1,0:T(8,128)(2,1)S(1)} %fusion.31.refs_0_), kind=kOutput, calls=%fused_computation.11 | convolution fusion | flops 2150105088 | bytes 10485760 | tf_op jit(solution)/shard_map/tc,dc->td/dot_general | solution.py:1064
  424.0 50.5 %shard_map.313 = (bf16[256,2048]{1,0:T(8,128)(2,1)}, f32[32,1024]{1,0:T(8,128)}, f32[16,1024]{1,0:T(8,128)}, f32[8,8,1024]{2,1,0:T(8,128)}, f32[32,128]{1,0:T(8,...) custom-call(bf16[256,2048]{1,0:T(8,128)(2,1)} %fusion.11.part, ...), custom_call_target="tpu_custom_call" | custom-call | flops 1000000 | bytes 100000000 | tf_op jit(solution)/shard_map/pallas_call | solution.py:754
  474.5 1.0 slice.179
  475.5 0.6 slice.205
  477.4 1.5 slice.182
  478.9 1.3 slice_bitcast_fusion
  480.2 7.0 %shard_map.314 = (f32[256,1024]{1,0:T(8,128)}, f32[256,1024]{1,0:T(8,128)}) custom-call(bf16[256,2048]{1,0:T(8,128)(2,1)} %bitcast.84, bf16[2048,1024]{1,0:T(8,128)(2,1)} %bitcast.89, bf16[2048,1024]{1,0:T(8,128)(2,1)} %bitcast.90), custom_call_target="tpu_custom_call" | custom-call | flops 2147483648 | bytes 8388608 | tf_op jit(solution)/shard_map/pallas_call | solution.py:421
  487.2 1.0 copy.72
  488.2 1.0 copy.73
  489.2 0.6 copy.74
  489.8 1.0 copy.75
  490.8 1.3 copy.76
  492.1 1.3 copy.77
  493.4 1.0 copy-done.2
  494.5 1.3 copy.78
  (107 shorter events, 4.2 us)
Async XLA Ops:
  7.2 2.9 copy-start.23
  7.2 2.9 copy-start.24
  7.2 3.7 copy-start.16
  7.2 3.7 copy-start.15
  7.2 3.7 copy-start.14
  7.2 208.5 %all-gather.3.cloned.1.call-start = ((), (), s32[]{:S(2)}) async-start(), calls=%async_computation | async-start | bytes 28311552 | tf_op jit(solution)/shard_map/all_gather | solution.py:1054
  12.6 78.0 %copy-start.38 = (s32[256]{0:T(256)S(1)}, s32[256]{0:T(256)}, u32[]{:S(2)}) copy-start(s32[256]{0:T(256)} %param.20) | copy-start | bytes 3076
  90.5 1.5 copy-start.39
  90.6 333.5 %all-gather.5.cloned.1.call-start = ((), (), s32[]{:S(2)}) async-start(), calls=%async_computation.1 | async-start | bytes 33030144 | tf_op jit(solution)/shard_map/all_gather | solution.py:1054
  90.6 19.7 %copy-start.25 = (f32[256]{0:T(256)}, f32[256]{0:T(256)S(1)}, u32[]{:S(2)}) copy-start(f32[256]{0:T(256)S(1)} %subtract_convert_fusion) | copy-start | bytes 3076
  92.0 10.2 %copy-start.27 = (f32[4,1024]{1,0:T(4,128)S(1)}, f32[4,1024]{1,0:T(4,128)}, u32[]{:S(2)}) copy-start(f32[4,1024]{1,0:T(4,128)} %param.24) | copy-start | bytes 49156
  92.0 10.3 %copy-start.20 = (f32[16,1024]{1,0:T(8,128)S(1)}, f32[16,1024]{1,0:T(8,128)}, u32[]{:S(2)}) copy-start(f32[16,1024]{1,0:T(8,128)} %param.29) | copy-start | bytes 196612
  99.1 9.6 %copy-start.10 = (bf16[8,4,64,256]{3,2,1,0:T(8,128)(2,1)S(1)}, bf16[8,4,64,256]{3,2,1,0:T(8,128)(2,1)}, u32[]{:S(2)}) copy-start(bf16[8,4,64,256]{3,2,1,0:T(8,128)(2,1)} %get-tuple-element.68) | copy-start | bytes 3145732
  99.2 11.0 %collective-permute-start = (bf16[3,1024]{1,0:T(4,128)(2,1)S(1)}, bf16[3,1024]{1,0:T(4,128)(2,1)S(1)}, u32[]{:S(2)}, u32[]{:S(2)}) collective-permute-start(bf16[3,1024]{1,0:T(4,128)(2,1)S(1)} %slice_multiply_fusion.5), channel_id=1, source_target_pairs={{0,4},{4,8},{8,12},{12,16},{16,20},{20,24},{24,28},{1,5},{5,9},{9,... | collective-permute-start | bytes 18440 | tf_op jit(solution)/shard_map/ppermute | solution.py:1060
  102.3 8.1 %copy-start.34 = (f32[256]{0:T(256)}, f32[256]{0:T(256)S(1)}, u32[]{:S(2)}) copy-start(f32[256]{0:T(256)S(1)} %get-tuple-element.133) | copy-start | bytes 3076
  102.3 8.1 %copy-start.35 = (f32[256]{0:T(256)}, f32[256]{0:T(256)S(1)}, u32[]{:S(2)}) copy-start(f32[256]{0:T(256)S(1)} %get-tuple-element.134) | copy-start | bytes 3076
  105.8 4.5 copy-start.28
  108.0 4.1 copy-start.5
  110.3 2.8 copy-start.9
  112.1 17.6 %copy-start.29 = (f32[1024]{0:T(1024)S(1)}, f32[1024]{0:T(1024)}, u32[]{:S(2)}) copy-start(f32[1024]{0:T(1024)} %param.28) | copy-start | bytes 12292
  133.9 19.6 %copy-start.30 = (f32[1024]{0:T(1024)S(1)}, f32[1024]{0:T(1024)}, u32[]{:S(2)}) copy-start(f32[1024]{0:T(1024)} %param.30) | copy-start | bytes 12292
  155.6 4.6 copy-start.1
  291.7 1.0 copy-start.11
  402.9 3.8 copy-start.37
  402.9 5.5 %copy-start.26 = (f32[1024]{0:T(1024)S(1)}, f32[1024]{0:T(1024)}, u32[]{:S(2)}) copy-start(f32[1024]{0:T(1024)} %get-tuple-element.110) | copy-start | bytes 12292
  402.9 5.5 %copy-start.36 = (f32[1024]{0:T(1024)S(1)}, f32[1024]{0:T(1024)}, u32[]{:S(2)}) copy-start(f32[1024]{0:T(1024)} %get-tuple-element.112) | copy-start | bytes 12292
  403.0 6.1 %copy-start.21 = (f32[16,8,128]{2,1,0:T(8,128)S(1)}, f32[16,8,128]{2,1,0:T(8,128)}, u32[]{:S(2)}) copy-start(f32[16,8,128]{2,1,0:T(8,128)} %get-tuple-element.86) | copy-start | bytes 196612
  403.0 6.7 %copy-start.6 = (f32[160,256]{1,0:T(8,128)S(1)}, f32[160,256]{1,0:T(8,128)}, u32[]{:S(2)}) copy-start(f32[160,256]{1,0:T(8,128)} %shard_map.306) | copy-start | bytes 491524
  406.6 5.1 %copy-start.17 = (bf16[256,1024]{1,0:T(8,128)(2,1)}, bf16[256,1024]{1,0:T(8,128)(2,1)S(1)}, u32[]{:S(2)}) copy-start(bf16[256,1024]{1,0:T(8,128)(2,1)S(1)} %get-tuple-element.141) | copy-start | bytes 1572868
  406.7 8.0 %copy-start.8 = (bf16[8,256,256]{2,1,0:T(8,128)(2,1)S(1)}, bf16[8,256,256]{2,1,0:T(8,128)(2,1)}, u32[]{:S(2)}) copy-start(bf16[8,256,256]{2,1,0:T(8,128)(2,1)} %get-tuple-element.88) | copy-start | bytes 3145732
  406.8 9.3 %collective-permute-start.1 = (bf16[3,1024]{1,0:T(4,128)(2,1)S(1)}, bf16[3,1024]{1,0:T(4,128)(2,1)S(1)}, u32[]{:S(2)}, u32[]{:S(2)}) collective-permute-start(bf16[3,1024]{1,0:T(4,128)(2,1)S(1)} %slice_multiply_fusion.4), channel_id=1, source_target_pairs={{4,0},{8,4},{12,8},{16,12},{20,16},{24,20},{28,24},{5,1},{9,5},{13... | collective-permute-start | bytes 18440 | tf_op jit(solution)/shard_map/ppermute | solution.py:1060
  411.7 4.5 copy-start.31
  411.7 4.5 copy-start.32
  411.7 4.5 copy-start.33
  411.8 4.3 copy-start.18
  416.1 1.0 copy-start.19
  417.1 6.9 %copy-start = (bf16[256,1024]{1,0:T(8,128)(2,1)}, bf16[256,1024]{1,0:T(8,128)(2,1)S(1)}, u32[]{:S(2)}) copy-start(bf16[256,1024]{1,0:T(8,128)(2,1)S(1)} %fusion.31.refs_0_) | copy-start | bytes 1572868
  480.2 7.0 %copy-start.7 = (bf16[256,2048]{1,0:T(8,128)(2,1)S(1)}, bf16[256,2048]{1,0:T(8,128)(2,1)}, u32[]{:S(2)}) copy-start(bf16[256,2048]{1,0:T(8,128)(2,1)} %get-tuple-element.163) | copy-start | bytes 3145732
  480.2 8.0 %copy-start.13 = (bf16[256,2048]{1,0:T(8,128)(2,1)S(1)}, bf16[256,2048]{1,0:T(8,128)(2,1)}, u32[]{:S(2)}) copy-start(bf16[256,2048]{1,0:T(8,128)(2,1)} %get-tuple-element.164) | copy-start | bytes 3145732
  487.2 2.0 copy-start.22
  487.2 2.6 copy-start.12
  487.2 3.6 copy-start.4
  489.8 2.3 copy-start.3
  492.1 2.3 copy-start.2
Sparse Core Ops, SparseCore 0:
  90.7 125.0 all-gather.2
  236.6 174.7 all-gather.4

commit v4 on v3

--- a/solution.py
+++ b/solution.py
@@ -20,6 +20,15 @@
 SMEM = pl.BlockSpec(memory_space=pltpu.SMEM)
 ANY = pl.BlockSpec(memory_space=pl.ANY)
 VMEM_BYTES = 60 * 2**20
+
+
+UNITS = 256
+
+
+def nt(left_op, right_op):
+    return lax.dot_general(
+        left_op, right_op, (((1,), (1,)), ((), ())), preferred_element_type=F32
+    )
 
 
 def greet(axes):
@@ -280,22 +289,28 @@
 
 
 def first_kernel(
-    mixer, small, cot, tok, gain, w_mixer, w_small, cot_f, act_f, act,
-    s_big, s_small, s_own, s_cot, s_act, s_cz, s_az,
+    pair, small, cot, tok, gain, taps, bias, masks,
+    w_first, cot_f, act_f, w_small, inner, prev, switch, conv, mixed, select,
+    first_in, w_near, ext, halo, part, recv,
+    s_pair, s_small, s_own, s_cot, s_act, s_cz, s_az, s_halo, s_scatter, s_gather,
 ):
-    kept = [keep(mixer, w_mixer, s_own.at[0]), keep(small, w_small, s_own.at[1])]
+    seq, n_seq = lax.axis_index("seq"), lax.axis_size("seq")
+    me = lax.axis_index("wt")
+    count, width = tok.shape
+    chan = inner.shape[1]
+    kept = [keep(pair, w_near, s_own.at[0]), keep(small, w_small, s_own.at[1])]
 
     def norm(at):
         v = tok[pl.ds(at, 16)].astype(F32)
         inverse = lax.rsqrt(jnp.mean(v * v, axis=-1, keepdims=True) + EPS)
-        act[pl.ds(at, 16)] = (v * inverse * gain[...]).astype(BF16)
-
-    step_rows(tok.shape[0], 16, norm)
+        first_in[pl.ds(at, 16)] = (v * inverse * gain[...]).astype(BF16)
+
+    step_rows(count, 16, norm)
     greet(("seq", "wt"))
     little = cube_first(small, w_small, s_small)
     sent1, kept1 = share(cot, cot_f, s_cot, s_own.at[2])
-    sent2, kept2 = share(act, act_f, s_act, s_own.at[3])
-    big = cube_first(mixer, w_mixer, s_big)
+    sent2, kept2 = share(first_in, act_f, s_act, s_own.at[3])
+    pair1 = cube_first(pair, w_near, s_pair)
     sent = sent1 + sent2
     arrived(sent)
     kept1.wait()
@@ -303,32 +318,108 @@
     along = pass_along(cot_f, s_cz) + pass_along(act_f, s_az)
     little2 = cube_second(w_small, s_small, little)
     little3 = cube_third(w_small, s_small, little2)
-    big2 = cube_second(w_mixer, s_big, big)
-    big3 = cube_third(w_mixer, s_big, big2)
+    pair2 = cube_second(w_near, s_pair, pair1)
+    pair3 = cube_third(w_near, s_pair, pair2)
     cube_end(little, little2, little3)
-    cube_end(big, big2, big3)
-    arrived(along)
-    left(along)
-    left(sent)
+    cube_end(pair1, pair2, pair3)
     for copy in kept:
         copy.wait()
-
-
-def first_gather(mixer, small, cot, tok, gain, n_wt, n_seq, ident):
+    far = pltpu.make_async_copy(w_near, w_first, s_own.at[0])
+    far.start()
+
+    def project(target, first_tile):
+        def one(j, carry):
+            columns = pl.ds(pl.multiple_of(j * UNITS, UNITS), UNITS)
+            source = pl.ds(pl.multiple_of((first_tile + j) * UNITS, UNITS), UNITS)
+            tile = w_near[:, :, source].reshape(width, UNITS)
+            out = jnp.dot(first_in[...], tile, preferred_element_type=F32)
+            target[:, columns] = out.astype(target.dtype)
+            return carry
+
+        lax.fori_loop(0, chan // UNITS, one, 0)
+
+    project(inner, 0)
+    halo[0] = (inner[count - 16 :].astype(F32) * masks[count - 16 :, 3:4]).astype(BF16)
+    ahead = remote(halo.at[0], halo.at[1], s_halo, 0, "seq", lax.rem(seq + 1, n_seq))
+
+    @pl.when(seq + 1 < n_seq)
+    def _():
+        ahead.start()
+
+    @pl.when(seq == 0)
+    def _():
+        halo[1] = jnp.zeros_like(halo[1])
+
+    project(switch, chan // UNITS)
+    ext[16:] = inner[...].astype(F32)
+
+    @pl.when(seq > 0)
+    def _():
+        ahead.wait_recv()
+
+    ext[:16] = halo[1].astype(F32)
+    prev[...] = ext[8:16]
+
+    def convolve(at):
+        v = ext[pl.ds(pl.multiple_of(at + 8, 8), 24)]
+        same = masks[pl.ds(at, 16)]
+        out = bias[...] + taps[0:1] * v[8:]
+        for k in range(1, KC):
+            out = out + taps[k : k + 1] * v[8 - k : 24 - k] * same[:, k - 1 : k]
+        conv[pl.ds(at, 16)] = out
+        mixed[pl.ds(at, 16)] = (out * jax.nn.sigmoid(out)).astype(BF16)
+
+    step_rows(count, 16, convolve)
+    deep = w_small.shape[1]
+    all_rows = nt(w_small[...].reshape(n_seq * deep, chan), mixed[...])
+    rows = part.shape[0] // n_seq
+    for j in range(n_seq):
+        part[j * rows : (j + 1) * rows] = all_rows[j * deep + 16 : j * deep + 16 + rows]
+    first = scatter_start(part, recv, s_scatter, "wt")
+    rows = recv.shape[1]
+    arrived(first)
+    select[pl.ds(me * rows, rows)] = summed(part, recv, 0, rows, me * rows)
+    second = gather_start(select, rows, s_gather, "wt")
+    arrived(second)
+    arrived(along)
+    far.wait()
+
+    @pl.when(seq + 1 < n_seq)
+    def _():
+        ahead.wait_send()
+
+    for group in (along, sent, first, second):
+        left(group)
+
+
+def first_gather(pair, small, cot, tok, gain, taps, bias, masks, rows_sel, n_wt, n_seq, ident):
     count, width = cot.shape
-    far = jax.ShapeDtypeStruct((n_seq, n_wt, count // n_wt, width // n_seq), BF16)
+    chan = pair.shape[1] // 2
+    lines = rows_sel * n_seq
+    share_shape = jax.ShapeDtypeStruct((n_seq, n_wt, count // n_wt, width // n_seq), BF16)
     return pl.pallas_call(
         first_kernel,
         out_shape=[
-            jax.ShapeDtypeStruct((n_seq,) + mixer.shape, BF16),
+            jax.ShapeDtypeStruct((n_seq,) + pair.shape, BF16),
+            share_shape,
+            share_shape,
             jax.ShapeDtypeStruct((n_seq,) + small.shape, BF16),
-            far,
-            far,
-            jax.ShapeDtypeStruct((count, width), BF16),
+            jax.ShapeDtypeStruct((count, chan), BF16),
+            jax.ShapeDtypeStruct((8, chan), F32),
+            jax.ShapeDtypeStruct((count, chan), F32),
+            jax.ShapeDtypeStruct((count, chan), F32),
+            jax.ShapeDtypeStruct((count, chan), BF16),
+            jax.ShapeDtypeStruct((lines, count), F32),
         ],
-        in_specs=[ANY, ANY] + [VMEM] * 3,
-        out_specs=[ANY] * 4 + [VMEM],
+        in_specs=[ANY] * 2 + [VMEM] * 6,
+        out_specs=[ANY] * 3 + [VMEM] * 7,
         scratch_shapes=[
+            pltpu.VMEM((count, width), BF16),
+            pltpu.VMEM((n_seq,) + pair.shape, BF16),
+            pltpu.VMEM((16 + count, chan), F32),
+            pltpu.VMEM((2, 16, chan), BF16),
+            pltpu.VMEM((lines, count), F32),
+            pltpu.VMEM((n_wt - 1, lines // n_wt, count), F32),
             cube_sems(),
             cube_sems(),
             pltpu.SemaphoreType.DMA((4,)),
@@ -336,21 +427,15 @@
             pair_sems(n_seq),
             pair_sems(n_wt),
             pair_sems(n_wt),
+            pltpu.SemaphoreType.DMA((2, 1)),
+            pair_sems(n_wt),
+            pair_sems(n_wt),
         ],
         compiler_params=pltpu.CompilerParams(
             collective_id=ident, has_side_effects=True, vmem_limit_bytes=VMEM_BYTES
         ),
-        cost_estimate=pl.CostEstimate(flops=10**6, bytes_accessed=10**8, transcendentals=0),
-    )(mixer, small, cot, tok, gain[None])
-
-
-UNITS = 256
-
-
-def nt(left_op, right_op):
-    return lax.dot_general(
-        left_op, right_op, (((1,), (1,)), ((), ())), preferred_element_type=F32
-    )
+        cost_estimate=pl.CostEstimate(flops=10**9, bytes_accessed=10**8, transcendentals=0),
+    )(pair, small, cot, tok, gain[None], taps, bias[None], masks)
 
 
 def ffn_kernel(x, c, wg, wu, wd, gated, acts, down, d_second, acc_down, acc_second):
@@ -432,73 +517,36 @@
     )(*left_ops, *acts)
 
 
-def wt_sum_kernel(n_cube, n_spread, n_line, part, *refs):
-    n = n_cube + n_spread
-    srcs, refs = refs[:n], refs[n:]
-    lines, out, refs = refs[:n_line], refs[n_line], refs[n_line + 1 :]
-    dsts, wholes, refs = refs[:n], refs[n : n + n_line], refs[n + n_line :]
-    recv, s_scatter, s_gather = refs[:3]
-    sems = refs[3:]
+def wt_sum_kernel(part, out, recv, s_scatter, s_gather):
     me = lax.axis_index("wt")
     rows = recv.shape[1]
-    for line, whole in zip(lines, wholes):
-        whole[pl.ds(pl.multiple_of(me * line.shape[0], 16), line.shape[0])] = line[...]
-    greet(("wt", "seq") if n else ("wt",))
+    greet(("wt",))
     first = scatter_start(part, recv, s_scatter, "wt")
-    cubes, sent, kept = [], [], []
-    for i in range(n):
-        if i < n_cube:
-            cubes.append(cube_first(srcs[i], dsts[i], sems[2 * i]))
-            kept.append(keep(srcs[i], dsts[i], sems[2 * i + 1]))
-        else:
-            new, own = spread(srcs[i], dsts[i], sems[2 * i], sems[2 * i + 1])
-            sent += new
-            kept.append(own)
     arrived(first)
     out[pl.ds(me * rows, rows)] = summed(part, recv, 0, rows, me * rows)
     second = gather_start(out, rows, s_gather, "wt")
-    along = [line_gather_start(w, w.shape[0] // lax.axis_size("wt"), sems[-1]) for w in wholes]
-    cubes2 = [cube_second(dsts[i], sems[2 * i], cubes[i]) for i in range(n_cube)]
-    cubes3 = [cube_third(dsts[i], sems[2 * i], cubes2[i]) for i in range(n_cube)]
-    along = [
-        line_gather_mid(w, w.shape[0] // lax.axis_size("wt"), sems[-1], a)
-        for w, a in zip(wholes, along)
-    ]
-    for copies in along:
-        line_gather_end(copies)
-    for one, two, three in zip(cubes, cubes2, cubes3):
-        cube_end(one, two, three)
-    for copy in kept:
-        copy.wait()
     arrived(second)
-    arrived(sent)
-    for group in (first, second, sent, *along):
-        left(group)
-
-
-def wt_sum(part, blocks, srcs, lines, n_wt, n_seq, ident):
+    left(first)
+    left(second)
+
+
+def wt_sum(part, n_wt, ident):
     rows, cols = part.shape
     return pl.pallas_call(
-        functools.partial(wt_sum_kernel, len(blocks), len(srcs), len(lines)),
-        out_shape=[jax.ShapeDtypeStruct((rows, cols), F32)]
-        + [jax.ShapeDtypeStruct((n_seq,) + a.shape, BF16) for a in blocks]
-        + [jax.ShapeDtypeStruct((n_seq, a.shape[0], a.shape[1] // n_seq), BF16) for a in srcs]
-        + [jax.ShapeDtypeStruct((n_wt * a.shape[0], a.shape[1]), BF16) for a in lines],
-        in_specs=[VMEM] + [ANY] * len(blocks) + [VMEM] * len(srcs + lines),
-        out_specs=[VMEM] + [ANY] * len(blocks + srcs) + [VMEM] * len(lines),
+        wt_sum_kernel,
+        out_shape=jax.ShapeDtypeStruct((rows, cols), F32),
+        in_specs=[VMEM],
+        out_specs=VMEM,
         scratch_shapes=[
             pltpu.VMEM((n_wt - 1, rows // n_wt, cols), F32),
             pair_sems(n_wt),
             pair_sems(n_wt),
-        ]
-        + [cube_sems(), pltpu.SemaphoreType.DMA] * len(blocks)
-        + [pair_sems(n_seq), pltpu.SemaphoreType.DMA] * len(srcs)
-        + [pair_sems(n_wt)] * len(lines),
+        ],
         compiler_params=pltpu.CompilerParams(
             collective_id=ident, has_side_effects=True, vmem_limit_bytes=VMEM_BYTES
         ),
         cost_estimate=pl.CostEstimate(flops=10**5, bytes_accessed=10**6, transcendentals=0),
-    )(part, *blocks, *srcs, *lines)
+    )(part)
 
 
 def second_norm_kernel(part, tok, gain, out, res, recv, pend, s_scatter, s_gather):
@@ -620,12 +668,12 @@
     )(part, res, cot_own, gain[None], *srcs)
 
 
-def last_kernel(cube, part, tok, d_res, gain, gain_grad2, sel, stp, taps, decays, bias3, *refs):
+def last_kernel(cube, part, tok, d_res, gain, gain_grad2, sel, stp, taps, decays, bias3, line, *refs):
     blocks, refs = refs[:cube], refs[cube:]
     if cube:
         cot_t, second_t, branch_t, acts, refs = refs[0], refs[1], refs[2], refs[3], refs[4:]
-    out, sel_out, stp_out, chan_out, gains_out = refs[:5]
-    wholes, refs = refs[5 : 5 + cube], refs[5 + cube :]
+    out, block_out, sel_out, stp_out, chan_out, gains_out = refs[:6]
+    wholes, refs = refs[6 : 6 + cube], refs[6 + cube :]
     if cube:
         grad_outs, refs = refs[:4], refs[4:]
         tile, s_tile, refs = refs[0], refs[1], refs[2:]
@@ -655,11 +703,12 @@
 
         fetch(0, 0).start()
     recv, pend, recv_sel, recv_stp, recv_chan, pack, gain_buf, recv_gz, recv_gs = refs[:9]
-    s_scatter, s_gather, s_sel, s_stp, s_chan, s_cg, s_gz, s_gs = refs[9:17]
-    refs = refs[17:]
+    s_scatter, s_gather, s_sel, s_stp, s_chan, s_cg, s_gz, s_gs, s_block = refs[9:18]
+    refs = refs[18:]
     me, n_wt = lax.axis_index("wt"), lax.axis_size("wt")
     seq, n_seq = lax.axis_index("seq"), lax.axis_size("seq")
     rows = recv.shape[1]
+    block_out[pl.ds(pl.multiple_of(me * rows, 16), rows)] = line[...]
     greet(("wt", "seq"))
     first = line_scatter_start(part, recv, s_scatter)
     share = -(-(KC + NS + 3) // n_seq)
@@ -708,6 +757,7 @@
 
     step_rows(rows, 16, body)
     second = line_gather_start(out, rows, s_gather)
+    third = line_gather_start(block_out, rows, s_block)
     high = recv_gz.shape[1] // 2
     for i, grad in enumerate((gain_buf, gain_grad2)):
         line = jnp.sum(grad[...], axis=0, keepdims=True)
@@ -719,6 +769,7 @@
     if cube:
         lax.fori_loop(tiles - 2, tiles, one_tile, 0)
     second = line_gather_mid(out, rows, s_gather, second)
+    third = line_gather_mid(block_out, rows, s_block, third)
     arrived(zs)
     total = recv_gz[0]
     for pos in range(1, n_wt):
@@ -739,11 +790,12 @@
         cube_end(one, two, three)
         kept.wait()
     line_gather_end(second)
-    for group in (first, second, smalls, chans, zs, ss):
+    line_gather_end(third)
+    for group in (first, second, third, smalls, chans, zs, ss):
         left(group)
 
 
-def last(part, tok_own, d_res, gain, gain_grad2, sel, stp, taps, decays, bias3, blocks, more, n_wt, n_seq, ident):
+def last(part, tok_own, d_res, gain, gain_grad2, sel, stp, taps, decays, bias3, line, blocks, more, n_wt, n_seq, ident):
     rows, cols = part.shape
     own = rows // n_wt
     chan = taps.shape[1]
@@ -755,6 +807,7 @@
         functools.partial(last_kernel, len(blocks)),
         out_shape=[
             jax.ShapeDtypeStruct((rows, cols), BF16),
+            jax.ShapeDtypeStruct((rows, cols), BF16),
             jax.ShapeDtypeStruct(sel.shape[1:], F32),
             jax.ShapeDtypeStruct(stp.shape[1:], F32),
             jax.ShapeDtypeStruct((n_seq, 8, chan), F32),
@@ -762,8 +815,8 @@
         ]
         + [jax.ShapeDtypeStruct((n_seq,) + a.shape, BF16) for a in blocks]
         + ([jax.ShapeDtypeStruct((deep, w), F32) for w in (units, units, units, chan)] if more else []),
-        in_specs=[VMEM] * 10 + [ANY] * len(blocks) + ([VMEM, VMEM, VMEM, ANY] if more else []),
-        out_specs=[VMEM] * 5 + [ANY] * len(blocks) + ([VMEM] * 4 if more else []),
+        in_specs=[VMEM] * 11 + [ANY] * len(blocks) + ([VMEM, VMEM, VMEM, ANY] if more else []),
+        out_specs=[VMEM] * 6 + [ANY] * len(blocks) + ([VMEM] * 4 if more else []),
         scratch_shapes=(
             [pltpu.VMEM((2, tok_all, span), BF16), pltpu.SemaphoreType.DMA((2,))]
             if more
@@ -787,13 +840,14 @@
             pair_sems(n_seq),
             pair_sems(n_wt),
             pair_sems(n_seq),
+            pair_sems(n_wt),
         ]
         + [cube_sems(), pltpu.SemaphoreType.DMA] * len(blocks),
         compiler_params=pltpu.CompilerParams(
             collective_id=ident, has_side_effects=True, vmem_limit_bytes=VMEM_BYTES
         ),
         cost_estimate=pl.CostEstimate(flops=10**6, bytes_accessed=10**8, transcendentals=0),
-    )(part, tok_own, d_res, gain[None], gain_grad2, sel, stp, taps, decays, bias3, *blocks, *more)
+    )(part, tok_own, d_res, gain[None], gain_grad2, sel, stp, taps, decays, bias3, line, *blocks, *more)
 
 
 def load(ref):
@@ -1107,30 +1161,6 @@
     cube = n_seq == 8 and n_seq * tok_count <= width
 
     rows_sel, rows_step = select_proj.shape[0], step_proj.shape[0]
-    if cube:
-        fill = jnp.zeros((-(rows_sel + rows_step) % 32, chan), BF16)
-        small = jnp.concatenate([select_proj, step_proj, fill], axis=0)
-        w_mixer, w_small, cot_f, first_f, first_in = first_gather(
-            jnp.concatenate([inner_proj, switch_proj, mixer_out], axis=1),
-            small, cotangent, tokens, premix_gain, n_wt, n_seq, 7,
-        )
-        w_mixer = w_mixer.reshape(width, 3 * chan)
-    else:
-        token_vals = tokens.astype(F32)
-        first_inv = lax.rsqrt(jnp.mean(token_vals * token_vals, axis=-1, keepdims=True) + EPS)
-        first_in = (token_vals * first_inv * premix_gain).astype(BF16)
-        w_mixer = gather(jnp.concatenate([inner_proj, switch_proj, mixer_out], axis=1))
-        w_small = lax.all_gather(jnp.concatenate([select_proj, step_proj], axis=0), "seq", axis=0)
-    ffn_own = jnp.concatenate([ffn_gate, ffn_up, ffn_down], axis=1)
-    ffn_own, w_small = lax.optimization_barrier((ffn_own, w_small))
-    w_all = gather(ffn_own)
-    w_first, w_mix = w_mixer[:, : 2 * chan], w_mixer[:, 2 * chan :]
-    w_select = w_small[:, :rows_sel].reshape(-1, chan)
-    w_step = w_small[:, rows_sel : rows_sel + rows_step].reshape(-1, chan)
-    both = contract(first_in, w_first, "td,dc->tc")
-    inner_act = both[:, :chan].astype(BF16)
-    switch = both[:, chan:]
-
     goes_on = (1 - doc_start).astype(F32)
     before = jnp.concatenate([jnp.ones((edge,), F32), goes_on])
     after = jnp.concatenate([goes_on, jnp.ones((edge,), F32)])
@@ -1155,19 +1185,51 @@
         * jnp.concatenate([one[:1], head[:2]])
         * jnp.concatenate([one, head[:1]])
     )
-    prev_rows = from_behind(inner_act[-edge:] * tail_keep[:, None].astype(BF16), "seq", 1)
-    extended = jnp.concatenate([prev_rows, inner_act], axis=0).astype(F32)
-    conv_out = jnp.zeros((tok_count, chan), F32) + conv_bias[None, :]
-    for offset in range(KC):
-        conv_out = (
-            conv_out
-            + conv_taps[offset][None, :]
-            * extended[edge - offset : edge - offset + tok_count]
-            * same_back(offset)
+    if cube:
+        fill = jnp.zeros((-(rows_sel + rows_step) % 32, chan), BF16)
+        ones = jnp.ones((tok_count - edge,), F32)
+        columns = [same_back(k)[:, 0] for k in range(1, KC)]
+        columns += [jnp.concatenate([ones, tail_keep])] * (9 - KC)
+        (
+            w_first, cot_f, first_f, w_small,
+            inner_act, prev_rows, switch, conv_out, mixed_in, select,
+        ) = first_gather(
+            jnp.concatenate([inner_proj, switch_proj], axis=1),
+            jnp.concatenate([step_proj, select_proj, fill], axis=0),
+            cotangent, tokens, premix_gain, conv_taps, conv_bias,
+            jnp.stack(columns, axis=1), rows_sel, n_wt, n_seq, 7,
         )
-    mixed_in = jax.nn.silu(conv_out).astype(BF16)
+        w_first = w_first.reshape(width, 2 * chan)
+        w_mix = gather(mixer_out)
+        prev_rows = prev_rows[8 - edge :]
+    else:
+        token_vals = tokens.astype(F32)
+        first_inv = lax.rsqrt(jnp.mean(token_vals * token_vals, axis=-1, keepdims=True) + EPS)
+        first_in = (token_vals * first_inv * premix_gain).astype(BF16)
+        w_mixer = gather(jnp.concatenate([inner_proj, switch_proj, mixer_out], axis=1))
+        w_first, w_mix = w_mixer[:, : 2 * chan], w_mixer[:, 2 * chan :]
+        w_small = lax.all_gather(jnp.concatenate([step_proj, select_proj], axis=0), "seq", axis=0)
+    w_all = gather(jnp.concatenate([ffn_gate, ffn_up, ffn_down], axis=1))
+    w_step = w_small[:, :rows_step].reshape(-1, chan)
+    w_select = w_small[:, rows_step : rows_step + rows_sel].reshape(-1, chan)
+    if not cube:
+        both = contract(first_in, w_first, "td,dc->tc")
+        inner_act = both[:, :chan].astype(BF16)
+        switch = both[:, chan:]
+        prev_rows = from_behind(inner_act[-edge:] * tail_keep[:, None].astype(BF16), "seq", 1)
+        extended = jnp.concatenate([prev_rows, inner_act], axis=0).astype(F32)
+        conv_out = jnp.zeros((tok_count, chan), F32) + conv_bias[None, :]
+        for offset in range(KC):
+            conv_out = (
+                conv_out
+                + conv_taps[offset][None, :]
+                * extended[edge - offset : edge - offset + tok_count]
+                * same_back(offset)
+            )
+        mixed_in = jax.nn.silu(conv_out).astype(BF16)
+        select = wt_sum(contract(w_select, mixed_in, "jc,tc->jt"), n_wt, 0)
     mixed_f = mixed_in.astype(F32)
-    (select,) = wt_sum(contract(w_select, mixed_in, "jc,tc->jt"), (), (), (), n_wt, n_seq, 0)
+    extended = jnp.concatenate([prev_rows.astype(F32), inner_act.astype(F32)], axis=0)
     low_rank = select[:R].astype(BF16)
     write_read = select[R:]
     step_pre = contract(low_rank, w_step, "rt,rc->tc") + step_bias[None, :]
@@ -1212,7 +1274,7 @@
         v.reshape(n_seq, -1, tok_count), ((0, 0), (0, -(v.shape[0] // n_seq) % 16), (0, 0))
     ).reshape(-1, tok_count)
     grad_step = contract(pad_rows(low_rank), d_pre_low, "rt,tc->rc").astype(BF16)
-    d_select, *gathered, block_out = wt_sum(
+    d_select = wt_sum(
         jnp.concatenate(
             [
                 contract(w_step, d_pre_low, "rc,tc->rt"),
@@ -1220,11 +1282,7 @@
             ],
             axis=0,
         ),
-        (d_switch,) if cube else (),
-        (),
-        (block_own,),
         n_wt,
-        n_seq,
         5,
     )
     d_select = d_select.astype(BF16)
@@ -1262,22 +1320,21 @@
     ).astype(BF16)
     more = ()
     if cube:
-        (switch_all,) = map(line_up, gathered)
         more = (cot_t, line_up(second_all[0]).T, line_up(branch_all[0]).T, gather(acts))
-    tokens_grad, out_select, out_step, by_chan, gains, *others = last(
+    tokens_grad, block_out, out_select, out_step, by_chan, gains, *others = last(
         d_first, tokens_own, d_residual, premix_gain, grad_preffn,
         grad_select.reshape(n_seq, -1, chan), grad_step.reshape(n_seq, -1, chan),
         jnp.stack(taps_rows, axis=0), grad_decay_log,
-        jnp.stack([grad_conv_bias, grad_step_bias, grad_skip]),
-        (d_inner_low,) if cube else (), more, n_wt, n_seq, 6,
+        jnp.stack([grad_conv_bias, grad_step_bias, grad_skip]), block_own,
+        (d_switch, d_inner_low) if cube else (), more, n_wt, n_seq, 6,
     )
     share = -(-(KC + NS + 3) // n_seq)
     by_chan = by_chan[:, :share].reshape(n_seq * share, chan)
     gains = gains.reshape(2, width)
     if cube:
-        out_down, out_gate, out_up, out_mix = others[1:]
+        out_down, out_gate, out_up, out_mix = others[2:]
         out_switch, out_inner = grads(
-            (first_t,), (0, 0), (switch_all, line_up(others[0]))
+            (first_t,), (0, 0), (line_up(others[0]), line_up(others[1]))
         )
     else:
         scatter = lambda v: lax.psum_scatter(v, "seq", scatter_dimension=0, tiled=True)

time: 504 us -> 478 us (0.948)
  Pallas kernels: 381 us -> 371 us
  matrix products: 33.1 us -> 24.9 us
  waiting for transfers between devices: 15 us -> 8.84 us
    pallas_call x3 -> x2, Pallas kernels: 146 us -> 117 us  [the longest x1 97.2 us: first_gather(): pl.pallas_call(first_kernel, out_shape=[jax.ShapeDtypeStruct((n_seq,) + p...]
    pallas_call x1, Pallas kernels: 50.5 us -> 66.7 us  [last(): pl.pallas_call(functools.partial(last_kernel, len(blocks)), out_shape=[ja...]
    dot_general x10 -> x8, matrix products: 33.1 us -> 24.9 us  [contract(): return jnp.einsum(pattern, left_op, right_op, preferred_element_type=F32)]
    all_gather x2 -> x3, waiting for transfers between devices: 15 us -> 8.12 us  [gather(): return lax.all_gather(block, 'seq', axis=0, tiled=True)]
    unnamed x91 -> x77, local copies, waits for them, and re-layouts: 14.1 us -> 14.6 us
  transfers between devices with their start and end apart: 4 -> 4, of which waited for: 1 -> 2; matrix products, arithmetic and copies ran while one was open for 13% -> 14% of each run, Pallas kernels for 45% -> 58%
where the time goes in v4:
time: 478 us; the launch traced here: 477 us
  Pallas kernels  371 us (78%)
  local copies, waits for them, and re-layouts  33.8 us (7%)
  matrix products  24.9 us (5%)
  other arithmetic  22.6 us (5%)
  between operations  14.2 us (3%)
  waiting for transfers between devices  8.84 us (2%)
    pallas_call x1, Pallas kernels, first_gather(): pl.pallas_call(first_kernel, out_shape=[jax.ShapeDtypeStruct((n_seq,) + p...  97.2 us
    pallas_call x1, Pallas kernels, last(): pl.pallas_call(functools.partial(last_kernel, len(blocks)), out_shape=[ja...  66.7 us
    pallas_call x1, Pallas kernels, bwd_scan(): pl.pallas_call(functools.partial(bwd_kernel, len(src)), out_shape=[jax.Sh...  49.7 us
    pallas_call x1, Pallas kernels, second_back(): pl.pallas_call(functools.partial(second_back_kernel, len(srcs)), out_shap...  47.7 us
    pallas_call x1, Pallas kernels, second_norm(): pl.pallas_call(second_norm_kernel, out_shape=[jax.ShapeDtypeStruct((rows,...  41.6 us
    dot_general x8, matrix products, contract(): return jnp.einsum(pattern, left_op, right_op, preferred_element_type=F32)  24.9 us
    pallas_call x1, Pallas kernels, ffn(): pl.pallas_call(ffn_kernel, grid=(steps,), in_specs=[whole, whole, tile(0)...  20.7 us
    pallas_call x1, Pallas kernels, fwd_scan(): pl.pallas_call(fwd_kernel, out_shape=[jax.ShapeDtypeStruct((tok, high, 12...  20.5 us
  transfers between devices with their start and end apart: 4, of which 2 were waited for; matrix products, arithmetic and copies ran while one was open for 14% of the time, Pallas kernels for 58%

profile of v4, /device:TPU:0, one launch (start us, length us, event | category | flops | bytes accessed | tf_op | source)
XLA Modules:
  0.0 476.9 jit_solution(215497725495271723)
XLA Ops:
  7.2 0.7 all-gather.4.cloned.1.call-update
  8.0 3.1 pad_maximum_fusion
  12.5 0.7 maximum_multiply_fusion
  13.4 0.8 copy.53.masks
  14.2 0.7 maximum_maximum_fusion.small
  15.0 1.1 pad_maximum_fusion.2.pair
  16.0 97.2 %shard_map.305 = (bf16[8,256,2048]{2,1,0:T(8,128)(2,1)}, bf16[8,4,64,256]{3,2,1,0:T(8,128)(2,1)}, bf16[8,4,64,256]{3,2,1,0:T(8,128)(2,1)}, bf16[8,64,1024]{2,1,0...) custom-call(bf16[256,2048]{1,0:T(8,128)(2,1)} %pad_maximum_fusion.2., ...), custom_call_target="tpu_custom_call" | custom-call | flops 1000000000 | bytes 100000000 | tf_op jit(solution)/shard_map/pallas_call | solution.py:400
  113.2 1.0 slice.127
  114.2 1.4 slice.128.wr
  115.6 1.2 convolution_add_fusion.1
  116.9 1.8 fusion.4
  118.6 1.2 copy.60
  119.8 1.2 copy.61
  121.0 0.6 copy.62
  121.6 1.4 copy.54
  123.0 1.4 copy.55
  124.5 20.5 %shard_map.306 = (f32[256,8,128]{2,1,0:T(8,128)}, f32[16,8,128]{2,1,0:T(8,128)}) custom-call(f32[256,8,128]{2,1,0:T(8,128)} %bitcast.104, f32[256,8,128]{2,1,0:T(8,128)} %bitcast.106, f32[32,256]{1,0:T(8,128)} %slice.128.wr, f32[16,8,128]{2,1,0:T(8,128)} %bitcast.118), custom_call_target="tpu_custom_call" | custom-call | flops 100000000 | bytes 80000000 | tf_op jit(solution)/shard_map/pallas_call | solution.py:934
  144.9 1.2 fusion.36
  146.2 1.8 dynamic-slice_convert_fusion.1.tok
  148.0 1.8 dynamic-slice_convert_fusion.cot
  149.8 1.7 multiply_convert_fusion.1.gated
  151.5 4.6 convolution_convert_fusion.part
  156.1 41.6 %shard_map.307 = (bf16[256,2048]{1,0:T(8,128)(2,1)}, f32[64,2048]{1,0:T(8,128)}) custom-call(bf16[256,2048]{1,0:T(8,128)(2,1)} %convolution_convert_fusion.part, f32[64,2048]{1,0:T(8,128)} %dynamic-slice_convert_fusion.1.tok, f32[1,2048]{1,0:T(1,128)} %bitcast.125), custom_call_target="tpu_custom_call" | custom-call | flops 1000000 | bytes 100000000 | tf_op jit(solution)/shard_map/pallas_call | solution.py:578
  197.8 2.1 all-gather.6.cloned.1.call-done.wg.wu.wd
  199.8 20.7 %shard_map.308 = (bf16[256,7168]{1,0:T(8,128)(2,1)}, bf16[256,2048]{1,0:T(8,128)(2,1)}, bf16[256,2048]{1,0:T(8,128)(2,1)}) custom-call(bf16[256,2048]{1,0:T(8,128)(2,1)} %get-tuple-element.71.x.refs_0_, bf16[256,2048]{1,0:T(8,128)(2,1)} %c.1, bf16[2048,6144]{1,0:T(8,128)(2,1)} %all-gather.6.cloned.1.call-done.wg.wu.wd, ...), custom_call_target="tpu_custom_call" | custom-call | flops 12884901888 | bytes 25165824 | tf_op jit(solution)/shard_map/pallas_call | solution.py:477
  220.5 1.0 slice.132
  221.6 2.1 convert_element_type.75
  223.7 0.8 reshape.136
  224.5 47.7 %shard_map.309 = (bf16[256,2048]{1,0:T(8,128)(2,1)}, f32[64,2048]{1,0:T(8,128)}, f32[8,2048]{1,0:T(8,128)}, bf16[8,256,256]{2,1,0:T(8,128)(2,1)}) custom-call(bf16[256,2048]{1,0:T(8,128)(2,1)} %get-tuple-element.72.part, f32[64,2048]{1,0:T(8,128)} %get-tuple-element.73.res, f32[64,2048]{1,0:T(8,128)} %dynamic-slice_convert_fusion.cot, f32[1,2048]{1,0:T(1,128)} %bitcast.126, ...), custom_call_target="tpu_custom_call" | custom-call | flops 1000000 | bytes 100000000 | tf_op jit(solution)/shard_map/pallas_call | solution.py:647
  272.2 5.3 %fusion.8 = (f32[1024]{0:T(1024)S(1)}, f32[256,1024]{1,0:T(8,128)S(1)}, bf16[256,1024]{1,0:T(8,128)(2,1)}) fusion(bf16[256,1024]{1,0:T(8,128)(2,1)S(1)} %copy-done, f32[256,1024]{1,0:T(8,128)S(1)} %copy-done.7, f32[1024]{0:T(1024)S(1)} %copy-done.29, f32[32,8,8,128]{3,2,1,0:T(8,128)} %bitcast.111, bf16[256,2048]{1,0:T(8,128)(2,1)} %get-tuple-element.75.refs_0_, ...), kind=kOutput, calls=%fused_computation.27 | convolution fusion | flops 1078197248 | bytes 9445376 | tf_op jit(solution)/shard_map/td,dc->tc/dot_general | solution.py:1118
  277.5 1.0 copy-done.9
  278.5 1.2 copy.64
  279.7 49.7 %shard_map.310 = (f32[256,8,128]{2,1,0:T(8,128)}, f32[256,8,128]{2,1,0:T(8,128)}, f32[16,8,128]{2,1,0:T(8,128)}, f32[16,512]{1,0:T(8,128)}, bf16[64,2048]{1,0:T(8,128)(2,1)}, /*index=5*/bf16[8,4,64,256]{3,2,1,0:T(8,128)(2,1)}) custom-call(f32[256,8,128]{2,1,0:T(8,128)} %bitcast.105, f32[256,8,128]{2,1,0:T(8,128)} %bitcast.107, f32[32,256]{1,0:T(8,128)} %slice.128.wr, ...), custom_call_target="tpu_custom_call" | custom-call | flops 100000000 | bytes 150000000 | tf_op jit(solution)/shard_map/pallas_call | solution.py:1072
  329.4 1.0 reshape.134
  330.4 1.4 broadcast_multiply_fusion
  331.9 0.7 fusion.38
  332.9 0.7 pad_maximum_fusion.3.part
  333.6 19.8 %shard_map.311 = f32[160,256]{1,0:T(8,128)} custom-call(f32[160,256]{1,0:T(8,128)} %pad_maximum_fusion.3.part), custom_call_target="tpu_custom_call" | custom-call | flops 100000 | bytes 1000000 | tf_op jit(solution)/shard_map/pallas_call | solution.py:535
  353.4 0.9 convert_element_type.65
  354.5 4.6 fusion.11
  359.1 1.6 collective-permute-start
  361.4 0.7 bitcast_multiply_fusion.1.decays
  362.1 0.9 convolution_convert_fusion.3
  363.0 1.1 convolution_convert_fusion.2
  364.1 0.6 pad_maximum_fusion.4.taps
  364.7 2.3 copy.58
  367.0 1.4 copy.59
  368.5 0.6 fusion.19.refs_1_
  369.4 6.9 %convolution_convert_fusion.1.part = bf16[256,2048]{1,0:T(8,128)(2,1)} fusion(bf16[2048,2048]{1,0:T(8,128)(2,1)} %bitcast.147, bf16[256,1024]{1,0:T(8,128)(2,1)S(1)} %copy-done.18, bf16[256,1024]{1,0:T(8,128)(2,1)S(1)} %fusion.19.refs_1_), kind=kOutput, calls=%fused_computation.3 | convolution fusion | flops 2150105088 | bytes 10485760 | tf_op jit(solution)/shard_map/tc,dc->td/dot_general | solution.py:1118
  376.3 6.0 %all-gather.8.cloned.1.call-done.refs_5_ = bf16[2048,7168]{1,0:T(8,128)(2,1)} async-done(((bf16[256,7168]{1,0:T(8,128)(2,1)}), bf16[2048,7168]{1,0:T(8,128)(2,1)}) %all-gather.8.cloned.1.call-update) | async-done | bytes 29360144 | tf_op jit(solution)/shard_map/all_gather | solution.py:1108
  382.4 66.7 %shard_map.312 = (bf16[256,2048]{1,0:T(8,128)(2,1)}, bf16[256,2048]{1,0:T(8,128)(2,1)}, f32[32,1024]{1,0:T(8,128)}, f32[16,1024]{1,0:T(8,128)}, f32[8,8,1024]{2,...) custom-call(bf16[256,2048]{1,0:T(8,128)(2,1)} %convolution_convert_f, ...), custom_call_target="tpu_custom_call" | custom-call | flops 1000000 | bytes 100000000 | tf_op jit(solution)/shard_map/pallas_call | solution.py:806
  449.0 1.0 slice.149
  450.1 0.6 slice.170
  451.9 1.5 slice.152
  453.5 1.3 slice_bitcast_fusion
  454.8 7.0 %shard_map.313 = (f32[256,1024]{1,0:T(8,128)}, f32[256,1024]{1,0:T(8,128)}) custom-call(bf16[256,2048]{1,0:T(8,128)(2,1)} %bitcast.89, bf16[2048,1024]{1,0:T(8,128)(2,1)} %bitcast.94, bf16[2048,1024]{1,0:T(8,128)(2,1)} %bitcast.95), custom_call_target="tpu_custom_call" | custom-call | flops 2147483648 | bytes 8388608 | tf_op jit(solution)/shard_map/pallas_call | solution.py:506
  461.8 1.0 copy.86
  462.8 1.0 copy.87
  463.7 0.6 copy.88
  464.4 1.0 copy.89
  465.3 1.3 copy.90
  466.7 1.3 copy.91
  468.0 1.0 copy-done.3
  469.0 1.3 copy.92
  (93 shorter events, 4.6 us)
Async XLA Ops:
  7.2 144.3 %all-gather.4.cloned.1.call-start = ((), (), s32[]{:S(2)}) async-start(), calls=%async_computation | async-start | bytes 4718592 | tf_op jit(solution)/shard_map/all_gather | solution.py:1108
  7.9 191.9 %all-gather.6.cloned.1.call-start = ((), (), s32[]{:S(2)}) async-start(), calls=%async_computation.1 | async-start | bytes 28311552 | tf_op jit(solution)/shard_map/all_gather | solution.py:1108
  11.1 0.7 copy-start.32
  11.1 3.1 copy-start.24
  11.1 3.1 copy-start.25
  11.1 3.9 copy-start.19
  11.1 3.8 copy-start.20
  11.2 371.2 %all-gather.8.cloned.1.call-start = ((), (), s32[]{:S(2)}) async-start(), calls=%async_computation.2 | async-start | bytes 33030144 | tf_op jit(solution)/shard_map/all_gather | solution.py:1108
  13.3 100.9 %copy-start.30 = (f32[256]{0:T(256)}, f32[256]{0:T(256)S(1)}, u32[]{:S(2)}) copy-start(f32[256]{0:T(256)S(1)} %get-tuple-element.136) | copy-start | bytes 3076
  15.0 100.6 %copy-start.28 = (f32[1024]{0:T(1024)S(1)}, f32[1024]{0:T(1024)}, u32[]{:S(2)}) copy-start(f32[1024]{0:T(1024)} %param.28) | copy-start | bytes 12292
  116.8 4.1 copy-start.21
  118.6 3.0 copy-start.14
  118.6 4.4 copy-start.13
  124.5 25.3 %copy-start = (bf16[256,1024]{1,0:T(8,128)(2,1)S(1)}, bf16[256,1024]{1,0:T(8,128)(2,1)}, u32[]{:S(2)}) copy-start(bf16[256,1024]{1,0:T(8,128)(2,1)} %get-tuple-element.65) | copy-start | bytes 1572868
  124.5 25.3 %copy-start.7 = (f32[256,1024]{1,0:T(8,128)S(1)}, f32[256,1024]{1,0:T(8,128)}, u32[]{:S(2)}) copy-start(f32[256,1024]{1,0:T(8,128)} %get-tuple-element.67) | copy-start | bytes 3145732
  124.5 25.3 %copy-start.29 = (f32[1024]{0:T(1024)S(1)}, f32[1024]{0:T(1024)}, u32[]{:S(2)}) copy-start(f32[1024]{0:T(1024)} %param.30) | copy-start | bytes 12292
  151.5 4.7 copy-start.2
  220.5 4.0 copy-start.26
  277.5 1.0 copy-start.9
  329.4 2.5 copy-start.6
  331.9 1.7 copy-start.27
  354.4 4.6 copy-start.31
  354.4 7.0 %copy-start.22 = (f32[16,8,128]{2,1,0:T(8,128)S(1)}, f32[16,8,128]{2,1,0:T(8,128)}, u32[]{:S(2)}) copy-start(f32[16,8,128]{2,1,0:T(8,128)} %get-tuple-element.88) | copy-start | bytes 196612
  354.4 7.6 %copy-start.17 = (f32[160,256]{1,0:T(8,128)S(1)}, f32[160,256]{1,0:T(8,128)}, u32[]{:S(2)}) copy-start(f32[160,256]{1,0:T(8,128)} %get-tuple-element.63) | copy-start | bytes 491524
  359.0 5.1 %copy-start.15 = (bf16[256,1024]{1,0:T(8,128)(2,1)}, bf16[256,1024]{1,0:T(8,128)(2,1)S(1)}, u32[]{:S(2)}) copy-start(bf16[256,1024]{1,0:T(8,128)(2,1)S(1)} %get-tuple-element.141) | copy-start | bytes 1572868
  359.0 8.0 %copy-start.8 = (bf16[8,256,256]{2,1,0:T(8,128)(2,1)S(1)}, bf16[8,256,256]{2,1,0:T(8,128)(2,1)}, u32[]{:S(2)}) copy-start(bf16[8,256,256]{2,1,0:T(8,128)(2,1)} %get-tuple-element.91) | copy-start | bytes 3145732
  359.1 9.3 %collective-permute-start = (bf16[3,1024]{1,0:T(4,128)(2,1)S(1)}, bf16[3,1024]{1,0:T(4,128)(2,1)S(1)}, u32[]{:S(2)}, u32[]{:S(2)}) collective-permute-start(bf16[3,1024]{1,0:T(4,128)(2,1)S(1)} %slice_multiply_fusion.4), channel_id=1, source_target_pairs={{4,0},{8,4},{12,8},{16,12},{20,16},{24,20},{28,24},{5,1},{9,5},{13... | collective-permute-start | bytes 18440 | tf_op jit(solution)/shard_map/ppermute | solution.py:1114
  364.1 4.3 copy-start.16
  368.4 1.0 copy-start.18
  369.2 7.2 %copy-start.1 = (bf16[256,1024]{1,0:T(8,128)(2,1)}, bf16[256,1024]{1,0:T(8,128)(2,1)S(1)}, u32[]{:S(2)}) copy-start(bf16[256,1024]{1,0:T(8,128)(2,1)S(1)} %fusion.19.refs_1_) | copy-start | bytes 1572868
  454.8 7.0 %copy-start.12 = (bf16[256,2048]{1,0:T(8,128)(2,1)S(1)}, bf16[256,2048]{1,0:T(8,128)(2,1)}, u32[]{:S(2)}) copy-start(bf16[256,2048]{1,0:T(8,128)(2,1)} %get-tuple-element.161) | copy-start | bytes 3145732
  454.8 8.0 %copy-start.11 = (bf16[256,2048]{1,0:T(8,128)(2,1)S(1)}, bf16[256,2048]{1,0:T(8,128)(2,1)}, u32[]{:S(2)}) copy-start(bf16[256,2048]{1,0:T(8,128)(2,1)} %get-tuple-element.162) | copy-start | bytes 3145732
  461.8 2.0 copy-start.23
  461.8 2.6 copy-start.10
  461.8 3.6 copy-start.5
  464.4 2.3 copy-start.4
  466.7 2.3 copy-start.3
Sparse Core Ops, SparseCore 0:
  9.9 56.7 all-gather.3
  68.6 131.2 all-gather.5
  220.7 161.6 all-gather.7

commit v5 on v4

--- a/solution.py
+++ b/solution.py
@@ -210,7 +210,7 @@
     return copy
 
 
-def spread(src, dst, sems, own_sem):
+def spread_plan(src, dst, sems, own_sem):
     seq, n_seq = lax.axis_index("seq"), lax.axis_size("seq")
     piece = dst.shape[2]
 
@@ -220,8 +220,15 @@
     out = []
     for k in range(1, n_seq):
         peer = lax.rem(seq + k, n_seq)
-        out.append(send(columns(peer), dst.at[seq], sems, k - 1, "seq", peer))
-    return out, keep(columns(seq), dst, own_sem)
+        out.append(remote(columns(peer), dst.at[seq], sems, k - 1, "seq", peer))
+    return out, pltpu.make_async_copy(columns(seq), dst.at[seq], own_sem)
+
+
+def spread(src, dst, sems, own_sem):
+    out, own = spread_plan(src, dst, sems, own_sem)
+    for copy in out + [own]:
+        copy.start()
+    return out, own
 
 
 def cube_second(whole, sems, first):
@@ -289,9 +296,9 @@
 
 
 def first_kernel(
-    pair, small, cot, tok, gain, taps, bias, masks,
+    pair, small, cot, tok, gain, taps, bias, goes,
     w_first, cot_f, act_f, w_small, inner, prev, switch, conv, mixed, select,
-    first_in, w_near, ext, halo, part, recv,
+    first_in, w_near, ext, before, halo, part, recv,
     s_pair, s_small, s_own, s_cot, s_act, s_cz, s_az, s_halo, s_scatter, s_gather,
 ):
     seq, n_seq = lax.axis_index("seq"), lax.axis_size("seq")
@@ -339,7 +346,13 @@
         lax.fori_loop(0, chan // UNITS, one, 0)
 
     project(inner, 0)
-    halo[0] = (inner[count - 16 :].astype(F32) * masks[count - 16 :, 3:4]).astype(BF16)
+    last_row, row_before = goes[count - 1 :], goes[count - 2 : count - 1]
+    cut = jnp.concatenate(
+        [jnp.ones((13, 1), F32), (last_row * row_before)[:, :1], last_row[:, :1], jnp.ones((1, 1), F32)]
+    )
+    halo[0] = (inner[count - 16 :].astype(F32) * cut).astype(BF16)
+    before[:16] = jnp.ones((16, 128), F32)
+    before[16:] = goes[...]
     ahead = remote(halo.at[0], halo.at[1], s_halo, 0, "seq", lax.rem(seq + 1, n_seq))
 
     @pl.when(seq + 1 < n_seq)
@@ -362,10 +375,13 @@
 
     def convolve(at):
         v = ext[pl.ds(pl.multiple_of(at + 8, 8), 24)]
-        same = masks[pl.ds(at, 16)]
+        g = before[pl.ds(pl.multiple_of(at + 8, 8), 24)]
+        same = None
         out = bias[...] + taps[0:1] * v[8:]
         for k in range(1, KC):
-            out = out + taps[k : k + 1] * v[8 - k : 24 - k] * same[:, k - 1 : k]
+            step = g[9 - k : 25 - k]
+            same = step if same is None else same * step
+            out = out + taps[k : k + 1] * v[8 - k : 24 - k] * same[:, :1]
         conv[pl.ds(at, 16)] = out
         mixed[pl.ds(at, 16)] = (out * jax.nn.sigmoid(out)).astype(BF16)
 
@@ -392,7 +408,7 @@
         left(group)
 
 
-def first_gather(pair, small, cot, tok, gain, taps, bias, masks, rows_sel, n_wt, n_seq, ident):
+def first_gather(pair, small, cot, tok, gain, taps, bias, goes, rows_sel, n_wt, n_seq, ident):
     count, width = cot.shape
     chan = pair.shape[1] // 2
     lines = rows_sel * n_seq
@@ -417,6 +433,7 @@
             pltpu.VMEM((count, width), BF16),
             pltpu.VMEM((n_seq,) + pair.shape, BF16),
             pltpu.VMEM((16 + count, chan), F32),
+            pltpu.VMEM((16 + count, 128), F32),
             pltpu.VMEM((2, 16, chan), BF16),
             pltpu.VMEM((lines, count), F32),
             pltpu.VMEM((n_wt - 1, lines // n_wt, count), F32),
@@ -435,11 +452,23 @@
             collective_id=ident, has_side_effects=True, vmem_limit_bytes=VMEM_BYTES
         ),
         cost_estimate=pl.CostEstimate(flops=10**9, bytes_accessed=10**8, transcendentals=0),
-    )(pair, small, cot, tok, gain[None], taps, bias[None], masks)
-
-
-def ffn_kernel(x, c, wg, wu, wd, gated, acts, down, d_second, acc_down, acc_second):
+    )(pair, small, cot, tok, gain[None], taps, bias[None], goes)
+
+
+def ffn_kernel(cube, x, c, wg, wu, wd, gated, acts, down, d_second, *refs):
+    pieces, refs = refs[:cube], refs[cube:]
+    acc_down, acc_second = refs[:2]
     step = pl.program_id(0)
+    if cube:
+        held, s_spread, s_own = refs[2:]
+        sent, kept = spread_plan(held, pieces[0], s_spread, s_own)
+
+        @pl.when(step == 0)
+        def _():
+            held[...] = x[...]
+            greet(("seq",))
+            for copy in sent + [kept]:
+                copy.start()
 
     @pl.when(step == 0)
     def _():
@@ -465,9 +494,13 @@
     def _():
         down[...] = acc_down[...].astype(BF16)
         d_second[...] = acc_second[...].astype(BF16)
-
-
-def ffn(x, c, w_all, gated):
+        if cube:
+            kept.wait()
+            arrived(sent)
+            left(sent)
+
+
+def ffn(x, c, w_all, gated, cube, n_seq, ident):
     tok, width = x.shape
     units, chan = w_all.shape[1] // 3, gated.shape[1]
     steps = units // UNITS
@@ -475,18 +508,23 @@
     whole = pl.BlockSpec((tok, width), lambda i: (0, 0))
     tile = lambda part: pl.BlockSpec((width, UNITS), lambda i: (0, part * steps + i))
     return pl.pallas_call(
-        ffn_kernel,
+        functools.partial(ffn_kernel, int(cube)),
         grid=(steps,),
         in_specs=[whole, whole, tile(0), tile(1), tile(2)]
         + [pl.BlockSpec((tok, chan // steps), lambda i: (0, i))],
-        out_specs=[pl.BlockSpec((tok, span), lambda i: (0, i)), whole, whole],
+        out_specs=[pl.BlockSpec((tok, span), lambda i: (0, i)), whole, whole] + [ANY] * cube,
         out_shape=[
             jax.ShapeDtypeStruct((tok, 3 * units + chan), BF16),
             jax.ShapeDtypeStruct((tok, width), BF16),
             jax.ShapeDtypeStruct((tok, width), BF16),
-        ],
-        scratch_shapes=[pltpu.VMEM((tok, width), F32)] * 2,
-        compiler_params=pltpu.CompilerParams(vmem_limit_bytes=VMEM_BYTES),
+        ]
+        + [jax.ShapeDtypeStruct((n_seq, tok, width // n_seq), BF16)] * cube,
+        scratch_shapes=[pltpu.VMEM((tok, width), F32)] * 2
+        + ([pltpu.VMEM((tok, width), BF16), pair_sems(n_seq), pltpu.SemaphoreType.DMA] if cube else []),
+        compiler_params=pltpu.CompilerParams(
+            vmem_limit_bytes=VMEM_BYTES,
+            **(dict(collective_id=ident, has_side_effects=True) if cube else {}),
+        ),
         cost_estimate=pl.CostEstimate(
             flops=12 * tok * width * units, bytes_accessed=6 * width * units, transcendentals=0
         ),
@@ -559,7 +597,8 @@
     row0 = me * rows
 
     def body(at):
-        r = tok[pl.ds(at, 16)] + line_summed(part, recv, at, 16, row0)
+        own = tok[pl.ds(pl.multiple_of(row0 + at, 16), 16)].astype(F32)
+        r = own + line_summed(part, recv, at, 16, row0)
         res[pl.ds(at, 16)] = r
         inverse = lax.rsqrt(jnp.mean(r * r, axis=-1, keepdims=True) + EPS)
         out[pl.ds(pl.multiple_of(row0 + at, 16), 16)] = (r * inverse * gain[...]).astype(BF16)
@@ -625,7 +664,7 @@
         grad = line_summed(part, recv, at, 16, row0)
         back, prod = norm_back_rows(grad, res[pl.ds(at, 16)], gain[...])
         gain_grad[...] += prod[:8] + prod[8:]
-        d = cot[pl.ds(at, 16)] + back
+        d = cot[pl.ds(pl.multiple_of(row0 + at, 16), 16)].astype(F32) + back
         d_res[pl.ds(at, 16)] = d
         out[pl.ds(pl.multiple_of(row0 + at, 16), 16)] = d.astype(BF16)
 
@@ -671,12 +710,13 @@
 def last_kernel(cube, part, tok, d_res, gain, gain_grad2, sel, stp, taps, decays, bias3, line, *refs):
     blocks, refs = refs[:cube], refs[cube:]
     if cube:
-        cot_t, second_t, branch_t, acts, refs = refs[0], refs[1], refs[2], refs[3], refs[4:]
-    out, block_out, sel_out, stp_out, chan_out, gains_out = refs[:6]
-    wholes, refs = refs[6 : 6 + cube], refs[6 + cube :]
+        cot_t, second_t, branch_t, first_t, acts = refs[:5]
+        refs = refs[5:]
+    out, block_out, sel_out, stp_out, taps_out, decays_out, *bias_outs = refs[:9]
+    gain_outs, refs = refs[9:11], refs[11:]
     if cube:
-        grad_outs, refs = refs[:4], refs[4:]
-        tile, s_tile, refs = refs[0], refs[1], refs[2:]
+        grad_outs, late_outs, refs = refs[:4], refs[4 : 4 + cube], refs[4 + cube :]
+        tile, s_tile, wholes, refs = refs[0], refs[1], refs[2 : 2 + cube], refs[2 + cube :]
         width = tile.shape[2]
         tiles = acts.shape[1] // width
 
@@ -702,9 +742,9 @@
             return carry
 
         fetch(0, 0).start()
-    recv, pend, recv_sel, recv_stp, recv_chan, pack, gain_buf, recv_gz, recv_gs = refs[:9]
-    s_scatter, s_gather, s_sel, s_stp, s_chan, s_cg, s_gz, s_gs, s_block = refs[9:18]
-    refs = refs[18:]
+    recv, pend, recv_sel, recv_stp, recv_chan, pack, chan_out, gain_buf, recv_gz, recv_gs = refs[:10]
+    s_scatter, s_gather, s_sel, s_stp, s_chan, s_cg, s_gz, s_gs, s_block = refs[10:19]
+    refs = refs[19:]
     me, n_wt = lax.axis_index("wt"), lax.axis_size("wt")
     seq, n_seq = lax.axis_index("seq"), lax.axis_size("seq")
     rows = recv.shape[1]
@@ -736,7 +776,7 @@
         total = src[seq].astype(F32)
         for k in range(n_seq - 1):
             total = total + recv_one[k].astype(F32)
-        one_out[...] = total
+        one_out[...] = total[: one_out.shape[0]]
     total = pack[seq]
     for k in range(n_seq - 1):
         total = total + recv_chan[k]
@@ -751,7 +791,8 @@
 
     def body(at):
         grad = line_summed(part, recv, at, 16, row0)
-        back, prod = norm_back_rows(grad, tok[pl.ds(at, 16)], gain[...])
+        own = tok[pl.ds(pl.multiple_of(row0 + at, 16), 16)].astype(F32)
+        back, prod = norm_back_rows(grad, own, gain[...])
         gain_buf[...] += prod[:8] + prod[8:]
         out[pl.ds(pl.multiple_of(row0 + at, 16), 16)] = (d_res[pl.ds(at, 16)] + back).astype(BF16)
 
@@ -784,41 +825,64 @@
     total = recv_gs[0]
     for pos in range(1, n_seq):
         total = total + recv_gs[pos]
-    gains_out[...] = total
+    for i, gain_out in enumerate(gain_outs):
+        for t in range(high):
+            gain_out[:, t * 128 : (t + 1) * 128] = total[i * high + t : i * high + t + 1]
     arrived(chans)
-    for (one, _, _, kept), two, three in zip(cubes, cubes2, cubes3):
+    outs = [(taps_out, i) for i in range(KC)] + [(decays_out, i) for i in range(NS)]
+    outs += [(bias_out, 0) for bias_out in bias_outs]
+    for at, (ref, i) in enumerate(outs):
+        ref[i : i + 1] = chan_out[at // share, at % share : at % share + 1]
+    for k, ((one, _, whole, kept), two, three) in enumerate(zip(cubes, cubes2, cubes3)):
         cube_end(one, two, three)
         kept.wait()
+
+        def late_tile(j, carry, whole=whole, late_out=late_outs[k]):
+            columns = pl.ds(pl.multiple_of(j * UNITS, UNITS), UNITS)
+            act = whole[:, :, columns].reshape(first_t.shape[1], UNITS)
+            late_out[:, columns] = jnp.dot(first_t[...], act, preferred_element_type=F32)
+            return carry
+
+        lax.fori_loop(0, whole.shape[2] // UNITS, late_tile, 0)
     line_gather_end(second)
     line_gather_end(third)
     for group in (first, second, third, smalls, chans, zs, ss):
         left(group)
 
 
-def last(part, tok_own, d_res, gain, gain_grad2, sel, stp, taps, decays, bias3, line, blocks, more, n_wt, n_seq, ident):
+def last(
+    part, tok_own, d_res, gain, gain_grad2, sel, stp, rows_small, taps, decays, bias3, line,
+    blocks, more, n_wt, n_seq, ident,
+):
     rows, cols = part.shape
     own = rows // n_wt
     chan = taps.shape[1]
     if more:
         deep, tok_all = more[0].shape
-        units = (more[3].shape[1] - chan) // 3
-        span = more[3].shape[1] // (units // UNITS)
+        units = (more[4].shape[1] - chan) // 3
+        span = more[4].shape[1] // (units // UNITS)
     return pl.pallas_call(
         functools.partial(last_kernel, len(blocks)),
         out_shape=[
             jax.ShapeDtypeStruct((rows, cols), BF16),
             jax.ShapeDtypeStruct((rows, cols), BF16),
-            jax.ShapeDtypeStruct(sel.shape[1:], F32),
-            jax.ShapeDtypeStruct(stp.shape[1:], F32),
-            jax.ShapeDtypeStruct((n_seq, 8, chan), F32),
-            jax.ShapeDtypeStruct((2 * cols // 128, 128), F32),
         ]
-        + [jax.ShapeDtypeStruct((n_seq,) + a.shape, BF16) for a in blocks]
-        + ([jax.ShapeDtypeStruct((deep, w), F32) for w in (units, units, units, chan)] if more else []),
-        in_specs=[VMEM] * 11 + [ANY] * len(blocks) + ([VMEM, VMEM, VMEM, ANY] if more else []),
-        out_specs=[VMEM] * 6 + [ANY] * len(blocks) + ([VMEM] * 4 if more else []),
+        + [
+            jax.ShapeDtypeStruct((n, chan), F32)
+            for n in rows_small + (taps.shape[0], decays.shape[0], 1, 1, 1)
+        ]
+        + [jax.ShapeDtypeStruct((1, cols), F32)] * 2
+        + (
+            [jax.ShapeDtypeStruct((deep, w), F32) for w in (units, units, units, chan)]
+            + [jax.ShapeDtypeStruct((deep, a.shape[1]), F32) for a in blocks]
+            if more
+            else []
+        ),
+        in_specs=[VMEM] * 11 + [ANY] * len(blocks) + ([VMEM] * 4 + [ANY] if more else []),
+        out_specs=[VMEM] * (11 + (4 + len(blocks) if more else 0)),
         scratch_shapes=(
             [pltpu.VMEM((2, tok_all, span), BF16), pltpu.SemaphoreType.DMA((2,))]
+            + [pltpu.VMEM((n_seq,) + a.shape, BF16) for a in blocks]
             if more
             else []
         )
@@ -828,6 +892,7 @@
             pltpu.VMEM((n_seq - 1,) + sel.shape[1:], BF16),
             pltpu.VMEM((n_seq - 1,) + stp.shape[1:], BF16),
             pltpu.VMEM((n_seq - 1, 8, chan), F32),
+            pltpu.VMEM((n_seq, 8, chan), F32),
             pltpu.VMEM((n_seq, 8, chan), F32),
             pltpu.VMEM((8, cols), F32),
             pltpu.VMEM((n_wt, 2 * cols // 128, 128), F32),
@@ -848,6 +913,34 @@
         ),
         cost_estimate=pl.CostEstimate(flops=10**6, bytes_accessed=10**8, transcendentals=0),
     )(part, tok_own, d_res, gain[None], gain_grad2, sel, stp, taps, decays, bias3, line, *blocks, *more)
+
+
+def hand_out_kernel(n, *refs):
+    srcs, dsts, held, sems = refs[:n], refs[n : 2 * n], refs[2 * n : 3 * n], refs[3 * n]
+    into = [pltpu.make_async_copy(srcs[i], held[i], sems.at[0, i]) for i in range(n)]
+    away = [pltpu.make_async_copy(held[i], dsts[i], sems.at[1, i]) for i in range(n)]
+    for copy in into:
+        copy.start()
+    for first, second in zip(into, away):
+        first.wait()
+        second.start()
+    for copy in away:
+        copy.wait()
+
+
+def hand_out(arrays):
+    n = len(arrays)
+    size = sum(a.size * a.dtype.itemsize for a in arrays)
+    return pl.pallas_call(
+        functools.partial(hand_out_kernel, n),
+        out_shape=[jax.ShapeDtypeStruct(a.shape, a.dtype) for a in arrays],
+        in_specs=[ANY] * n,
+        out_specs=[ANY] * n,
+        scratch_shapes=[pltpu.VMEM(a.shape, a.dtype) for a in arrays]
+        + [pltpu.SemaphoreType.DMA((2, n))],
+        compiler_params=pltpu.CompilerParams(vmem_limit_bytes=VMEM_BYTES),
+        cost_estimate=pl.CostEstimate(flops=0, bytes_accessed=2 * size, transcendentals=0),
+    )(*arrays)
 
 
 def load(ref):
@@ -1187,9 +1280,6 @@
     )
     if cube:
         fill = jnp.zeros((-(rows_sel + rows_step) % 32, chan), BF16)
-        ones = jnp.ones((tok_count - edge,), F32)
-        columns = [same_back(k)[:, 0] for k in range(1, KC)]
-        columns += [jnp.concatenate([ones, tail_keep])] * (9 - KC)
         (
             w_first, cot_f, first_f, w_small,
             inner_act, prev_rows, switch, conv_out, mixed_in, select,
@@ -1197,7 +1287,7 @@
             jnp.concatenate([inner_proj, switch_proj], axis=1),
             jnp.concatenate([step_proj, select_proj, fill], axis=0),
             cotangent, tokens, premix_gain, conv_taps, conv_bias,
-            jnp.stack(columns, axis=1), rows_sel, n_wt, n_seq, 7,
+            jnp.broadcast_to(goes_on[:, None], (tok_count, 128)), rows_sel, n_wt, n_seq, 7,
         )
         w_first = w_first.reshape(width, 2 * chan)
         w_mix = gather(mixer_out)
@@ -1244,17 +1334,17 @@
     switch_act = jax.nn.silu(switch)
     gated = (scanned * switch_act).astype(BF16)
     mix_part = contract(gated, w_mix, "tc,dc->td").astype(BF16)
-    tokens_own = lax.dynamic_slice_in_dim(tokens, z * own, own, 0).astype(F32)
-    cot_own = lax.dynamic_slice_in_dim(cotangent, z * own, own, 0).astype(F32)
-    second_in, residual = second_norm(mix_part, tokens_own, preffn_gain, n_wt, 2)
+    second_in, residual = second_norm(mix_part, tokens, preffn_gain, n_wt, 2)
     if cube:
         line_up = lambda v: v.reshape(n_seq * tok_count, v.shape[-1])
-        second_in, cot_own, head_keep, cot_t, first_t = lax.optimization_barrier(
-            (second_in, cot_own, head_keep, line_up(cot_f).T, line_up(first_f).T)
+        second_in, head_keep, extended, cot_t, first_t = lax.optimization_barrier(
+            (second_in, head_keep, extended, line_up(cot_f).T, line_up(first_f).T)
         )
-    acts, down_part, d_second = ffn(second_in, cotangent, w_all, gated)
-    d_branch, d_residual, grad_preffn, *second_all = second_back(
-        d_second, residual, cot_own, preffn_gain, (second_in,) if cube else (), n_wt, n_seq, 3
+    acts, down_part, d_second, *second_all = ffn(
+        second_in, cotangent, w_all, gated, cube, n_seq, 8
+    )
+    d_branch, d_residual, grad_preffn = second_back(
+        d_second, residual, cotangent, preffn_gain, (), n_wt, n_seq, 3
     )
     d_gated = contract(d_branch, w_mix, "td,dc->tc")
     d_scanned = d_gated * switch_act
@@ -1320,22 +1410,20 @@
     ).astype(BF16)
     more = ()
     if cube:
-        more = (cot_t, line_up(second_all[0]).T, line_up(branch_all[0]).T, gather(acts))
-    tokens_grad, block_out, out_select, out_step, by_chan, gains, *others = last(
-        d_first, tokens_own, d_residual, premix_gain, grad_preffn,
-        grad_select.reshape(n_seq, -1, chan), grad_step.reshape(n_seq, -1, chan),
+        more = (cot_t, line_up(second_all[0]).T, line_up(branch_all[0]).T, first_t, gather(acts))
+    results = last(
+        d_first, tokens, d_residual, premix_gain, grad_preffn,
+        grad_select.reshape(n_seq, -1, chan), grad_step.reshape(n_seq, -1, chan), (rows_sel, rows_step),
         jnp.stack(taps_rows, axis=0), grad_decay_log,
         jnp.stack([grad_conv_bias, grad_step_bias, grad_skip]), block_own,
         (d_switch, d_inner_low) if cube else (), more, n_wt, n_seq, 6,
     )
-    share = -(-(KC + NS + 3) // n_seq)
-    by_chan = by_chan[:, :share].reshape(n_seq * share, chan)
-    gains = gains.reshape(2, width)
+    (
+        tokens_grad, block_out, out_select, out_step, g_taps, g_decay, g_conv, g_step, g_skip,
+        *others,
+    ) = hand_out(results)
     if cube:
-        out_down, out_gate, out_up, out_mix = others[2:]
-        out_switch, out_inner = grads(
-            (first_t,), (0, 0), (line_up(others[0]), line_up(others[1]))
-        )
+        out_down, out_gate, out_up, out_mix, out_switch, out_inner = others[2:]
     else:
         scatter = lambda v: lax.psum_scatter(v, "seq", scatter_dimension=0, tiled=True)
         by_unit = acts.reshape(tok_count, units // UNITS, -1)
@@ -1351,18 +1439,18 @@
     return (
         block_out,
         tokens_grad,
-        gains[0],
+        others[0][0],
         out_inner,
         out_switch,
-        by_chan[:KC],
-        by_chan[KC + NS],
-        out_select[:rows_sel],
-        out_step[:rows_step],
-        by_chan[KC + NS + 1],
-        by_chan[KC : KC + NS],
-        by_chan[KC + NS + 2],
+        g_taps,
+        g_conv[0],
+        out_select,
+        out_step,
+        g_step[0],
+        g_decay,
+        g_skip[0],
         out_mix,
-        gains[1],
+        others[1][0],
         out_gate,
         out_up,
         out_down,

time: 478 us -> 463 us (0.969)
  local copies, waits for them, and re-layouts: 33.8 us -> 20.6 us
  other arithmetic: 22.6 us -> 14.6 us
    unnamed x77 -> x54, local copies, waits for them, and re-layouts: 14.6 us -> 6.43 us
    pallas_call x2, Pallas kernels: 27.6 us -> 35.7 us  [the longest x1 26.5 us: ffn(): pl.pallas_call(functools.partial(ffn_kernel, int(cube)), grid=(steps,), i...]
  transfers between devices with their start and end apart: 4 -> 4, of which waited for: 2 -> 2; matrix products, arithmetic and copies ran while one was open for 14% -> 13% of each run, Pallas kernels for 58% -> 58%
where the time goes in v5:
time: 463 us; the launch traced here: 462 us
  Pallas kernels  372 us (80%)
  matrix products  25.4 us (5%)
  local copies, waits for them, and re-layouts  20.6 us (4%)
  other arithmetic  14.6 us (3%)
  between operations  14.2 us (3%)
  waiting for transfers between devices  13.2 us (3%)
    pallas_call x1, Pallas kernels, first_gather(): pl.pallas_call(first_kernel, out_shape=[jax.ShapeDtypeStruct((n_seq,) + p...  95.8 us
    pallas_call x1, Pallas kernels, last(): pl.pallas_call(functools.partial(last_kernel, len(blocks)), out_shape=[ja...  68.5 us
    pallas_call x1, Pallas kernels, bwd_scan(): pl.pallas_call(functools.partial(bwd_kernel, len(src)), out_shape=[jax.Sh...  48.9 us
    pallas_call x1, Pallas kernels, second_back(): pl.pallas_call(functools.partial(second_back_kernel, len(srcs)), out_shap...  43.6 us
    pallas_call x1, Pallas kernels, second_norm(): pl.pallas_call(second_norm_kernel, out_shape=[jax.ShapeDtypeStruct((rows,...  41.5 us
    pallas_call x1, Pallas kernels, ffn(): pl.pallas_call(functools.partial(ffn_kernel, int(cube)), grid=(steps,), i...  26.5 us
    dot_general x8, matrix products, contract(): return jnp.einsum(pattern, left_op, right_op, preferred_element_type=F32)  25.4 us
    pallas_call x1, Pallas kernels, fwd_scan(): pl.pallas_call(fwd_kernel, out_shape=[jax.ShapeDtypeStruct((tok, high, 12...  20.3 us
  transfers between devices with their start and end apart: 4, of which 2 were waited for; matrix products, arithmetic and copies ran while one was open for 13% of the time, Pallas kernels for 58%

profile of v5, /device:TPU:0, one launch (start us, length us, event | category | flops | bytes accessed | tf_op | source)
XLA Modules:
  0.0 461.9 jit_solution(2482360613480600783)
XLA Ops:
  7.2 0.7 all-gather.4.cloned.1.call-update
  7.9 0.0 all-gather.6.cloned.1.call-start
  8.0 3.2 pad_maximum_fusion
  11.2 0.0 all-gather.8.cloned.1.call-start
  11.2 0.6 copy-done.24
  11.8 0.5 slice.91
  12.3 0.1 pad.30.clone
  12.4 0.7 maximum_maximum_fusion.small
  13.2 1.1 pad_maximum_fusion.2.pair
  14.2 0.8 broadcast_in_dim.27.goes
  15.0 95.8 %shard_map.305 = (bf16[8,256,2048]{2,1,0:T(8,128)(2,1)}, bf16[8,4,64,256]{3,2,1,0:T(8,128)(2,1)}, bf16[8,4,64,256]{3,2,1,0:T(8,128)(2,1)}, bf16[8,64,1024]{2,1,0...) custom-call(bf16[256,2048]{1,0:T(8,128)(2,1)} %pad_maximum_fusion.2., ...), custom_call_target="tpu_custom_call" | custom-call | flops 1000000000 | bytes 100000000 | tf_op jit(solution)/shard_map/pallas_call | solution.py:416
  110.8 1.0 slice.87
  111.9 1.4 slice.88.wr
  113.2 1.2 convolution_add_fusion.1
  114.5 0.7 fusion.2
  115.2 1.2 copy.46
  116.4 1.2 copy.47
  117.5 0.6 copy.48
  118.2 0.1 convert_element_type.56
  118.3 2.3 copy.40
  120.6 2.3 copy.41
  122.9 20.3 %shard_map.306 = (f32[256,8,128]{2,1,0:T(8,128)}, f32[16,8,128]{2,1,0:T(8,128)}) custom-call(f32[256,8,128]{2,1,0:T(8,128)} %bitcast.94, f32[256,8,128]{2,1,0:T(8,128)} %bitcast.96, f32[32,256]{1,0:T(8,128)} %slice.88.wr, f32[16,8,128]{2,1,0:T(8,128)} %bitcast.108), custom_call_target="tpu_custom_call" | custom-call | flops 100000000 | bytes 80000000 | tf_op jit(solution)/shard_map/pallas_call | solution.py:1027
  143.2 1.1 pad_maximum_fusion.1
  144.3 0.7 fusion.34
  145.1 0.1 copy-done.7
  145.1 0.5 multiply_convert_fusion.1.gated
  145.7 4.6 convolution_convert_fusion.part
  150.3 41.5 %shard_map.307 = (bf16[256,2048]{1,0:T(8,128)(2,1)}, f32[64,2048]{1,0:T(8,128)}) custom-call(bf16[256,2048]{1,0:T(8,128)(2,1)} %convolution_convert_fusion.part, bf16[256,2048]{1,0:T(8,128)(2,1)} %tok.5, f32[1,2048]{1,0:T(1,128)} %bitcast.110), custom_call_target="tpu_custom_call" | custom-call | flops 1000000 | bytes 100000000 | tf_op jit(solution)/shard_map/pallas_call | solution.py:617
  191.8 8.1 %all-gather.6.cloned.1.call-done.wg.wu.wd = bf16[2048,6144]{1,0:T(8,128)(2,1)} async-done(((bf16[256,6144]{1,0:T(8,128)(2,1)}), bf16[2048,6144]{1,0:T(8,128)(2,1)}) %all-gather.6.cloned.1.call-update) | async-done | bytes 25165840 | tf_op jit(solution)/shard_map/all_gather | solution.py:1201
  200.0 26.5 %shard_map.308 = (bf16[256,7168]{1,0:T(8,128)(2,1)}, bf16[256,2048]{1,0:T(8,128)(2,1)}, bf16[256,2048]{1,0:T(8,128)(2,1)}, bf16[8,256,256]{2,1,0:T(8,128)(2,1)}) custom-call(bf16[256,2048]{1,0:T(8,128)(2,1)} %get-tuple-element.93.x, bf16[256,2048]{1,0:T(8,128)(2,1)} %cot.3, bf16[2048,6144]{1,0:T(8,128)(2,1)} %all-gather.6.cloned.1.call-done.wg.wu.wd, ...), custom_call_target="tpu_custom_call" | custom-call | flops 12884901888 | bytes 25165824 | tf_op jit(solution)/shard_map/pallas_call | solution.py:510
  226.5 1.1 slice.93
  227.7 0.1 fusion.31
  227.8 43.6 %shard_map.309 = (bf16[256,2048]{1,0:T(8,128)(2,1)}, f32[64,2048]{1,0:T(8,128)}, f32[8,2048]{1,0:T(8,128)}) custom-call(bf16[256,2048]{1,0:T(8,128)(2,1)} %get-tuple-element.94.part, f32[64,2048]{1,0:T(8,128)} %get-tuple-element.95.res, bf16[256,2048]{1,0:T(8,128)(2,1)} %cot.3, f32[1,2048]{1,0:T(1,128)} %bitcast.111), custom_call_target="tpu_custom_call" | custom-call | flops 1000000 | bytes 100000000 | tf_op jit(solution)/shard_map/pallas_call | solution.py:686
  271.4 5.3 %fusion.6 = (f32[1024]{0:T(1024)S(1)}, f32[256,1024]{1,0:T(8,128)S(1)}, bf16[256,1024]{1,0:T(8,128)(2,1)}) fusion(bf16[256,1024]{1,0:T(8,128)(2,1)S(1)} %copy-done, f32[256,1024]{1,0:T(8,128)S(1)} %copy-done.6, f32[1024]{0:T(1024)S(1)} %copy-done.23, f32[32,8,8,128]{3,2,1,0:T(8,128)} %bitcast.99, bf16[256,2048]{1,0:T(8,128)(2,1)} %get-tuple-element.96.refs_0_, ...), kind=kOutput, calls=%fused_computation.24 | convolution fusion | flops 1078197248 | bytes 9445376 | tf_op jit(solution)/shard_map/td,dc->tc/dot_general | solution.py:1211
  276.7 1.0 copy-done.8
  277.7 1.2 copy.50
  278.8 48.9 %shard_map.310 = (f32[256,8,128]{2,1,0:T(8,128)}, f32[256,8,128]{2,1,0:T(8,128)}, f32[16,8,128]{2,1,0:T(8,128)}, f32[16,512]{1,0:T(8,128)}, bf16[64,2048]{1,0:T(8,128)(2,1)}, /*index=5*/bf16[8,4,64,256]{3,2,1,0:T(8,128)(2,1)}) custom-call(f32[256,8,128]{2,1,0:T(8,128)} %bitcast.95, f32[256,8,128]{2,1,0:T(8,128)} %bitcast.97, f32[32,256]{1,0:T(8,128)} %slice.88.wr, ...), custom_call_target="tpu_custom_call" | custom-call | flops 100000000 | bytes 150000000 | tf_op jit(solution)/shard_map/pallas_call | solution.py:1165
  327.7 0.9 reshape.120
  328.6 0.1 copy.42
  328.7 1.4 broadcast_multiply_fusion
  330.1 0.1 copy-done.3
  330.3 0.7 fusion.36
  331.0 0.3 fusion.27
  331.3 0.7 pad_maximum_fusion.3.part
  332.0 0.1 reshape.122
  332.0 17.9 %shard_map.311 = f32[160,256]{1,0:T(8,128)} custom-call(f32[160,256]{1,0:T(8,128)} %pad_maximum_fusion.3.part), custom_call_target="tpu_custom_call" | custom-call | flops 100000 | bytes 1000000 | tf_op jit(solution)/shard_map/pallas_call | solution.py:573
  350.0 0.9 convert_element_type.58
  351.0 5.2 %fusion.7 = (f32[1024]{0:T(1024)S(1)}, f32[1024]{0:T(1024)S(1)}, f32[1024]{0:T(1024)S(1)}, f32[1024]{0:T(1024)S(1)}, f32[1024]{0:T(1024)S(1)}, /*index=5*/bf16[256,1024]{1,0:T(8,128)(2,1)S(1)}) fusion(f32[259,1024]{1,0:T(8,128)} %pad_maximum_fusion.1, f32[256]{0:T(256)S(1)} %copy-done.20, f32[256]{0:T(256)S(1)} %get-tuple-element.159, ...), kind=kOutput, calls=%fused_computation.25 | convolution fusion | flops 92269568 | bytes 9350144 | tf_op jit(solution)/shard_map/jt,jc->tc/dot_general | solution.py:1211
  356.2 0.1 slice_multiply_fusion.4
  356.3 1.5 collective-permute-start
  357.8 0.6 pad_maximum_fusion.5.bias3
  358.4 0.7 bitcast_multiply_fusion.1.decays
  359.1 0.9 convolution_convert_fusion.3
  360.0 1.1 convolution_convert_fusion.2
  361.1 0.6 pad_maximum_fusion.4.taps
  361.7 2.3 copy.44
  364.0 1.4 copy.45
  365.4 0.1 maximum_convert_fusion
  365.6 0.6 fusion.17.refs_1_
  366.2 0.4 copy-done.10
  366.6 6.7 %convolution_convert_fusion.1.part = bf16[256,2048]{1,0:T(8,128)(2,1)} fusion(bf16[2048,2048]{1,0:T(8,128)(2,1)} %bitcast.131, bf16[256,1024]{1,0:T(8,128)(2,1)S(1)} %copy-done.10, bf16[256,1024]{1,0:T(8,128)(2,1)S(1)} %fusion.17.refs_1_), kind=kOutput, calls=%fused_computation.3 | convolution fusion | flops 2150105088 | bytes 10485760 | tf_op jit(solution)/shard_map/tc,dc->td/dot_general | solution.py:1211
  373.3 4.3 all-gather.8.cloned.1.call-done.refs_6_
  377.6 68.5 %shard_map.312 = (bf16[256,2048]{1,0:T(8,128)(2,1)}, bf16[256,2048]{1,0:T(8,128)(2,1)}, f32[20,1024]{1,0:T(8,128)}, f32[16,1024]{1,0:T(8,128)}, f32[4,1024]{1,0:...) custom-call(bf16[256,2048]{1,0:T(8,128)(2,1)} %convolution_convert_f, ...), custom_call_target="tpu_custom_call" | custom-call | flops 1000000 | bytes 100000000 | tf_op jit(solution)/shard_map/pallas_call | solution.py:864
  446.2 9.2 %shard_map.313 = (bf16[256,2048]{1,0:T(8,128)(2,1)}, bf16[256,2048]{1,0:T(8,128)(2,1)}, f32[20,1024]{1,0:T(8,128)}, f32[16,1024]{1,0:T(8,128)}, f32[4,1024]{1,0:...) custom-call(bf16[256,2048]{1,0:T(8,128)(2,1)} %get-tuple-element.115, ...), custom_call_target="tpu_custom_call" | custom-call | bytes 23584768 | tf_op jit(solution)/shard_map/pallas_call | solution.py:934
  (60 shorter events, 0.3 us)
Async XLA Ops:
  7.2 138.5 %all-gather.4.cloned.1.call-start = ((), (), s32[]{:S(2)}) async-start(), calls=%async_computation | async-start | bytes 4718592 | tf_op jit(solution)/shard_map/all_gather | solution.py:1201
  7.9 192.0 %all-gather.6.cloned.1.call-start = ((), (), s32[]{:S(2)}) async-start(), calls=%async_computation.1 | async-start | bytes 28311552 | tf_op jit(solution)/shard_map/all_gather | solution.py:1201
  11.1 0.7 copy-start.24
  11.1 1.3 copy-start.16
  11.1 1.3 copy-start.17
  11.1 2.0 copy-start.12
  11.2 2.0 copy-start.13
  11.2 366.5 %all-gather.8.cloned.1.call-start = ((), (), s32[]{:S(2)}) async-start(), calls=%async_computation.2 | async-start | bytes 33030144 | tf_op jit(solution)/shard_map/all_gather | solution.py:1201
  11.8 99.0 %copy-start.19 = (f32[256]{0:T(256)}, f32[256]{0:T(256)S(1)}, u32[]{:S(2)}) copy-start(f32[256]{0:T(256)S(1)} %subtract_convert_fusion) | copy-start | bytes 3076
  15.0 98.3 %copy-start.22 = (f32[1024]{0:T(1024)S(1)}, f32[1024]{0:T(1024)}, u32[]{:S(2)}) copy-start(f32[1024]{0:T(1024)} %param.28) | copy-start | bytes 12292
  110.8 3.7 copy-start
  115.2 2.4 copy-start.14
  115.2 3.0 copy-start.11
  116.3 2.0 copy-start.21
  143.2 1.1 copy-start.20
  143.2 1.1 slice-start
  143.2 1.9 copy-start.5
  143.2 1.9 copy-start.7
  143.2 1.9 copy-start.23
  145.6 4.7 %copy-start.2 = (bf16[256,1024]{1,0:T(8,128)(2,1)}, bf16[256,1024]{1,0:T(8,128)(2,1)S(1)}, u32[]{:S(2)}) copy-start(bf16[256,1024]{1,0:T(8,128)(2,1)S(1)} %multiply_convert_fusion.1.gated) | copy-start | bytes 1572868
  226.5 1.2 copy-start.18
  226.5 44.9 %copy-start.6 = (f32[256,1024]{1,0:T(8,128)S(1)}, f32[256,1024]{1,0:T(8,128)}, u32[]{:S(2)}) copy-start(f32[256,1024]{1,0:T(8,128)} %get-tuple-element.87) | copy-start | bytes 3145732
  276.7 1.0 copy-start.8
  328.7 1.6 copy-start.3
  351.0 7.4 %copy-start.15 = (f32[16,8,128]{2,1,0:T(8,128)S(1)}, f32[16,8,128]{2,1,0:T(8,128)}, u32[]{:S(2)}) copy-start(f32[16,8,128]{2,1,0:T(8,128)} %get-tuple-element.108) | copy-start | bytes 196612
  351.0 8.1 %copy-start.9 = (f32[160,256]{1,0:T(8,128)S(1)}, f32[160,256]{1,0:T(8,128)}, u32[]{:S(2)}) copy-start(f32[160,256]{1,0:T(8,128)} %get-tuple-element.83) | copy-start | bytes 491524
  356.3 9.1 %collective-permute-start = (bf16[3,1024]{1,0:T(4,128)(2,1)S(1)}, bf16[3,1024]{1,0:T(4,128)(2,1)S(1)}, u32[]{:S(2)}, u32[]{:S(2)}) collective-permute-start(bf16[3,1024]{1,0:T(4,128)(2,1)S(1)} %slice_multiply_fusion.4), channel_id=1, source_target_pairs={{4,0},{8,4},{12,8},{16,12},{20,16},{24,20},{28,24},{5,1},{9,5},{13... | collective-permute-start | bytes 18440 | tf_op jit(solution)/shard_map/ppermute | solution.py:1207
  359.1 4.9 %copy-start.4 = (bf16[8,256,256]{2,1,0:T(8,128)(2,1)S(1)}, bf16[8,256,256]{2,1,0:T(8,128)(2,1)}, u32[]{:S(2)}) copy-start(bf16[8,256,256]{2,1,0:T(8,128)(2,1)} %get-tuple-element.111) | copy-start | bytes 3145732
  365.5 1.1 copy-start.10
  366.2 7.2 %copy-start.1 = (bf16[256,1024]{1,0:T(8,128)(2,1)}, bf16[256,1024]{1,0:T(8,128)(2,1)S(1)}, u32[]{:S(2)}) copy-start(bf16[256,1024]{1,0:T(8,128)(2,1)S(1)} %fusion.17.refs_1_) | copy-start | bytes 1572868
Sparse Core Ops, SparseCore 0:
  9.9 59.2 all-gather.3
  71.1 128.8 all-gather.5
  226.6 150.9 all-gather.7

commit v6 on v5

--- a/solution.py
+++ b/solution.py
@@ -295,8 +295,21 @@
     return [send(lines, lines, sems, k - 1, "wt", lax.rem(z + k, n_wt)) for k in range(1, n_wt)]
 
 
+def pass_pairs(dst, sems):
+    z, mate, far, _ = mates()
+    lines = dst.at[:, z]
+    return [send(lines, lines, sems, 0, "wt", far), send(lines, lines, sems, 1, "wt", mate)]
+
+
+def pass_pairs_on(dst, sems, copies):
+    _, mate, far, _ = mates()
+    copies[0].wait_recv()
+    lines = dst.at[:, far]
+    return copies + [send(lines, lines, sems, 2, "wt", mate)]
+
+
 def first_kernel(
-    pair, small, cot, tok, gain, taps, bias, goes,
+    left_w, right_w, small, cot, tok, gain, taps, bias, goes,
     w_first, cot_f, act_f, w_small, inner, prev, switch, conv, mixed, select,
     first_in, w_near, ext, before, halo, part, recv,
     s_pair, s_small, s_own, s_cot, s_act, s_cz, s_az, s_halo, s_scatter, s_gather,
@@ -305,7 +318,15 @@
     me = lax.axis_index("wt")
     count, width = tok.shape
     chan = inner.shape[1]
-    kept = [keep(pair, w_near, s_own.at[0]), keep(small, w_small, s_own.at[1])]
+    half = left_w.shape[1]
+    own_block = w_near.at[seq]
+    placed = [
+        pltpu.make_async_copy(left_w, own_block.at[:, pl.ds(0, half)], s_own.at[0]),
+        pltpu.make_async_copy(right_w, own_block.at[:, pl.ds(half, half)], s_own.at[4]),
+    ]
+    for copy in placed:
+        copy.start()
+    kept = [keep(small, w_small, s_own.at[1])]
 
     def norm(at):
         v = tok[pl.ds(at, 16)].astype(F32)
@@ -317,7 +338,9 @@
     little = cube_first(small, w_small, s_small)
     sent1, kept1 = share(cot, cot_f, s_cot, s_own.at[2])
     sent2, kept2 = share(first_in, act_f, s_act, s_own.at[3])
-    pair1 = cube_first(pair, w_near, s_pair)
+    for copy in placed:
+        copy.wait()
+    pair1 = cube_first(own_block, w_near, s_pair)
     sent = sent1 + sent2
     arrived(sent)
     kept1.wait()
@@ -408,15 +431,16 @@
         left(group)
 
 
-def first_gather(pair, small, cot, tok, gain, taps, bias, goes, rows_sel, n_wt, n_seq, ident):
+def first_gather(left_w, right_w, small, cot, tok, gain, taps, bias, goes, rows_sel, n_wt, n_seq, ident):
     count, width = cot.shape
-    chan = pair.shape[1] // 2
+    rows, chan = left_w.shape
+    pair_shape = (n_seq, rows, 2 * chan)
     lines = rows_sel * n_seq
     share_shape = jax.ShapeDtypeStruct((n_seq, n_wt, count // n_wt, width // n_seq), BF16)
     return pl.pallas_call(
         first_kernel,
         out_shape=[
-            jax.ShapeDtypeStruct((n_seq,) + pair.shape, BF16),
+            jax.ShapeDtypeStruct(pair_shape, BF16),
             share_shape,
             share_shape,
             jax.ShapeDtypeStruct((n_seq,) + small.shape, BF16),
@@ -427,11 +451,11 @@
             jax.ShapeDtypeStruct((count, chan), BF16),
             jax.ShapeDtypeStruct((lines, count), F32),
         ],
-        in_specs=[ANY] * 2 + [VMEM] * 6,
+        in_specs=[ANY] * 3 + [VMEM] * 6,
         out_specs=[ANY] * 3 + [VMEM] * 7,
         scratch_shapes=[
             pltpu.VMEM((count, width), BF16),
-            pltpu.VMEM((n_seq,) + pair.shape, BF16),
+            pltpu.VMEM(pair_shape, BF16),
             pltpu.VMEM((16 + count, chan), F32),
             pltpu.VMEM((16 + count, 128), F32),
             pltpu.VMEM((2, 16, chan), BF16),
@@ -439,7 +463,7 @@
             pltpu.VMEM((n_wt - 1, lines // n_wt, count), F32),
             cube_sems(),
             cube_sems(),
-            pltpu.SemaphoreType.DMA((4,)),
+            pltpu.SemaphoreType.DMA((5,)),
             pair_sems(n_seq),
             pair_sems(n_seq),
             pair_sems(n_wt),
@@ -452,7 +476,7 @@
             collective_id=ident, has_side_effects=True, vmem_limit_bytes=VMEM_BYTES
         ),
         cost_estimate=pl.CostEstimate(flops=10**9, bytes_accessed=10**8, transcendentals=0),
-    )(pair, small, cot, tok, gain[None], taps, bias[None], goes)
+    )(left_w, right_w, small, cot, tok, gain[None], taps, bias[None], goes)
 
 
 def ffn_kernel(cube, x, c, wg, wu, wd, gated, acts, down, d_second, *refs):
@@ -751,6 +775,11 @@
     block_out[pl.ds(pl.multiple_of(me * rows, 16), rows)] = line[...]
     greet(("wt", "seq"))
     first = line_scatter_start(part, recv, s_scatter)
+    cubes = []
+    for i in range(cube):
+        s_cube, s_own = refs[2 * i : 2 * i + 2]
+        cubes.append([cube_first(blocks[i], wholes[i], s_cube), s_cube, wholes[i]])
+        cubes[-1].append(keep(blocks[i], wholes[i], s_own))
     share = -(-(KC + NS + 3) // n_seq)
     lines = [(taps, i) for i in range(KC)] + [(decays, i) for i in range(NS)]
     lines += [(bias3, i) for i in range(3)]
@@ -761,16 +790,35 @@
         for k in range(1, n_seq):
             peer = lax.rem(seq + k, n_seq)
             smalls.append(send(src.at[peer], dst.at[k - 1], sems, k - 1, "seq", peer))
-    cubes = []
-    for i in range(cube):
-        s_cube, s_own = refs[2 * i : 2 * i + 2]
-        cubes.append([cube_first(blocks[i], wholes[i], s_cube), s_cube, wholes[i]])
-        cubes[-1].append(keep(blocks[i], wholes[i], s_own))
     if cube:
         lax.fori_loop(0, 3, one_tile, 0)
     first = line_scatter_mid(part, recv, pend, s_scatter, first)
     if cube:
         lax.fori_loop(3, tiles - 2, one_tile, 0)
+    line_scatter_end(first)
+    row0 = me * rows
+    gain_buf[...] = jnp.zeros_like(gain_buf)
+
+    def body(at):
+        grad = line_summed(part, recv, at, 16, row0)
+        own = tok[pl.ds(pl.multiple_of(row0 + at, 16), 16)].astype(F32)
+        back, prod = norm_back_rows(grad, own, gain[...])
+        gain_buf[...] += prod[:8] + prod[8:]
+        out[pl.ds(pl.multiple_of(row0 + at, 16), 16)] = (d_res[pl.ds(at, 16)] + back).astype(BF16)
+
+    step_rows(rows, 16, body)
+    second = line_gather_start(out, rows, s_gather)
+    third = line_gather_start(block_out, rows, s_block)
+    high = recv_gz.shape[1] // 2
+    for i, grad in enumerate((gain_buf, gain_grad2)):
+        line = jnp.sum(grad[...], axis=0, keepdims=True)
+        for t in range(high):
+            recv_gz[me, i * high + t : i * high + t + 1] = line[:, t * 128 : (t + 1) * 128]
+    mine_z = recv_gz.at[me]
+    zs = [send(mine_z, mine_z, s_gz, k - 1, "wt", lax.rem(me + k, n_wt)) for k in range(1, n_wt)]
+    cubes2 = [cube_second(whole, sems, one) for one, sems, whole, _ in cubes]
+    if cube:
+        lax.fori_loop(tiles - 2, tiles, one_tile, 0)
     arrived(smalls)
     for src, recv_one, one_out in ((sel, recv_sel, sel_out), (stp, recv_stp, stp_out)):
         total = src[seq].astype(F32)
@@ -785,30 +833,6 @@
     chans = [
         send(mine, mine, s_cg, k - 1, "seq", lax.rem(seq + k, n_seq)) for k in range(1, n_seq)
     ]
-    line_scatter_end(first)
-    row0 = me * rows
-    gain_buf[...] = jnp.zeros_like(gain_buf)
-
-    def body(at):
-        grad = line_summed(part, recv, at, 16, row0)
-        own = tok[pl.ds(pl.multiple_of(row0 + at, 16), 16)].astype(F32)
-        back, prod = norm_back_rows(grad, own, gain[...])
-        gain_buf[...] += prod[:8] + prod[8:]
-        out[pl.ds(pl.multiple_of(row0 + at, 16), 16)] = (d_res[pl.ds(at, 16)] + back).astype(BF16)
-
-    step_rows(rows, 16, body)
-    second = line_gather_start(out, rows, s_gather)
-    third = line_gather_start(block_out, rows, s_block)
-    high = recv_gz.shape[1] // 2
-    for i, grad in enumerate((gain_buf, gain_grad2)):
-        line = jnp.sum(grad[...], axis=0, keepdims=True)
-        for t in range(high):
-            recv_gz[me, i * high + t : i * high + t + 1] = line[:, t * 128 : (t + 1) * 128]
-    mine_z = recv_gz.at[me]
-    zs = [send(mine_z, mine_z, s_gz, k - 1, "wt", lax.rem(me + k, n_wt)) for k in range(1, n_wt)]
-    cubes2 = [cube_second(whole, sems, one) for one, sems, whole, _ in cubes]
-    if cube:
-        lax.fori_loop(tiles - 2, tiles, one_tile, 0)
     second = line_gather_mid(out, rows, s_gather, second)
     third = line_gather_mid(block_out, rows, s_block, third)
     arrived(zs)
@@ -1047,20 +1071,23 @@
 
 
 def bwd_kernel(
-    cube, sa, dx, wr, do, a2, h0, part, res, *refs
+    cube, sa, dx, wr, do_flat, a2, h0, part, res, *refs
 ):
     src, refs = refs[:cube], refs[cube:]
     along, ds2, grad_a, sums, out = refs[:5]
     dst, refs = refs[5 : 5 + cube], refs[5 + cube :]
-    hs, qw, qr, pw, pr, g0, mine, recv, recv_z, box, s_scatter = refs[:11]
+    hs, qw, qr, pw, pr, g0, mine, recv, recv_z, pend, do, al2, d22, box, s_scatter = refs[:15]
     tok = sa.shape[0]
     chunk = qw.shape[0] // (NS * 8)
+    high = sa.shape[1]
+    for c in range(high):
+        do[pl.ds(c, tok, stride=high), :] = do_flat[:, c * 128 : (c + 1) * 128]
     greet(("wt", "seq"))
-    first = scatter_start(part, recv_z, s_scatter, "wt")
+    first = line_scatter_start(part, recv_z, s_scatter)
 
     def end(i, carry):
         t = tok - 1 - i
-        s, d = sa[t], do[t]
+        s, d = sa[t], do[pl.ds(pl.multiple_of(t * high, high), high), :]
         g, total = carry
         return (
             tuple(jnp.exp2(s * a2[n]) * (g[n] + wr[NS + n, t] * d) for n in range(NS)),
@@ -1073,8 +1100,9 @@
     mine[NS] = total
     hand_on(mine, recv, box, True)
     if cube:
-        s_seq, s_wt, s_own = refs[11:]
+        s_seq, s_wt, s_own = refs[15:]
         sent, kept = share(src[0], dst[0], s_seq, s_own)
+    first = line_scatter_mid(part, recv_z, pend, s_scatter, first)
 
     def again(t, h):
         s, d = sa[t], dx[t]
@@ -1090,7 +1118,7 @@
     if cube:
         arrived(sent)
         kept.wait()
-        passed = pass_along(dst[0], s_wt)
+        passed = pass_pairs(dst[0], s_wt)
     grad_a[...] = jnp.zeros_like(grad_a)
 
     def one_chunk(j, g):
@@ -1099,7 +1127,7 @@
         def body(i, g):
             at = chunk - 1 - i
             t = base + at
-            s, d, o = sa[t], dx[t], do[t]
+            s, d, o = sa[t], dx[t], do[pl.ds(pl.multiple_of(t * high, high), high), :]
             al = d2 = None
             new = []
             for n in range(NS):
@@ -1118,8 +1146,8 @@
                 row = pl.multiple_of((at * NS + n) * 8, 8)
                 qw[pl.ds(row, 8), :] = gn * d
                 qr[pl.ds(row, 8), :] = hn * o
-            along[t] = al
-            ds2[t] = d2
+            al2[pl.ds(pl.multiple_of(at * high, high), high), :] = al
+            d22[pl.ds(pl.multiple_of(at * high, high), high), :] = d2
             return tuple(new)
 
         g = lax.fori_loop(0, chunk, body, g)
@@ -1133,27 +1161,36 @@
             return carry
 
         lax.fori_loop(0, chunk, lanes, 0, unroll=4)
+        lines = pl.ds(pl.multiple_of(base, chunk), chunk)
+        for c in range(high):
+            columns = slice(c * 128, (c + 1) * 128)
+            along[lines, columns] = al2[pl.ds(c, chunk, stride=high), :]
+            ds2[lines, columns] = d22[pl.ds(c, chunk, stride=high), :]
         ones = jnp.ones((8, 128), BF16)
         for which, p in enumerate((pw, pr)):
-            high = p[...].astype(BF16)
-            low = (p[...] - high.astype(F32)).astype(BF16)
+            upper = p[...].astype(BF16)
+            lower = (p[...] - upper.astype(F32)).astype(BF16)
             row = which * (tok // chunk) + base // chunk
-            sums[pl.ds(row, 1), :] = (nt(ones, high) + nt(ones, low))[:1]
+            sums[pl.ds(row, 1), :] = (nt(ones, upper) + nt(ones, lower))[:1]
         return g
 
-    lax.fori_loop(0, tok // chunk, one_chunk, load(g0))
+    half = tok // chunk // 2
+    g = lax.fori_loop(0, half, one_chunk, load(g0))
+    if cube:
+        passed = pass_pairs_on(dst[0], s_wt, passed)
+    lax.fori_loop(half, tok // chunk, one_chunk, g)
     handed(mine, recv, box, True)
-    arrived(first)
+    line_scatter_end(first)
     rows = recv_z.shape[1]
     row0 = lax.axis_index("wt") * rows
 
     def block_rows(at):
-        out[pl.ds(at, 16)] = (res[pl.ds(at, 16)] + summed(part, recv_z, at, 16, row0)).astype(BF16)
+        out[pl.ds(at, 16)] = (res[pl.ds(at, 16)] + line_summed(part, recv_z, at, 16, row0)).astype(BF16)
 
     step_rows(rows, 16, block_rows)
     left(first)
     if cube:
-        arrived(passed)
+        arrived(passed[1:])
         left(sent)
         left(passed)
 
@@ -1165,8 +1202,8 @@
     return pl.pallas_call(
         functools.partial(bwd_kernel, len(src)),
         out_shape=[
-            jax.ShapeDtypeStruct((tok, high, 128), F32),
-            jax.ShapeDtypeStruct((tok, high, 128), F32),
+            jax.ShapeDtypeStruct((tok, high * 128), F32),
+            jax.ShapeDtypeStruct((tok, high * 128), F32),
             jax.ShapeDtypeStruct((NS, high, 128), F32),
             jax.ShapeDtypeStruct((2 * tok // chunk, chunk * NS), F32),
             jax.ShapeDtypeStruct((rows // n_wt, cols), BF16),
@@ -1184,6 +1221,10 @@
             pltpu.VMEM((NS + 1, high, 128), F32),
             pltpu.VMEM((n_seq - 1, NS + 1, high, 128), F32),
             pltpu.VMEM((n_wt - 1, rows // n_wt, cols), BF16),
+            pltpu.VMEM((rows // n_wt, cols), BF16),
+            pltpu.VMEM((tok * high, 128), F32),
+            pltpu.VMEM((chunk * high, 128), F32),
+            pltpu.VMEM((chunk * high, 128), F32),
             pair_sems(n_seq),
             pair_sems(n_wt),
         ]
@@ -1251,7 +1292,7 @@
     n_seq, n_wt = lax.axis_size("seq"), lax.axis_size("wt")
     z = lax.axis_index("wt")
     own = tok_count // n_wt
-    cube = n_seq == 8 and n_seq * tok_count <= width
+    cube = n_seq == 8 and n_wt == 4 and n_seq * tok_count <= width
 
     rows_sel, rows_step = select_proj.shape[0], step_proj.shape[0]
     goes_on = (1 - doc_start).astype(F32)
@@ -1284,7 +1325,7 @@
             w_first, cot_f, first_f, w_small,
             inner_act, prev_rows, switch, conv_out, mixed_in, select,
         ) = first_gather(
-            jnp.concatenate([inner_proj, switch_proj], axis=1),
+            inner_proj, switch_proj,
             jnp.concatenate([step_proj, select_proj, fill], axis=0),
             cotangent, tokens, premix_gain, conv_taps, conv_bias,
             jnp.broadcast_to(goes_on[:, None], (tok_count, 128)), rows_sel, n_wt, n_seq, 7,
@@ -1351,11 +1392,10 @@
     d_switch = (d_gated * scanned * silu_slope(switch)).astype(BF16)
     grad_skip = jnp.sum(d_scanned * mixed_f, axis=0)
     along, through_sum, grad_decay, d_write_read, block_own, *branch_all = bwd_scan(
-        step_a, drive, write_read, tiles(d_scanned), decay2, carried_in,
+        step_a, drive, write_read, d_scanned, decay2, carried_in,
         down_part, residual, (d_branch,) if cube else (), n_wt, n_seq, 4,
     )
-    along = flat(along)
-    d_step = along * mixed_f + flat(through_sum) * (1.0 / LOG2E)
+    d_step = along * mixed_f + through_sum * (1.0 / LOG2E)
     grad_decay_log = flat(grad_decay) * decay
     d_pre = d_step * jax.nn.sigmoid(step_pre)
     grad_step_bias = jnp.sum(d_pre, axis=0)

time: 463 us -> 462 us (level)
    pallas_call x1, Pallas kernels: 17.9 us -> 13 us  [wt_sum(): pl.pallas_call(wt_sum_kernel, out_shape=jax.ShapeDtypeStruct((rows, cols)...]
where the time goes in v6:
time: 462 us; the launch traced here: 461 us
  Pallas kernels  372 us (81%)
  matrix products  26.4 us (6%)
  local copies, waits for them, and re-layouts  17.8 us (4%)
  other arithmetic  16 us (3%)
  between operations  14.1 us (3%)
  waiting for transfers between devices  13.2 us (3%)
    pallas_call x1, Pallas kernels, first_gather(): pl.pallas_call(first_kernel, out_shape=[jax.ShapeDtypeStruct(pair_shape,...  95.9 us
    pallas_call x1, Pallas kernels, last(): pl.pallas_call(functools.partial(last_kernel, len(blocks)), out_shape=[ja...  68.2 us
    pallas_call x1, Pallas kernels, bwd_scan(): pl.pallas_call(functools.partial(bwd_kernel, len(src)), out_shape=[jax.Sh...  52.6 us
    pallas_call x1, Pallas kernels, second_back(): pl.pallas_call(functools.partial(second_back_kernel, len(srcs)), out_shap...  43.6 us
    pallas_call x1, Pallas kernels, second_norm(): pl.pallas_call(second_norm_kernel, out_shape=[jax.ShapeDtypeStruct((rows,...  41.6 us
    pallas_call x1, Pallas kernels, ffn(): pl.pallas_call(functools.partial(ffn_kernel, int(cube)), grid=(steps,), i...  26.5 us
    dot_general x8, matrix products, contract(): return jnp.einsum(pattern, left_op, right_op, preferred_element_type=F32)  26.4 us
    pallas_call x1, Pallas kernels, fwd_scan(): pl.pallas_call(fwd_kernel, out_shape=[jax.ShapeDtypeStruct((tok, high, 12...  21 us
  transfers between devices with their start and end apart: 4, of which 2 were waited for; matrix products, arithmetic and copies ran while one was open for 13% of the time, Pallas kernels for 58%

profile of v6, /device:TPU:0, one launch (start us, length us, event | category | flops | bytes accessed | tf_op | source)
XLA Modules:
  0.0 460.9 jit_solution(7560466248755871684)
XLA Ops:
  7.2 0.0 all-gather.4.cloned.1.call-start
  7.2 0.7 all-gather.4.cloned.1.call-update
  7.9 0.0 all-gather.6.cloned.1.call-start
  8.0 3.2 pad_maximum_fusion
  11.2 0.0 copy-start.18
  11.2 0.0 all-gather.6.cloned.1.call-update
  11.2 0.0 all-gather.8.cloned.1.call-start
  11.3 0.6 copy-done.20
  11.9 0.5 slice.91
  12.4 0.1 pad.30.clone
  12.5 0.7 maximum_maximum_fusion.small
  13.2 0.8 broadcast_in_dim.27.goes
  14.0 95.9 %shard_map.305 = (bf16[8,256,2048]{2,1,0:T(8,128)(2,1)}, bf16[8,4,64,256]{3,2,1,0:T(8,128)(2,1)}, bf16[8,4,64,256]{3,2,1,0:T(8,128)(2,1)}, bf16[8,64,1024]{2,1,0...) custom-call(bf16[256,1024]{1,0:T(8,128)(2,1)} %left_w.1, ...), custom_call_target="tpu_custom_call" | custom-call | flops 1000000000 | bytes 100000000 | tf_op jit(solution)/shard_map/pallas_call | solution.py:440
  109.8 1.0 slice.87
  110.8 1.4 slice.88.wr
  112.2 1.2 convolution_add_fusion.1
  113.4 1.8 fusion.2
  115.2 1.2 copy.46
  116.4 1.2 copy.47
  117.6 0.6 copy.48
  118.2 0.1 convert_element_type.56
  118.4 2.3 copy.40
  120.6 2.3 copy.41
  122.9 21.0 %shard_map.306 = (f32[256,8,128]{2,1,0:T(8,128)}, f32[16,8,128]{2,1,0:T(8,128)}) custom-call(f32[256,8,128]{2,1,0:T(8,128)} %bitcast.76, f32[256,8,128]{2,1,0:T(8,128)} %bitcast.78, f32[32,256]{1,0:T(8,128)} %slice.88.wr, f32[16,8,128]{2,1,0:T(8,128)} %bitcast.88), custom_call_target="tpu_custom_call" | custom-call | flops 100000000 | bytes 80000000 | tf_op jit(solution)/shard_map/pallas_call | solution.py:1051
  143.9 1.1 pad_maximum_fusion.1
  145.0 0.7 fusion.33
  145.8 2.0 multiply_convert_fusion.1.gated
  147.7 0.0 copy-start.2
  147.8 0.0 all-gather.4.cloned.1.call-done
  147.8 4.6 %convolution_convert_fusion.part = bf16[256,2048]{1,0:T(8,128)(2,1)} fusion(bf16[256,1024]{1,0:T(8,128)(2,1)S(1)} %multiply_convert_fusion.1.gated, bf16[2048,1024]{1,0:T(8,128)(2,1)} %all-gather.4.cloned.1.call-done), kind=kOutput, calls=%fused_computation.2 | convolution fusion | flops 1074266112 | bytes 5767168 | tf_op jit(solution)/shard_map/tc,dc->td/dot_general | solution.py:1252
  152.4 41.6 %shard_map.307 = (bf16[256,2048]{1,0:T(8,128)(2,1)}, f32[64,2048]{1,0:T(8,128)}) custom-call(bf16[256,2048]{1,0:T(8,128)(2,1)} %convolution_convert_fusion.part, bf16[256,2048]{1,0:T(8,128)(2,1)} %tok.5, f32[1,2048]{1,0:T(1,128)} %bitcast.90), custom_call_target="tpu_custom_call" | custom-call | flops 1000000 | bytes 100000000 | tf_op jit(solution)/shard_map/pallas_call | solution.py:641
  194.0 5.3 %all-gather.6.cloned.1.call-done.wg.wu.wd = bf16[2048,6144]{1,0:T(8,128)(2,1)} async-done(((bf16[256,6144]{1,0:T(8,128)(2,1)}), bf16[2048,6144]{1,0:T(8,128)(2,1)}) %all-gather.6.cloned.1.call-update) | async-done | bytes 25165840 | tf_op jit(solution)/shard_map/all_gather | solution.py:1242
  199.3 26.5 %shard_map.308 = (bf16[256,7168]{1,0:T(8,128)(2,1)}, bf16[256,2048]{1,0:T(8,128)(2,1)}, bf16[256,2048]{1,0:T(8,128)(2,1)}, bf16[8,256,256]{2,1,0:T(8,128)(2,1)}) custom-call(bf16[256,2048]{1,0:T(8,128)(2,1)} %get-tuple-element.93.x, bf16[256,2048]{1,0:T(8,128)(2,1)} %cot.3, bf16[2048,6144]{1,0:T(8,128)(2,1)} %all-gather.6.cloned.1.call-done.wg.wu.wd, ...), custom_call_target="tpu_custom_call" | custom-call | flops 12884901888 | bytes 25165824 | tf_op jit(solution)/shard_map/pallas_call | solution.py:534
  225.8 0.0 all-gather.8.cloned.1.call-update
  225.9 1.0 slice.93
  226.9 0.1 fusion.30
  227.0 43.6 %shard_map.309 = (bf16[256,2048]{1,0:T(8,128)(2,1)}, f32[64,2048]{1,0:T(8,128)}, f32[8,2048]{1,0:T(8,128)}) custom-call(bf16[256,2048]{1,0:T(8,128)(2,1)} %get-tuple-element.94.part, f32[64,2048]{1,0:T(8,128)} %get-tuple-element.95.res, bf16[256,2048]{1,0:T(8,128)(2,1)} %cot.3, f32[1,2048]{1,0:T(1,128)} %bitcast.91), custom_call_target="tpu_custom_call" | custom-call | flops 1000000 | bytes 100000000 | tf_op jit(solution)/shard_map/pallas_call | solution.py:710
  270.6 6.0 %fusion.6 = (f32[1024]{0:T(1024)S(1)}, f32[256,1024]{1,0:T(8,128)}, bf16[256,1024]{1,0:T(8,128)(2,1)}) fusion(bf16[256,1024]{1,0:T(8,128)(2,1)S(1)} %copy-done, f32[256,1024]{1,0:T(8,128)} %get-tuple-element.87, f32[1024]{0:T(1024)S(1)} %copy-done.19, f32[32,8,8,128]{3,2,1,0:T(8,128)} %bitcast.82, bf16[256,2048]{1,0:T(8,128)(2,1)} %get-tuple-element.96.refs_0_, ...), kind=kOutput, calls=%fused_computation.24 | convolution fusion | flops 1078197248 | bytes 9445376 | tf_op jit(solution)/shard_map/td,dc->tc/dot_general | solution.py:1252
  276.6 52.6 %shard_map.310 = (f32[256,1024]{1,0:T(8,128)}, f32[256,1024]{1,0:T(8,128)}, f32[16,8,128]{2,1,0:T(8,128)}, f32[16,512]{1,0:T(8,128)}, bf16[64,2048]{1,0:T(8,128)(2,1)}, /*index=5*/bf16[8,4,64,256]{3,2,1,0:T(8,128)(2,1)}) custom-call(f32[256,8,128]{2,1,0:T(8,128)} %bitcast.77, f32[256,8,128]{2,1,0:T(8,128)} %bitcast.79, f32[32,256]{1,0:T(8,128)} %slice.88.wr, ...), custom_call_target="tpu_custom_call" | custom-call | flops 100000000 | bytes 150000000 | tf_op jit(solution)/shard_map/pallas_call | solution.py:1202
  329.2 0.9 reshape.109
  330.1 0.1 copy.42
  330.2 2.0 fusion.35
  332.2 0.3 fusion.26
  332.5 0.7 pad_maximum_fusion.2.part
  333.2 0.8 reshape.111
  334.0 13.0 %shard_map.311 = f32[160,256]{1,0:T(8,128)} custom-call(f32[160,256]{1,0:T(8,128)} %pad_maximum_fusion.2.part), custom_call_target="tpu_custom_call" | custom-call | flops 100000 | bytes 1000000 | tf_op jit(solution)/shard_map/pallas_call | solution.py:597
  347.0 0.9 convert_element_type.58
  348.0 5.4 %fusion.7 = (f32[1024]{0:T(1024)S(1)}, f32[1024]{0:T(1024)S(1)}, f32[1024]{0:T(1024)S(1)}, f32[1024]{0:T(1024)S(1)}, f32[1024]{0:T(1024)S(1)}, /*index=5*/bf16[256,1024]{1,0:T(8,128)(2,1)S(1)}) fusion(f32[259,1024]{1,0:T(8,128)} %pad_maximum_fusion.1, f32[256]{0:T(256)S(1)} %copy-done.16, f32[256]{0:T(256)S(1)} %get-tuple-element.159, ...), kind=kOutput, calls=%fused_computation.25 | convolution fusion | flops 92269568 | bytes 9350144 | tf_op jit(solution)/shard_map/jt,jc->tc/dot_general | solution.py:1252
  353.4 0.1 slice_multiply_fusion.4
  353.5 1.6 collective-permute-start
  355.1 0.6 pad_maximum_fusion.4.bias3
  355.8 0.7 bitcast_multiply_fusion.decays
  356.4 0.9 convolution_convert_fusion.3
  357.4 1.1 convolution_convert_fusion.2
  358.5 0.6 pad_maximum_fusion.3.taps
  359.1 1.4 copy.44
  360.5 1.4 copy.45
  361.9 0.1 maximum_convert_fusion
  362.1 0.6 fusion.16.refs_1_
  362.7 0.3 copy-done.8
  363.0 6.9 %convolution_convert_fusion.1.part = bf16[256,2048]{1,0:T(8,128)(2,1)} fusion(bf16[2048,2048]{1,0:T(8,128)(2,1)} %bitcast.111, bf16[256,1024]{1,0:T(8,128)(2,1)S(1)} %copy-done.8, bf16[256,1024]{1,0:T(8,128)(2,1)S(1)} %fusion.16.refs_1_), kind=kOutput, calls=%fused_computation.3 | convolution fusion | flops 2150105088 | bytes 10485760 | tf_op jit(solution)/shard_map/tc,dc->td/dot_general | solution.py:1252
  369.9 7.1 %all-gather.8.cloned.1.call-done.refs_6_ = bf16[2048,7168]{1,0:T(8,128)(2,1)} async-done(((bf16[256,7168]{1,0:T(8,128)(2,1)}), bf16[2048,7168]{1,0:T(8,128)(2,1)}) %all-gather.8.cloned.1.call-update) | async-done | bytes 29360144 | tf_op jit(solution)/shard_map/all_gather | solution.py:1242
  377.0 68.2 %shard_map.312 = (bf16[256,2048]{1,0:T(8,128)(2,1)}, bf16[256,2048]{1,0:T(8,128)(2,1)}, f32[20,1024]{1,0:T(8,128)}, f32[16,1024]{1,0:T(8,128)}, f32[4,1024]{1,0:...) custom-call(bf16[256,2048]{1,0:T(8,128)(2,1)} %convolution_convert_f, ...), custom_call_target="tpu_custom_call" | custom-call | flops 1000000 | bytes 100000000 | tf_op jit(solution)/shard_map/pallas_call | solution.py:888
  445.2 9.2 %shard_map.313 = (bf16[256,2048]{1,0:T(8,128)(2,1)}, bf16[256,2048]{1,0:T(8,128)(2,1)}, f32[20,1024]{1,0:T(8,128)}, f32[16,1024]{1,0:T(8,128)}, f32[4,1024]{1,0:...) custom-call(bf16[256,2048]{1,0:T(8,128)(2,1)} %get-tuple-element.115, ...), custom_call_target="tpu_custom_call" | custom-call | bytes 23584768 | tf_op jit(solution)/shard_map/pallas_call | solution.py:958
  (49 shorter events, 0.2 us)
Async XLA Ops:
  7.2 140.6 %all-gather.4.cloned.1.call-start = ((), (), s32[]{:S(2)}) async-start(), calls=%async_computation | async-start | bytes 4718592 | tf_op jit(solution)/shard_map/all_gather | solution.py:1242
  7.9 191.4 %all-gather.6.cloned.1.call-start = ((), (), s32[]{:S(2)}) async-start(), calls=%async_computation.1 | async-start | bytes 28311552 | tf_op jit(solution)/shard_map/all_gather | solution.py:1242
  11.2 0.7 copy-start.20
  11.2 1.3 copy-start.12
  11.2 1.3 copy-start.13
  11.2 101.0 %copy-start.18 = (f32[1024]{0:T(1024)S(1)}, f32[1024]{0:T(1024)}, u32[]{:S(2)}) copy-start(f32[1024]{0:T(1024)} %param.28) | copy-start | bytes 12292
  11.2 365.8 %all-gather.8.cloned.1.call-start = ((), (), s32[]{:S(2)}) async-start(), calls=%async_computation.2 | async-start | bytes 33030144 | tf_op jit(solution)/shard_map/all_gather | solution.py:1242
  11.9 103.3 %copy-start.15 = (f32[256]{0:T(256)}, f32[256]{0:T(256)S(1)}, u32[]{:S(2)}) copy-start(f32[256]{0:T(256)S(1)} %subtract_convert_fusion) | copy-start | bytes 3076
  113.4 4.1 copy-start.10
  115.2 3.0 copy-start.9
  115.2 3.1 copy-start.17
  122.9 22.1 %copy-start.16 = (f32[256]{0:T(256)S(1)}, f32[256]{0:T(256)}, u32[]{:S(2)}) copy-start(f32[256]{0:T(256)} %copy-done.15) | copy-start | bytes 3076
  122.9 22.1 %slice-start = ((f32[256]{0:T(256)}), f32[2]{0:T(128)S(1)}, s32[]{:S(2)}) async-start(f32[256]{0:T(256)} %copy-done.15), calls=%async_computation.3 | async-start | bytes 1024 | tf_op jit(solution)/shard_map/slice | solution.py:1319
  122.9 22.9 %copy-start = (bf16[256,1024]{1,0:T(8,128)(2,1)S(1)}, bf16[256,1024]{1,0:T(8,128)(2,1)}, u32[]{:S(2)}) copy-start(bf16[256,1024]{1,0:T(8,128)(2,1)} %get-tuple-element.85) | copy-start | bytes 1572868
  122.9 22.9 %copy-start.19 = (f32[1024]{0:T(1024)S(1)}, f32[1024]{0:T(1024)}, u32[]{:S(2)}) copy-start(f32[1024]{0:T(1024)} %param.30) | copy-start | bytes 12292
  147.7 4.7 %copy-start.2 = (bf16[256,1024]{1,0:T(8,128)(2,1)}, bf16[256,1024]{1,0:T(8,128)(2,1)S(1)}, u32[]{:S(2)}) copy-start(bf16[256,1024]{1,0:T(8,128)(2,1)S(1)} %multiply_convert_fusion.1.gated) | copy-start | bytes 1572868
  225.8 1.1 copy-start.14
  348.0 7.8 %copy-start.11 = (f32[16,8,128]{2,1,0:T(8,128)S(1)}, f32[16,8,128]{2,1,0:T(8,128)}, u32[]{:S(2)}) copy-start(f32[16,8,128]{2,1,0:T(8,128)} %get-tuple-element.108) | copy-start | bytes 196612
  348.0 8.4 %copy-start.7 = (f32[160,256]{1,0:T(8,128)S(1)}, f32[160,256]{1,0:T(8,128)}, u32[]{:S(2)}) copy-start(f32[160,256]{1,0:T(8,128)} %get-tuple-element.83) | copy-start | bytes 491524
  348.0 11.1 %copy-start.4 = (bf16[8,4,64,256]{3,2,1,0:T(8,128)(2,1)S(1)}, bf16[8,4,64,256]{3,2,1,0:T(8,128)(2,1)}, u32[]{:S(2)}) copy-start(bf16[8,4,64,256]{3,2,1,0:T(8,128)(2,1)} %get-tuple-element.112) | copy-start | bytes 3145732
  353.4 5.1 %copy-start.5 = (bf16[256,1024]{1,0:T(8,128)(2,1)}, bf16[256,1024]{1,0:T(8,128)(2,1)S(1)}, u32[]{:S(2)}) copy-start(bf16[256,1024]{1,0:T(8,128)(2,1)S(1)} %get-tuple-element.172) | copy-start | bytes 1572868
  353.4 7.1 %copy-start.3 = (bf16[8,256,256]{2,1,0:T(8,128)(2,1)S(1)}, bf16[8,256,256]{2,1,0:T(8,128)(2,1)}, u32[]{:S(2)}) copy-start(bf16[8,256,256]{2,1,0:T(8,128)(2,1)} %get-tuple-element.111) | copy-start | bytes 3145732
  353.5 8.4 %collective-permute-start = (bf16[3,1024]{1,0:T(4,128)(2,1)S(1)}, bf16[3,1024]{1,0:T(4,128)(2,1)S(1)}, u32[]{:S(2)}, u32[]{:S(2)}) collective-permute-start(bf16[3,1024]{1,0:T(4,128)(2,1)S(1)} %slice_multiply_fusion.4), channel_id=1, source_target_pairs={{4,0},{8,4},{12,8},{16,12},{20,16},{24,20},{28,24},{5,1},{9,5},{13... | collective-permute-start | bytes 18440 | tf_op jit(solution)/shard_map/ppermute | solution.py:1248
  358.5 3.5 copy-start.6
  361.9 1.0 copy-start.8
  362.7 7.2 %copy-start.1 = (bf16[256,1024]{1,0:T(8,128)(2,1)}, bf16[256,1024]{1,0:T(8,128)(2,1)S(1)}, u32[]{:S(2)}) copy-start(bf16[256,1024]{1,0:T(8,128)(2,1)S(1)} %fusion.16.refs_1_) | copy-start | bytes 1572868
Sparse Core Ops, SparseCore 0:
  9.9 59.1 all-gather.3
  71.0 128.2 all-gather.5
  226.0 150.9 all-gather.7

commit v7 on v6

--- a/solution.py
+++ b/solution.py
@@ -309,7 +309,7 @@
 
 
 def first_kernel(
-    left_w, right_w, small, cot, tok, gain, taps, bias, goes,
+    left_w, right_w, step_w, select_w, cot, tok, gain, taps, bias, goes,
     w_first, cot_f, act_f, w_small, inner, prev, switch, conv, mixed, select,
     first_in, w_near, ext, before, halo, part, recv,
     s_pair, s_small, s_own, s_cot, s_act, s_cz, s_az, s_halo, s_scatter, s_gather,
@@ -326,7 +326,10 @@
     ]
     for copy in placed:
         copy.start()
-    kept = [keep(small, w_small, s_own.at[1])]
+    lines = step_w.shape[0]
+    w_small[seq, 2 * lines :] = jnp.zeros_like(w_small[seq, 2 * lines :])
+    w_small[seq, :lines] = step_w[...]
+    w_small[seq, lines : lines + select_w.shape[0]] = select_w[...]
 
     def norm(at):
         v = tok[pl.ds(at, 16)].astype(F32)
@@ -335,7 +338,7 @@
 
     step_rows(count, 16, norm)
     greet(("seq", "wt"))
-    little = cube_first(small, w_small, s_small)
+    little = cube_first(w_small.at[seq], w_small, s_small)
     sent1, kept1 = share(cot, cot_f, s_cot, s_own.at[2])
     sent2, kept2 = share(first_in, act_f, s_act, s_own.at[3])
     for copy in placed:
@@ -352,8 +355,6 @@
     pair3 = cube_third(w_near, s_pair, pair2)
     cube_end(little, little2, little3)
     cube_end(pair1, pair2, pair3)
-    for copy in kept:
-        copy.wait()
     far = pltpu.make_async_copy(w_near, w_first, s_own.at[0])
     far.start()
 
@@ -431,7 +432,7 @@
         left(group)
 
 
-def first_gather(left_w, right_w, small, cot, tok, gain, taps, bias, goes, rows_sel, n_wt, n_seq, ident):
+def first_gather(left_w, right_w, step_w, select_w, cot, tok, gain, taps, bias, goes, rows_sel, n_wt, n_seq, ident):
     count, width = cot.shape
     rows, chan = left_w.shape
     pair_shape = (n_seq, rows, 2 * chan)
@@ -443,7 +444,7 @@
             jax.ShapeDtypeStruct(pair_shape, BF16),
             share_shape,
             share_shape,
-            jax.ShapeDtypeStruct((n_seq,) + small.shape, BF16),
+            jax.ShapeDtypeStruct((n_seq, 64, chan), BF16),
             jax.ShapeDtypeStruct((count, chan), BF16),
             jax.ShapeDtypeStruct((8, chan), F32),
             jax.ShapeDtypeStruct((count, chan), F32),
@@ -451,7 +452,7 @@
             jax.ShapeDtypeStruct((count, chan), BF16),
             jax.ShapeDtypeStruct((lines, count), F32),
         ],
-        in_specs=[ANY] * 3 + [VMEM] * 6,
+        in_specs=[ANY] * 2 + [VMEM] * 8,
         out_specs=[ANY] * 3 + [VMEM] * 7,
         scratch_shapes=[
             pltpu.VMEM((count, width), BF16),
@@ -476,7 +477,7 @@
             collective_id=ident, has_side_effects=True, vmem_limit_bytes=VMEM_BYTES
         ),
         cost_estimate=pl.CostEstimate(flops=10**9, bytes_accessed=10**8, transcendentals=0),
-    )(left_w, right_w, small, cot, tok, gain[None], taps, bias[None], goes)
+    )(left_w, right_w, step_w, select_w, cot, tok, gain[None], taps, bias[None], goes)
 
 
 def ffn_kernel(cube, x, c, wg, wu, wd, gated, acts, down, d_second, *refs):
@@ -1320,13 +1321,12 @@
         * jnp.concatenate([one, head[:1]])
     )
     if cube:
-        fill = jnp.zeros((-(rows_sel + rows_step) % 32, chan), BF16)
         (
             w_first, cot_f, first_f, w_small,
             inner_act, prev_rows, switch, conv_out, mixed_in, select,
         ) = first_gather(
             inner_proj, switch_proj,
-            jnp.concatenate([step_proj, select_proj, fill], axis=0),
+            step_proj, select_proj,
             cotangent, tokens, premix_gain, conv_taps, conv_bias,
             jnp.broadcast_to(goes_on[:, None], (tok_count, 128)), rows_sel, n_wt, n_seq, 7,
         )

time: 462 us -> 462 us (level)
  no operation moved by 1% of the time
where the time goes in v7:
time: 462 us; the launch traced here: 461 us
  Pallas kernels  372 us (81%)
  matrix products  26.3 us (6%)
  local copies, waits for them, and re-layouts  17 us (4%)
  other arithmetic  15.3 us (3%)
  waiting for transfers between devices  14.1 us (3%)
  between operations  14.1 us (3%)
    pallas_call x1, Pallas kernels, first_gather(): pl.pallas_call(first_kernel, out_shape=[jax.ShapeDtypeStruct(pair_shape,...  96.3 us
    pallas_call x1, Pallas kernels, last(): pl.pallas_call(functools.partial(last_kernel, len(blocks)), out_shape=[ja...  68.2 us
    pallas_call x1, Pallas kernels, bwd_scan(): pl.pallas_call(functools.partial(bwd_kernel, len(src)), out_shape=[jax.Sh...  52.7 us
    pallas_call x1, Pallas kernels, second_back(): pl.pallas_call(functools.partial(second_back_kernel, len(srcs)), out_shap...  43.6 us
    pallas_call x1, Pallas kernels, second_norm(): pl.pallas_call(second_norm_kernel, out_shape=[jax.ShapeDtypeStruct((rows,...  41.9 us
    pallas_call x1, Pallas kernels, ffn(): pl.pallas_call(functools.partial(ffn_kernel, int(cube)), grid=(steps,), i...  26.5 us
    dot_general x8, matrix products, contract(): return jnp.einsum(pattern, left_op, right_op, preferred_element_type=F32)  26.3 us
    pallas_call x1, Pallas kernels, fwd_scan(): pl.pallas_call(fwd_kernel, out_shape=[jax.ShapeDtypeStruct((tok, high, 12...  21.1 us
  transfers between devices with their start and end apart: 4, of which 2 were waited for; matrix products, arithmetic and copies ran while one was open for 13% of the time, Pallas kernels for 58%

profile of v7, /device:TPU:0, one launch (start us, length us, event | category | flops | bytes accessed | tf_op | source)
XLA Modules:
  0.0 460.9 jit_solution(9565148135127088147)
XLA Ops:
  7.2 0.0 all-gather.4.cloned.1.call-start
  7.2 0.7 all-gather.4.cloned.1.call-update
  7.9 0.0 all-gather.6.cloned.1.call-start
  8.0 3.2 pad_maximum_fusion
  11.2 0.0 all-gather.6.cloned.1.call-update
  11.2 0.0 all-gather.8.cloned.1.call-start
  11.3 0.6 copy-done.18
  11.9 0.5 slice.91
  12.4 0.8 broadcast_in_dim.24.goes
  13.1 96.3 %shard_map.305 = (bf16[8,256,2048]{2,1,0:T(8,128)(2,1)}, bf16[8,4,64,256]{3,2,1,0:T(8,128)(2,1)}, bf16[8,4,64,256]{3,2,1,0:T(8,128)(2,1)}, bf16[8,64,1024]{2,1,0...) custom-call(bf16[256,1024]{1,0:T(8,128)(2,1)} %left_w.1, ...), custom_call_target="tpu_custom_call" | custom-call | flops 1000000000 | bytes 100000000 | tf_op jit(solution)/shard_map/pallas_call | solution.py:441
  109.4 1.0 slice.87
  110.4 1.4 slice.88.wr
  111.8 1.2 convolution_add_fusion.1
  113.0 0.0 copy-start.10
  113.0 1.8 fusion.2
  114.8 1.2 copy.46
  116.0 1.2 copy.47
  117.1 0.6 copy.48
  117.8 0.1 convert_element_type.56
  117.9 2.3 copy.40
  120.2 2.3 copy.41
  122.5 21.1 %shard_map.306 = (f32[256,8,128]{2,1,0:T(8,128)}, f32[16,8,128]{2,1,0:T(8,128)}) custom-call(f32[256,8,128]{2,1,0:T(8,128)} %bitcast.76, f32[256,8,128]{2,1,0:T(8,128)} %bitcast.78, f32[32,256]{1,0:T(8,128)} %slice.88.wr, f32[16,8,128]{2,1,0:T(8,128)} %bitcast.88), custom_call_target="tpu_custom_call" | custom-call | flops 100000000 | bytes 80000000 | tf_op jit(solution)/shard_map/pallas_call | solution.py:1052
  143.5 1.1 pad_maximum_fusion.1
  144.6 0.7 fusion.33
  145.4 2.0 multiply_convert_fusion.1.gated
  147.4 0.0 copy-start.2
  147.4 0.0 all-gather.4.cloned.1.call-done
  147.4 4.7 %convolution_convert_fusion.part = bf16[256,2048]{1,0:T(8,128)(2,1)} fusion(bf16[256,1024]{1,0:T(8,128)(2,1)S(1)} %multiply_convert_fusion.1.gated, bf16[2048,1024]{1,0:T(8,128)(2,1)} %all-gather.4.cloned.1.call-done), kind=kOutput, calls=%fused_computation.2 | convolution fusion | flops 1074266112 | bytes 5767168 | tf_op jit(solution)/shard_map/tc,dc->td/dot_general | solution.py:1253
  152.1 41.9 %shard_map.307 = (bf16[256,2048]{1,0:T(8,128)(2,1)}, f32[64,2048]{1,0:T(8,128)}) custom-call(bf16[256,2048]{1,0:T(8,128)(2,1)} %convolution_convert_fusion.part, bf16[256,2048]{1,0:T(8,128)(2,1)} %tok.5, f32[1,2048]{1,0:T(1,128)} %bitcast.90), custom_call_target="tpu_custom_call" | custom-call | flops 1000000 | bytes 100000000 | tf_op jit(solution)/shard_map/pallas_call | solution.py:642
  194.0 5.3 %all-gather.6.cloned.1.call-done.wg.wu.wd = bf16[2048,6144]{1,0:T(8,128)(2,1)} async-done(((bf16[256,6144]{1,0:T(8,128)(2,1)}), bf16[2048,6144]{1,0:T(8,128)(2,1)}) %all-gather.6.cloned.1.call-update) | async-done | bytes 25165840 | tf_op jit(solution)/shard_map/all_gather | solution.py:1243
  199.3 26.5 %shard_map.308 = (bf16[256,7168]{1,0:T(8,128)(2,1)}, bf16[256,2048]{1,0:T(8,128)(2,1)}, bf16[256,2048]{1,0:T(8,128)(2,1)}, bf16[8,256,256]{2,1,0:T(8,128)(2,1)}) custom-call(bf16[256,2048]{1,0:T(8,128)(2,1)} %get-tuple-element.93.x, bf16[256,2048]{1,0:T(8,128)(2,1)} %cot.3, bf16[2048,6144]{1,0:T(8,128)(2,1)} %all-gather.6.cloned.1.call-done.wg.wu.wd, ...), custom_call_target="tpu_custom_call" | custom-call | flops 12884901888 | bytes 25165824 | tf_op jit(solution)/shard_map/pallas_call | solution.py:535
  225.8 0.0 copy-start.12
  225.8 0.0 all-gather.8.cloned.1.call-update
  225.8 1.0 slice.93
  226.9 0.1 fusion.30
  227.0 43.6 %shard_map.309 = (bf16[256,2048]{1,0:T(8,128)(2,1)}, f32[64,2048]{1,0:T(8,128)}, f32[8,2048]{1,0:T(8,128)}) custom-call(bf16[256,2048]{1,0:T(8,128)(2,1)} %get-tuple-element.94.part, f32[64,2048]{1,0:T(8,128)} %get-tuple-element.95.res, bf16[256,2048]{1,0:T(8,128)(2,1)} %cot.3, f32[1,2048]{1,0:T(1,128)} %bitcast.91), custom_call_target="tpu_custom_call" | custom-call | flops 1000000 | bytes 100000000 | tf_op jit(solution)/shard_map/pallas_call | solution.py:711
  270.6 6.0 %fusion.6 = (f32[1024]{0:T(1024)S(1)}, f32[256,1024]{1,0:T(8,128)}, bf16[256,1024]{1,0:T(8,128)(2,1)}) fusion(bf16[256,1024]{1,0:T(8,128)(2,1)S(1)} %copy-done, f32[256,1024]{1,0:T(8,128)} %get-tuple-element.87, f32[1024]{0:T(1024)S(1)} %copy-done.17, f32[32,8,8,128]{3,2,1,0:T(8,128)} %bitcast.82, bf16[256,2048]{1,0:T(8,128)(2,1)} %get-tuple-element.96.refs_0_, ...), kind=kOutput, calls=%fused_computation.24 | convolution fusion | flops 1078197248 | bytes 9445376 | tf_op jit(solution)/shard_map/td,dc->tc/dot_general | solution.py:1253
  276.5 52.7 %shard_map.310 = (f32[256,1024]{1,0:T(8,128)}, f32[256,1024]{1,0:T(8,128)}, f32[16,8,128]{2,1,0:T(8,128)}, f32[16,512]{1,0:T(8,128)}, bf16[64,2048]{1,0:T(8,128)(2,1)}, /*index=5*/bf16[8,4,64,256]{3,2,1,0:T(8,128)(2,1)}) custom-call(f32[256,8,128]{2,1,0:T(8,128)} %bitcast.77, f32[256,8,128]{2,1,0:T(8,128)} %bitcast.79, f32[32,256]{1,0:T(8,128)} %slice.88.wr, ...), custom_call_target="tpu_custom_call" | custom-call | flops 100000000 | bytes 150000000 | tf_op jit(solution)/shard_map/pallas_call | solution.py:1203
  329.2 0.9 reshape.109
  330.1 0.1 copy.42
  330.2 2.0 fusion.35
  332.2 0.3 fusion.26
  332.5 0.7 pad_maximum_fusion.2.part
  333.2 0.1 reshape.111
  333.3 13.0 %shard_map.311 = f32[160,256]{1,0:T(8,128)} custom-call(f32[160,256]{1,0:T(8,128)} %pad_maximum_fusion.2.part), custom_call_target="tpu_custom_call" | custom-call | flops 100000 | bytes 1000000 | tf_op jit(solution)/shard_map/pallas_call | solution.py:598
  346.3 0.9 convert_element_type.58
  347.3 5.3 %fusion.7 = (f32[1024]{0:T(1024)S(1)}, f32[1024]{0:T(1024)S(1)}, f32[1024]{0:T(1024)S(1)}, f32[1024]{0:T(1024)S(1)}, f32[1024]{0:T(1024)S(1)}, /*index=5*/bf16[256,1024]{1,0:T(8,128)(2,1)S(1)}) fusion(f32[259,1024]{1,0:T(8,128)} %pad_maximum_fusion.1, f32[256]{0:T(256)S(1)} %copy-done.14, f32[256]{0:T(256)S(1)} %get-tuple-element.159, ...), kind=kOutput, calls=%fused_computation.25 | convolution fusion | flops 92269568 | bytes 9350144 | tf_op jit(solution)/shard_map/jt,jc->tc/dot_general | solution.py:1253
  352.6 0.0 copy-start.5
  352.6 0.1 slice_multiply_fusion.4
  352.7 1.6 collective-permute-start
  354.3 0.6 pad_maximum_fusion.4.bias3
  355.0 0.7 bitcast_multiply_fusion.decays
  355.6 0.9 convolution_convert_fusion.3
  356.5 1.1 convolution_convert_fusion.2
  357.6 0.6 pad_maximum_fusion.3.taps
  358.3 1.4 copy.44
  359.7 1.4 copy.45
  361.1 0.1 maximum_convert_fusion
  361.2 0.6 fusion.16.refs_1_
  361.9 0.3 copy-done.8
  362.2 6.8 %convolution_convert_fusion.1.part = bf16[256,2048]{1,0:T(8,128)(2,1)} fusion(bf16[2048,2048]{1,0:T(8,128)(2,1)} %bitcast.111, bf16[256,1024]{1,0:T(8,128)(2,1)S(1)} %copy-done.8, bf16[256,1024]{1,0:T(8,128)(2,1)S(1)} %fusion.16.refs_1_), kind=kOutput, calls=%fused_computation.3 | convolution fusion | flops 2150105088 | bytes 10485760 | tf_op jit(solution)/shard_map/tc,dc->td/dot_general | solution.py:1253
  368.9 8.0 %all-gather.8.cloned.1.call-done.refs_6_ = bf16[2048,7168]{1,0:T(8,128)(2,1)} async-done(((bf16[256,7168]{1,0:T(8,128)(2,1)}), bf16[2048,7168]{1,0:T(8,128)(2,1)}) %all-gather.8.cloned.1.call-update) | async-done | bytes 29360144 | tf_op jit(solution)/shard_map/all_gather | solution.py:1243
  377.0 68.2 %shard_map.312 = (bf16[256,2048]{1,0:T(8,128)(2,1)}, bf16[256,2048]{1,0:T(8,128)(2,1)}, f32[20,1024]{1,0:T(8,128)}, f32[16,1024]{1,0:T(8,128)}, f32[4,1024]{1,0:...) custom-call(bf16[256,2048]{1,0:T(8,128)(2,1)} %convolution_convert_f, ...), custom_call_target="tpu_custom_call" | custom-call | flops 1000000 | bytes 100000000 | tf_op jit(solution)/shard_map/pallas_call | solution.py:889
  445.1 9.2 %shard_map.313 = (bf16[256,2048]{1,0:T(8,128)(2,1)}, bf16[256,2048]{1,0:T(8,128)(2,1)}, f32[20,1024]{1,0:T(8,128)}, f32[16,1024]{1,0:T(8,128)}, f32[4,1024]{1,0:...) custom-call(bf16[256,2048]{1,0:T(8,128)(2,1)} %get-tuple-element.115, ...), custom_call_target="tpu_custom_call" | custom-call | bytes 23584768 | tf_op jit(solution)/shard_map/pallas_call | solution.py:959
  (42 shorter events, 0.2 us)
Async XLA Ops:
  7.2 140.2 %all-gather.4.cloned.1.call-start = ((), (), s32[]{:S(2)}) async-start(), calls=%async_computation | async-start | bytes 4718592 | tf_op jit(solution)/shard_map/all_gather | solution.py:1243
  7.9 191.4 %all-gather.6.cloned.1.call-start = ((), (), s32[]{:S(2)}) async-start(), calls=%async_computation.1 | async-start | bytes 28311552 | tf_op jit(solution)/shard_map/all_gather | solution.py:1243
  11.2 0.7 copy-start.18
  11.2 100.6 %copy-start.16 = (f32[1024]{0:T(1024)S(1)}, f32[1024]{0:T(1024)}, u32[]{:S(2)}) copy-start(f32[1024]{0:T(1024)} %param.28) | copy-start | bytes 12292
  11.2 365.7 %all-gather.8.cloned.1.call-start = ((), (), s32[]{:S(2)}) async-start(), calls=%async_computation.2 | async-start | bytes 33030144 | tf_op jit(solution)/shard_map/all_gather | solution.py:1243
  11.9 102.9 %copy-start.13 = (f32[256]{0:T(256)}, f32[256]{0:T(256)S(1)}, u32[]{:S(2)}) copy-start(f32[256]{0:T(256)S(1)} %subtract_convert_fusion) | copy-start | bytes 3076
  113.0 4.1 copy-start.10
  114.8 3.0 copy-start.9
  114.8 3.1 copy-start.15
  122.5 22.2 %copy-start.14 = (f32[256]{0:T(256)S(1)}, f32[256]{0:T(256)}, u32[]{:S(2)}) copy-start(f32[256]{0:T(256)} %copy-done.13) | copy-start | bytes 3076
  122.5 22.2 %slice-start = ((f32[256]{0:T(256)}), f32[2]{0:T(128)S(1)}, s32[]{:S(2)}) async-start(f32[256]{0:T(256)} %copy-done.13), calls=%async_computation.3 | async-start | bytes 1024 | tf_op jit(solution)/shard_map/slice | solution.py:1320
  122.5 22.9 %copy-start = (bf16[256,1024]{1,0:T(8,128)(2,1)S(1)}, bf16[256,1024]{1,0:T(8,128)(2,1)}, u32[]{:S(2)}) copy-start(bf16[256,1024]{1,0:T(8,128)(2,1)} %get-tuple-element.85) | copy-start | bytes 1572868
  122.5 22.9 %copy-start.17 = (f32[1024]{0:T(1024)S(1)}, f32[1024]{0:T(1024)}, u32[]{:S(2)}) copy-start(f32[1024]{0:T(1024)} %param.30) | copy-start | bytes 12292
  147.4 4.7 %copy-start.2 = (bf16[256,1024]{1,0:T(8,128)(2,1)}, bf16[256,1024]{1,0:T(8,128)(2,1)S(1)}, u32[]{:S(2)}) copy-start(bf16[256,1024]{1,0:T(8,128)(2,1)S(1)} %multiply_convert_fusion.1.gated) | copy-start | bytes 1572868
  225.8 1.1 copy-start.12
  347.3 7.7 %copy-start.11 = (f32[16,8,128]{2,1,0:T(8,128)S(1)}, f32[16,8,128]{2,1,0:T(8,128)}, u32[]{:S(2)}) copy-start(f32[16,8,128]{2,1,0:T(8,128)} %get-tuple-element.108) | copy-start | bytes 196612
  347.3 8.3 %copy-start.7 = (f32[160,256]{1,0:T(8,128)S(1)}, f32[160,256]{1,0:T(8,128)}, u32[]{:S(2)}) copy-start(f32[160,256]{1,0:T(8,128)} %get-tuple-element.83) | copy-start | bytes 491524
  352.6 5.1 %copy-start.5 = (bf16[256,1024]{1,0:T(8,128)(2,1)}, bf16[256,1024]{1,0:T(8,128)(2,1)S(1)}, u32[]{:S(2)}) copy-start(bf16[256,1024]{1,0:T(8,128)(2,1)S(1)} %get-tuple-element.172) | copy-start | bytes 1572868
  352.6 5.7 %copy-start.4 = (bf16[8,4,64,256]{3,2,1,0:T(8,128)(2,1)S(1)}, bf16[8,4,64,256]{3,2,1,0:T(8,128)(2,1)}, u32[]{:S(2)}) copy-start(bf16[8,4,64,256]{3,2,1,0:T(8,128)(2,1)} %get-tuple-element.112) | copy-start | bytes 3145732
  352.6 7.1 %copy-start.3 = (bf16[8,256,256]{2,1,0:T(8,128)(2,1)S(1)}, bf16[8,256,256]{2,1,0:T(8,128)(2,1)}, u32[]{:S(2)}) copy-start(bf16[8,256,256]{2,1,0:T(8,128)(2,1)} %get-tuple-element.111) | copy-start | bytes 3145732
  352.7 8.4 %collective-permute-start = (bf16[3,1024]{1,0:T(4,128)(2,1)S(1)}, bf16[3,1024]{1,0:T(4,128)(2,1)S(1)}, u32[]{:S(2)}, u32[]{:S(2)}) collective-permute-start(bf16[3,1024]{1,0:T(4,128)(2,1)S(1)} %slice_multiply_fusion.4), channel_id=1, source_target_pairs={{4,0},{8,4},{12,8},{16,12},{20,16},{24,20},{28,24},{5,1},{9,5},{13... | collective-permute-start | bytes 18440 | tf_op jit(solution)/shard_map/ppermute | solution.py:1249
  357.6 3.5 copy-start.6
  361.1 1.0 copy-start.8
  361.9 7.1 %copy-start.1 = (bf16[256,1024]{1,0:T(8,128)(2,1)}, bf16[256,1024]{1,0:T(8,128)(2,1)S(1)}, u32[]{:S(2)}) copy-start(bf16[256,1024]{1,0:T(8,128)(2,1)S(1)} %fusion.16.refs_1_) | copy-start | bytes 1572868
Sparse Core Ops, SparseCore 0:
  9.9 59.2 all-gather.3
  71.1 128.1 all-gather.5
  226.0 150.9 all-gather.7
